TPU v7x, 32 devices: a whole 2x2x4 slice. The times are simulated.
32 devices in a mesh: ctx: 16 (over z, y, core), head: 2 (over x).
Axes of the slice: x: 2, y: 2, z: 4, core: 2. Of those that a mesh axis runs over, the one named last changes fastest.
Arguments:
- queries: bfloat16 [4096, 2048], P('ctx', 'head'), parts along dimension 1, may hold values from -4.6 to 4.6
- key_vectors: bfloat16 [4096, 256], P('ctx', 'head'), parts along dimension 1, may hold values from -4.6 to 4.6
- value_vectors: bfloat16 [4096, 256], P('ctx', 'head'), parts along dimension 1, may hold values from -6 to 6
- doc_ids: int32 [4096], replicated, may hold values from 0 to 9, never falling along the last dimension, each value on 1 to 768 neighbouring positions
- grad_out: bfloat16 [4096, 2048], P('ctx', 'head'), parts along dimension 1, may hold values from -6 to 6
Outputs:
- attended: bfloat16 [4096, 2048], P('ctx', 'head'), parts along dimension 1
- grad_query: bfloat16 [4096, 2048], P('ctx', 'head'), parts along dimension 1
- grad_key: bfloat16 [4096, 256], P('ctx', 'head'), parts along dimension 1
- grad_value: bfloat16 [4096, 256], P('ctx', 'head'), parts along dimension 1
There are 2 independent parts, one for each index of `head`. A program takes and returns all parts, laid end to end along the dimension named above; an argument that names none is the same for every part. Nothing has to cross between parts.
Inputs may be any that keep to these rules, and one draw needn't show every extreme that they name: doc_ids never fall along the sequence; each document holds 1 to 768 positions and one holds exactly 768.
All inputs are finite; a program needn't handle non-finite values.
Results may differ from a plain program's by a relative error of at most 0.029.
Values may be sent and summed in bfloat16 or wider, within the bound.
No kernel may reach another device: no remote copies, remote signals or barrier semaphores. Data moves between devices by JAX's collectives and lax.ppermute only.
A program may use at most 64 MiB of HBM per device.

v0:
```python
import jax
import jax.numpy as jnp
from jax import lax
from jax.sharding import PartitionSpec as P

REACH = 3


def from_behind(value, axis, by):
    size = lax.axis_size(axis)
    pairs = [(i, i + by) for i in range(size) if 0 <= i + by < size]
    return lax.ppermute(value, axis, pairs)


def block_grads(query_rows, grad_rows, key_value, query_pos, key_pos, query_doc, key_doc):
    row_count = query_rows.shape[0]
    head_dim = key_value.shape[1] // 2
    score_scale = head_dim ** (-0.5)
    query_heads = query_rows.reshape(row_count, -1, head_dim)
    grad_heads = grad_rows.reshape(row_count, -1, head_dim)
    key_part = key_value[:, :head_dim]
    value_part = key_value[:, head_dim:]
    allowed = (
        (query_doc[:, None] == key_doc[None, :])
        & (key_pos[None, :] <= query_pos[:, None])
        & (key_pos[None, :] >= 0)
    )
    scores = (
        jnp.einsum("thd,kd->htk", query_heads, key_part, preferred_element_type=jnp.float32)
        * score_scale
    )
    scores = jnp.where(allowed[None], scores, -1e30)
    row_max = jnp.max(scores, axis=-1, keepdims=True)
    row_sum = jnp.sum(
        jnp.where(allowed[None], jnp.exp(scores - row_max), 0.0), axis=-1, keepdims=True
    )
    log_norm = row_max + jnp.log(row_sum)
    probs = jnp.where(allowed[None], jnp.exp(scores - log_norm), 0.0)
    weights = probs.astype(jnp.bfloat16)
    attended = jnp.einsum(
        "htk,kd->thd", weights, value_part, preferred_element_type=jnp.float32
    ).astype(jnp.bfloat16)
    delta = jnp.sum(grad_heads.astype(jnp.float32) * attended.astype(jnp.float32), axis=-1)
    grad_prob = jnp.einsum(
        "thd,kd->htk", grad_heads, value_part, preferred_element_type=jnp.float32
    )
    dscore = (probs * (grad_prob - jnp.transpose(delta)[:, :, None])).astype(jnp.bfloat16)
    grad_query = (
        jnp.einsum("htk,kd->thd", dscore, key_part, preferred_element_type=jnp.float32)
        * score_scale
    ).astype(jnp.bfloat16)
    grad_key = (
        jnp.einsum("htk,thd->kd", dscore, query_heads, preferred_element_type=jnp.float32)
        * score_scale
    )
    grad_value = jnp.einsum("htk,thd->kd", weights, grad_heads, preferred_element_type=jnp.float32)
    return (
        attended.reshape(row_count, -1),
        grad_query.reshape(row_count, -1),
        jnp.concatenate([grad_key, grad_value], axis=1),
    )


def body(queries, key_vectors, value_vectors, doc_ids, grad_out):
    row_count = queries.shape[0]
    head_dim = key_vectors.shape[1]
    key_span = (REACH + 1) * row_count
    first_row = lax.axis_index("ctx") * row_count
    key_value = jnp.concatenate([key_vectors, value_vectors], axis=1)
    held_blocks = [key_value]
    visiting = key_value
    for repeat in range(REACH):
        visiting = from_behind(visiting, "ctx", 1)
        held_blocks.append(visiting)
    stacked = jnp.stack(held_blocks)
    window = stacked[::-1].reshape(key_span, 2 * head_dim)
    padded_doc = jnp.concatenate([jnp.full((REACH * row_count,), -1, jnp.int32), doc_ids], axis=0)
    key_doc = lax.dynamic_slice_in_dim(padded_doc, first_row, key_span, 0)
    query_doc = lax.dynamic_slice_in_dim(doc_ids, first_row, row_count, 0)
    query_pos = first_row + jnp.arange(row_count, dtype=jnp.int32)
    key_pos = first_row - REACH * row_count + jnp.arange(key_span, dtype=jnp.int32)
    attended, grad_query, grad_pair = block_grads(
        queries, grad_out, window, query_pos, key_pos, query_doc, key_doc
    )
    partials = grad_pair.reshape(REACH + 1, row_count, 2 * head_dim)[::-1]
    gathered = partials[REACH]
    for offset in range(REACH - 1, -1, -1):
        gathered = from_behind(gathered, "ctx", -1) + partials[offset]
    return (
        attended,
        grad_query,
        gathered[:, :head_dim].astype(jnp.bfloat16),
        gathered[:, head_dim:].astype(jnp.bfloat16),
    )


def solution(mesh):
    return jax.shard_map(
        body,
        mesh=mesh,
        in_specs=(P("ctx", "head"), P("ctx", "head"), P("ctx", "head"), P(), P("ctx", "head")),
        out_specs=(P("ctx", "head"), P("ctx", "head"), P("ctx", "head"), P("ctx", "head")),
        check_vma=False,
    )
```

profile of v0, /device:TPU:21, one launch (start us, length us, event | category | flops | bytes accessed | tf_op | source)
XLA Modules:
  0.0 65.6 jit_solution(9569337267288407789)
XLA Ops:
  0.6 0.9 %constant_dynamic-update-slice_fusion.1 = bf16[256,256]{1,0:T(8,128)(2,1)S(1)} fusion(bf16[256,128]{1,0:T(8,128)(2,1)} %param.6), kind=kLoop, calls=%fused_computation.37 | loop fusion | bytes 131072
  1.5 0.9 %constant_dynamic-update-slice_fusion = bf16[256,256]{1,0:T(8,128)(2,1)S(1)} fusion(bf16[256,256]{1,0:T(8,128)(2,1)S(1)} %constant_dynamic-update-slice_fusion.1, bf16[256,128]{1,0:T(8,128)(2,1)} %param.7), kind=kLoop, calls=%fused_computation.36 | loop fusion | bytes 131072 | tf_op jit(solution)/shard_map/concatenate | solution.py:69
  2.3 3.7 %collective-permute-start = (bf16[256,256]{1,0:T(8,128)(2,1)S(1)}, bf16[256,256]{1,0:T(8,128)(2,1)S(1)}, u32[]{:S(2)}, u32[]{:S(2)}) collective-permute-start(bf16[256,256]{1,0:T(8,128)(2,1)S(1)} %constant_dynamic-update-slice_fusion), channel_id=1, source_target_pairs={{0,2},{2,4},{4,6},{6,8},{8,10},{10,12},{12,14},{14,16},{16,18},{18... | collective-permute-start | bytes 393224 | tf_op jit(solution)/shard_map/ppermute | solution.py:12
  6.1 1.9 %collective-permute-done = bf16[256,256]{1,0:T(8,128)(2,1)S(1)} collective-permute-done((bf16[256,256]{1,0:T(8,128)(2,1)S(1)}, bf16[256,256]{1,0:T(8,128)(2,1)S(1)}, u32[]{:S(2)}, u32[]{:S(2)}) %collective-permute-start) | collective-permute-done | bytes 131104 | tf_op jit(solution)/shard_map/ppermute | solution.py:12
  8.0 5.2 %collective-permute-start.1 = (bf16[256,256]{1,0:T(8,128)(2,1)S(1)}, bf16[256,256]{1,0:T(8,128)(2,1)S(1)}, u32[]{:S(2)}, u32[]{:S(2)}) collective-permute-start(bf16[256,256]{1,0:T(8,128)(2,1)S(1)} %collective-permute-done), channel_id=1, source_target_pairs={{0,2},{2,4},{4,6},{6,8},{8,10},{10,12},{12,14},{14,16},{16,18},{18... | collective-permute-start | bytes 393224 | tf_op jit(solution)/shard_map/ppermute | solution.py:12
  13.3 1.2 %copy.12 = bf16[256,1024]{0,1:T(8,128)(2,1)S(1)} copy(bf16[256,1024]{1,0:T(8,128)(2,1)} %param.9) | data formatting | bytes 1048576 | tf_op args[4]
  14.5 1.2 %copy.32 = bf16[256,1024]{0,1:T(8,128)(2,1)S(1)} copy(bf16[256,1024]{1,0:T(8,128)(2,1)} %param.5) | data formatting | bytes 1048576 | tf_op jit(solution)/shard_map/reshape | solution.py:19
  15.8 0.8 %dynamic_slice.6 = s32[256]{0:T(256)S(1)} dynamic-slice(s32[4096]{0:T(1024)} %param.8, s32[]{:T(128)S(6)} %select_n.16), dynamic_slice_sizes={256} | dynamic-slice | bytes 2052 | tf_op jit(solution)/shard_map/dynamic_slice | solution.py:79
  16.5 0.8 %pad_dynamic-slice_fusion = (s32[1024]{0:T(1024)S(1)}, s32[1024]{0:T(1024)S(1)}) fusion(s32[]{:T(128)S(6)} %select_n.17, s32[4096]{0:T(1024)} %param.8, s32[]{:T(128)S(6)} %sub.27), kind=kLoop, calls=%fused_computation.34 | loop fusion | flops 1024 | bytes 24584 | tf_op jit(solution)/shard_map/dynamic_slice | solution.py:78
  17.3 0.0 collective-permute-done.1
  17.3 3.1 %collective-permute-start.2 = (bf16[256,256]{1,0:T(8,128)(2,1)S(1)}, bf16[256,256]{1,0:T(8,128)(2,1)S(1)}, u32[]{:S(2)}, u32[]{:S(2)}) collective-permute-start(bf16[256,256]{1,0:T(8,128)(2,1)S(1)} %collective-permute-done.1), channel_id=1, source_target_pairs={{0,2},{2,4},{4,6},{6,8},{8,10},{10,12},{12,14},{14,16},{16,18},{18... | collective-permute-start | bytes 393224 | tf_op jit(solution)/shard_map/ppermute | solution.py:12
  20.4 0.9 %and_and_fusion = pred[256,1024]{0,1:T(8,128)(4,1)S(1)} fusion(s32[256]{0:T(256)S(1)} %iota_add_fusion.1, s32[256]{0:T(256)S(1)} %dynamic_slice.6, s32[1024]{0:T(1024)S(1)} %get-tuple-element.15, s32[1024]{0:T(1024)S(1)} %get-tuple-element.14, pred[1024]{0:T(1024)(128)(4,1)S(1)} %broadcast_compare_fusion), kind=kLoop, calls=%fused_computation.21 | loop fusion | flops 1048576 | bytes 273408 | tf_op jit(solution)/shard_map/and | solution.py:24
  21.3 1.0 %collective-permute-done.2 = bf16[256,256]{1,0:T(8,128)(2,1)S(1)} collective-permute-done((bf16[256,256]{1,0:T(8,128)(2,1)S(1)}, bf16[256,256]{1,0:T(8,128)(2,1)S(1)}, u32[]{:S(2)}, u32[]{:S(2)}) %collective-permute-start.2) | collective-permute-done | bytes 131104 | tf_op jit(solution)/shard_map/ppermute | solution.py:12
  22.3 0.1 pad_maximum_fusion
  22.5 1.4 %fusion.3 = (f32[8,256]{1,0:T(8,128)S(1)}, f32[1024,256,8]{1,0,2:T(8,128)S(1)}) fusion(pred[256,1024]{0,1:T(8,128)(4,1)S(1)} %and_and_fusion, bf16[256,8,128]{0,2,1:T(8,128)(2,1)S(1)} %bitcast.67, bf16[1024,256]{1,0:T(8,128)(2,1)S(1)} %bitcast.62), kind=kOutput, calls=%fused_computation.7 | convolution fusion | flops 543160320 | bytes 9445376 | tf_op jit(solution)/shard_map/thd,kd->htk/dot_general | solution.py:29
  23.9 2.0 %select_reduce_fusion = f32[8,256]{1,0:T(8,128)S(1)} fusion(f32[1024,256,8]{1,0,2:T(8,128)S(1)} %get-tuple-element.11, f32[8,256]{1,0:T(8,128)S(1)} %get-tuple-element.10, pred[256,1024]{0,1:T(8,128)(4,1)S(1)} %and_and_fusion), kind=kLoop, calls=%fused_computation.5 | loop fusion | flops 10483712 | bytes 8667136 | tf_op jit(solution)/shard_map/reduce_sum | solution.py:34
  25.9 2.3 %multiply_reduce_fusion = (f32[256,8]{0,1:T(8,128)S(1)}, bf16[128,8,256]{2,0,1:T(8,128)(2,1)S(1)}) fusion(bf16[256,1024]{0,1:T(8,128)(2,1)S(1)} %copy.12, f32[1024,256,8]{1,0,2:T(8,128)S(1)} %get-tuple-element.11, f32[8,256]{1,0:T(8,128)S(1)} %log_add_fusion, pred[256,1024]{0,1:T(8,128)(4,1)S(1)} %and_and_fusion, bf16[1024,256]{1,0:T(8,128)(2,1)S(1)} %bitcast.63), kind=kOutput, calls=%fused_computation.20 | convolution fusion | flops 548665344 | bytes 9977856 | tf_op jit(solution)/shard_map/htk,kd->thd/dot_general | solution.py:40
  28.3 2.7 %convolution_bitcast_fusion = f32[1024,128]{0,1:T(8,128)S(1)} fusion(bf16[256,8,128]{0,2,1:T(8,128)(2,1)S(1)} %bitcast.69, f32[1024,256,8]{1,0,2:T(8,128)S(1)} %get-tuple-element.11, f32[8,256]{1,0:T(8,128)S(1)} %log_add_fusion, pred[256,1024]{0,1:T(8,128)(4,1)S(1)} %and_and_fusion), kind=kOutput, calls=%fused_computation.17 | convolution fusion | flops 547356672 | bytes 9707520 | tf_op jit(solution)/shard_map/htk,thd->kd/dot_general | solution.py:56
  31.0 3.1 %fusion.1 = bf16[8,256,1024]{1,2,0:T(8,128)(2,1)S(1)} fusion(f32[1024,256,8]{1,0,2:T(8,128)S(1)} %get-tuple-element.11, f32[8,256]{1,0:T(8,128)S(1)} %bitcast.76, f32[8,256]{1,0:T(8,128)S(1)} %log_add_fusion, pred[256,1024]{0,1:T(8,128)(4,1)S(1)} %and_and_fusion, bf16[256,8,128]{0,2,1:T(8,128)(2,1)S(1)} %bitcast.70, bf16[1024,256]{1,0:T(8,128)(2,1)S(1)} %bitcast.64), kind=kOutput, calls=%fused_computation.2 | convolution fusion | flops 551550976 | bytes 13647872 | tf_op jit(solution)/shard_map/thd,kd->htk/dot_general | solution.py:44
  34.0 0.0 copy-start
  34.1 1.9 %copy-done = bf16[8,256,1024]{1,2,0:T(8,128)(2,1)} copy-done((bf16[8,256,1024]{1,2,0:T(8,128)(2,1)}, bf16[8,256,1024]{1,2,0:T(8,128)(2,1)S(1)}, u32[]{:S(2)}) %copy-start) | copy-done | bytes 4194328
  36.0 1.5 %fusion.5 = f32[1024,128]{0,1:T(8,128)S(1)} fusion(bf16[8,256,1024]{1,2,0:T(8,128)(2,1)S(1)} %fusion.1, bf16[256,8,128]{0,2,1:T(8,128)(2,1)S(1)} %bitcast.68), kind=kOutput, calls=%fused_computation.19 | convolution fusion | flops 537001984 | bytes 5242880 | tf_op jit(solution)/shard_map/htk,thd->kd/dot_general | solution.py:53
  37.5 1.9 %collective-permute-start.3 = (f32[256,256]{0,1:T(8,128)S(1)}, f32[256,256]{0,1:T(8,128)S(1)}, u32[]{:S(2)}, u32[]{:S(2)}) collective-permute-start(f32[256,256]{0,1:T(8,128)S(1)} %fusion.8), channel_id=1, source_target_pairs={{2,0},{4,2},{6,4},{8,6},{10,8},{12,10},{14,12},{16,14},{18,16},{20... | collective-permute-start | bytes 786440 | tf_op jit(solution)/shard_map/ppermute | solution.py:12
  39.4 7.4 %collective-permute-done.3 = f32[256,256]{0,1:T(8,128)S(1)} collective-permute-done((f32[256,256]{0,1:T(8,128)S(1)}, f32[256,256]{0,1:T(8,128)S(1)}, u32[]{:S(2)}, u32[]{:S(2)}) %collective-permute-start.3) | collective-permute-done | bytes 262176 | tf_op jit(solution)/shard_map/ppermute | solution.py:12
  46.8 1.9 %collective-permute-start.4 = (f32[256,256]{0,1:T(8,128)S(1)}, f32[256,256]{0,1:T(8,128)S(1)}, u32[]{:S(2)}, u32[]{:S(2)}) collective-permute-start(f32[256,256]{0,1:T(8,128)S(1)} %fusion.10), channel_id=1, source_target_pairs={{2,0},{4,2},{6,4},{8,6},{10,8},{12,10},{14,12},{16,14},{18,16},{20... | collective-permute-start | bytes 786440 | tf_op jit(solution)/shard_map/ppermute | solution.py:12
  48.8 1.0 %copy.19 = bf16[256,1024]{1,0:T(8,128)(2,1)} copy(bf16[256,1024]{0,1:T(8,128)(2,1)S(1)} %bitcast.71) | data formatting | bytes 1048576
  49.8 5.7 %collective-permute-done.4 = f32[256,256]{0,1:T(8,128)S(1)} collective-permute-done((f32[256,256]{0,1:T(8,128)S(1)}, f32[256,256]{0,1:T(8,128)S(1)}, u32[]{:S(2)}, u32[]{:S(2)}) %collective-permute-start.4) | collective-permute-done | bytes 262176 | tf_op jit(solution)/shard_map/ppermute | solution.py:12
  55.5 1.9 %collective-permute-start.5 = (f32[256,256]{0,1:T(8,128)S(1)}, f32[256,256]{0,1:T(8,128)S(1)}, u32[]{:S(2)}, u32[]{:S(2)}) collective-permute-start(f32[256,256]{0,1:T(8,128)S(1)} %fusion.7), channel_id=1, source_target_pairs={{2,0},{4,2},{6,4},{8,6},{10,8},{12,10},{14,12},{16,14},{18,16},{20... | collective-permute-start | bytes 786440 | tf_op jit(solution)/shard_map/ppermute | solution.py:12
  57.4 2.9 %fusion.4 = bf16[128,8,256]{2,0,1:T(8,128)(2,1)S(1)} fusion(bf16[8,256,1024]{1,2,0:T(8,128)(2,1)} %copy-done, bf16[1024,256]{1,0:T(8,128)(2,1)S(1)} %bitcast.65), kind=kOutput, calls=%fused_computation.15 | convolution fusion | flops 537395200 | bytes 4980736 | tf_op jit(solution)/shard_map/htk,kd->thd/dot_general | solution.py:49
  60.3 1.0 %copy.20 = bf16[256,1024]{1,0:T(8,128)(2,1)} copy(bf16[256,1024]{0,1:T(8,128)(2,1)S(1)} %bitcast.66) | data formatting | bytes 1048576
  61.3 2.7 %collective-permute-done.5 = f32[256,256]{0,1:T(8,128)S(1)} collective-permute-done((f32[256,256]{0,1:T(8,128)S(1)}, f32[256,256]{0,1:T(8,128)S(1)}, u32[]{:S(2)}, u32[]{:S(2)}) %collective-permute-start.5) | collective-permute-done | bytes 262176 | tf_op jit(solution)/shard_map/ppermute | solution.py:12
  64.1 0.7 %copy.21 = bf16[256,128]{1,0:T(8,128)(2,1)} copy(bf16[256,128]{0,1:T(8,128)(2,1)S(1)} %get-tuple-element.9) | data formatting | bytes 131072
  64.9 0.7 %copy.22 = bf16[256,128]{1,0:T(8,128)(2,1)} copy(bf16[256,128]{0,1:T(8,128)(2,1)S(1)} %get-tuple-element.8) | data formatting | bytes 131072
  (9 shorter events, 0.2 us)
Async XLA Ops:
  2.3 5.6 %collective-permute-start = (bf16[256,256]{1,0:T(8,128)(2,1)S(1)}, bf16[256,256]{1,0:T(8,128)(2,1)S(1)}, u32[]{:S(2)}, u32[]{:S(2)}) collective-permute-start(bf16[256,256]{1,0:T(8,128)(2,1)S(1)} %constant_dynamic-update-slice_fusion), channel_id=1, source_target_pairs={{0,2},{2,4},{4,6},{6,8},{8,10},{10,12},{12,14},{14,16},{16,18},{18... | collective-permute-start | bytes 393224 | tf_op jit(solution)/shard_map/ppermute | solution.py:12
  8.0 9.3 %collective-permute-start.1 = (bf16[256,256]{1,0:T(8,128)(2,1)S(1)}, bf16[256,256]{1,0:T(8,128)(2,1)S(1)}, u32[]{:S(2)}, u32[]{:S(2)}) collective-permute-start(bf16[256,256]{1,0:T(8,128)(2,1)S(1)} %collective-permute-done), channel_id=1, source_target_pairs={{0,2},{2,4},{4,6},{6,8},{8,10},{10,12},{12,14},{14,16},{16,18},{18... | collective-permute-start | bytes 393224 | tf_op jit(solution)/shard_map/ppermute | solution.py:12
  17.3 5.0 %collective-permute-start.2 = (bf16[256,256]{1,0:T(8,128)(2,1)S(1)}, bf16[256,256]{1,0:T(8,128)(2,1)S(1)}, u32[]{:S(2)}, u32[]{:S(2)}) collective-permute-start(bf16[256,256]{1,0:T(8,128)(2,1)S(1)} %collective-permute-done.1), channel_id=1, source_target_pairs={{0,2},{2,4},{4,6},{6,8},{8,10},{10,12},{12,14},{14,16},{16,18},{18... | collective-permute-start | bytes 393224 | tf_op jit(solution)/shard_map/ppermute | solution.py:12
  34.0 1.9 %copy-start = (bf16[8,256,1024]{1,2,0:T(8,128)(2,1)}, bf16[8,256,1024]{1,2,0:T(8,128)(2,1)S(1)}, u32[]{:S(2)}) copy-start(bf16[8,256,1024]{1,2,0:T(8,128)(2,1)S(1)} %fusion.1) | copy-start | bytes 12582916
  37.5 9.3 %collective-permute-start.3 = (f32[256,256]{0,1:T(8,128)S(1)}, f32[256,256]{0,1:T(8,128)S(1)}, u32[]{:S(2)}, u32[]{:S(2)}) collective-permute-start(f32[256,256]{0,1:T(8,128)S(1)} %fusion.8), channel_id=1, source_target_pairs={{2,0},{4,2},{6,4},{8,6},{10,8},{12,10},{14,12},{16,14},{18,16},{20... | collective-permute-start | bytes 786440 | tf_op jit(solution)/shard_map/ppermute | solution.py:12
  46.8 8.6 %collective-permute-start.4 = (f32[256,256]{0,1:T(8,128)S(1)}, f32[256,256]{0,1:T(8,128)S(1)}, u32[]{:S(2)}, u32[]{:S(2)}) collective-permute-start(f32[256,256]{0,1:T(8,128)S(1)} %fusion.10), channel_id=1, source_target_pairs={{2,0},{4,2},{6,4},{8,6},{10,8},{12,10},{14,12},{16,14},{18,16},{20... | collective-permute-start | bytes 786440 | tf_op jit(solution)/shard_map/ppermute | solution.py:12
  55.5 8.6 %collective-permute-start.5 = (f32[256,256]{0,1:T(8,128)S(1)}, f32[256,256]{0,1:T(8,128)S(1)}, u32[]{:S(2)}, u32[]{:S(2)}) collective-permute-start(f32[256,256]{0,1:T(8,128)S(1)} %fusion.7), channel_id=1, source_target_pairs={{2,0},{4,2},{6,4},{8,6},{10,8},{12,10},{14,12},{16,14},{18,16},{20... | collective-permute-start | bytes 786440 | tf_op jit(solution)/shard_map/ppermute | solution.py:12
where the time goes:
time: 66.1 us; the launch traced here: 65.6 us
  waiting for transfers between devices  18.7 us (28%)
  starting transfers between devices  17.8 us (27%)
  matrix products  13.9 us (21%)
  local copies, waits for them, and re-layouts  10.4 us (16%)
  other arithmetic  3.95 us (6%)
  between operations  0.83 us (1%)
    ppermute x6, waiting for transfers between devices, from_behind(): return lax.ppermute(value, axis, pairs)  18.7 us
    ppermute x6, starting transfers between devices, from_behind(): return lax.ppermute(value, axis, pairs)  17.8 us
    unnamed x8, local copies, waits for them, and re-layouts  7.5 us
    dot_general x1, matrix products, block_grads(): jnp.einsum('thd,kd->htk', grad_heads, value_part, preferred_element_type=...  3.08 us
    dot_general x1, matrix products, block_grads(): jnp.einsum('htk,kd->thd', dscore, key_part, preferred_element_type=jnp.fl...  2.93 us
    dot_general x1, matrix products, block_grads(): jnp.einsum('htk,thd->kd', weights, grad_heads, preferred_element_type=jnp...  2.68 us
    dot_general x1, matrix products, block_grads(): jnp.einsum('htk,kd->thd', weights, value_part, preferred_element_type=jnp...  2.33 us
    reduce_sum x1, other arithmetic, block_grads(): jnp.sum(jnp.where(allowed[None], jnp.exp(scores - row_max), 0.0), axis=-1...  2.04 us
  transfers between devices with their start and end apart: 6, of which 5 were waited for; matrix products, arithmetic and copies ran while one was open for 15% of the time, Pallas kernels for 0%

commit v1 on v0

v1 whole, which is shorter than its diff:
```python
import functools

import jax
import jax.numpy as jnp
from jax import lax
from jax.experimental import pallas as pl
from jax.experimental.pallas import tpu as pltpu
from jax.sharding import PartitionSpec as P

LANES = 128
LOG2_E = 1.4426950408889634
MASKED = -1e30

OWN, MATE, LINE, SIDE = range(4)


def nt(a, b):
    return lax.dot_general(a, b, (((1,), (1,)), ((), ())), preferred_element_type=jnp.float32)


def nn(a, b):
    return lax.dot_general(a, b, (((1,), (0,)), ((), ())), preferred_element_type=jnp.float32)


def row_sums(rows):
    high = rows.astype(jnp.bfloat16)
    low = (rows - high.astype(jnp.float32)).astype(jnp.bfloat16)
    ones = jnp.ones((8, rows.shape[1]), jnp.bfloat16)
    return (nt(ones, high) + nt(ones, low))[:1]


def attend_kernel(
    doc_ref, q_ref, g_ref, own_ref, mate_ref, line_ref, side_ref,
    att_ref, gq_ref, own_out, mate_out, line_out, side_out,
    bias, s_ref, e_ref, acc_k, acc_v, kt_ref, vt_ref,
):
    rows, dim = q_ref.shape[0], own_ref.shape[1] // 2
    heads = q_ref.shape[1] // dim
    steps = rows // LANES
    scale = dim**-0.5
    here = lax.axis_index("ctx")
    odd = lax.rem(here, 2)
    count = lax.axis_size("ctx")
    kv_refs = (own_ref, mate_ref, line_ref, side_ref)
    behind = (0, 1 + 2 * odd, 2, 3 - 2 * odd)

    own_doc = jnp.concatenate([doc_ref[pl.ds(here * steps + i, 1), :] for i in range(steps)], axis=1)
    for b in range(4):
        block = here - behind[b]
        valid = block >= 0
        at = lax.rem(block + count, count) * steps
        for i in range(steps):
            row = jnp.where(valid, doc_ref[pl.ds(at + i, 1), :], -1)
            column = jnp.transpose(jnp.broadcast_to(row, (LANES, LANES)).astype(jnp.float32)).astype(jnp.int32)
            same = jnp.concatenate([column] * steps, axis=1) == own_doc
            if b == OWN:
                key_at = lax.broadcasted_iota(jnp.int32, (LANES, rows), 0) + i * LANES
                same = same & (key_at <= lax.broadcasted_iota(jnp.int32, (LANES, rows), 1))
            bias[b, i * LANES : (i + 1) * LANES, :] = jnp.where(same, 0.0, MASKED)
        kt_ref[b] = jnp.transpose(kv_refs[b][:, :dim])
        vt_ref[b] = jnp.transpose(kv_refs[b][:, dim:])

    for h in range(heads):
        cols = slice(h * dim, (h + 1) * dim)
        q, g = q_ref[:, cols], g_ref[:, cols]
        top = None
        for b in range(4):
            s = nt(kv_refs[b][:, :dim], q) + bias[b]
            s_ref[b] = s
            most = jnp.max(s, axis=0, keepdims=True)
            top = most if top is None else jnp.maximum(top, most)
        total, out = 0.0, 0.0
        for b in range(4):
            e = jnp.exp2((s_ref[b] - top) * (scale * LOG2_E))
            e_ref[b] = e
            total = total + jnp.sum(e, axis=0, keepdims=True)
            out = out + nn(vt_ref[b], e.astype(jnp.bfloat16))
        inverse = 1.0 / total
        out = jnp.transpose(out * inverse)
        att_ref[:, cols] = out.astype(jnp.bfloat16)
        delta = row_sums(out * g.astype(jnp.float32))
        grad = 0.0
        for b in range(4):
            probs = e_ref[b] * inverse
            ds = (probs * (nt(kv_refs[b][:, dim:], g) - delta)).astype(jnp.bfloat16)
            gv = nn(probs.astype(jnp.bfloat16), g)
            gk = nn(ds, q)
            acc_v[b] = gv if h == 0 else acc_v[b] + gv
            acc_k[b] = gk if h == 0 else acc_k[b] + gk
            grad = grad + nn(kt_ref[b], ds)
        gq_ref[:, cols] = jnp.transpose(grad * scale).astype(jnp.bfloat16)
    for b, out_ref in enumerate((own_out, mate_out, line_out, side_out)):
        out_ref[:, :dim] = (acc_k[b] * scale).astype(out_ref.dtype)
        out_ref[:, dim:] = acc_v[b].astype(out_ref.dtype)


def attend(docs, queries, grads, own, mate, line, side):
    rows, width = own.shape
    dim = width // 2
    pair = lambda kind: jax.ShapeDtypeStruct((rows, width), kind)
    vmem = pl.BlockSpec(memory_space=pltpu.VMEM)
    return pl.pallas_call(
        attend_kernel,
        out_shape=(
            jax.ShapeDtypeStruct(queries.shape, jnp.bfloat16),
            jax.ShapeDtypeStruct(queries.shape, jnp.bfloat16),
            pair(jnp.float32), pair(jnp.bfloat16), pair(jnp.float32), pair(jnp.bfloat16),
        ),
        in_specs=[vmem] * 7,
        out_specs=[vmem] * 6,
        scratch_shapes=[
            pltpu.VMEM((4, rows, rows), jnp.float32),
            pltpu.VMEM((4, rows, rows), jnp.float32),
            pltpu.VMEM((4, rows, rows), jnp.float32),
            pltpu.VMEM((4, rows, dim), jnp.float32),
            pltpu.VMEM((4, rows, dim), jnp.float32),
            pltpu.VMEM((4, dim, rows), jnp.bfloat16),
            pltpu.VMEM((4, dim, rows), jnp.bfloat16),
        ],
        compiler_params=pltpu.CompilerParams(vmem_limit_bytes=48 << 20),
    )(docs, queries, grads, own, mate, line, side)


def body(queries, key_vectors, value_vectors, doc_ids, grad_out):
    dim = key_vectors.shape[1]
    count = lax.axis_size("ctx")
    to_mate = [(i, i ^ 1) for i in range(count)]
    to_line = [(i, (i + 2) % count) for i in range(count)]
    to_side = [(i, (i + 1 + 2 * (i % 2)) % count) for i in range(count)]
    flip = lambda pairs: [(b, a) for a, b in pairs]

    own = jnp.concatenate([key_vectors, value_vectors], axis=1)
    line = lax.ppermute(own, "ctx", to_line)
    side = lax.ppermute(own, "ctx", to_side)
    mate = lax.ppermute(line, "ctx", to_mate)
    docs = doc_ids.reshape(-1, LANES)
    attended, grad_query, own_part, mate_part, line_part, side_part = attend(
        docs, queries, grad_out, own, mate, line, side
    )
    side_back = lax.ppermute(side_part, "ctx", flip(to_side))
    mate_back = lax.ppermute(mate_part, "ctx", to_mate)
    line_part = (line_part + mate_back.astype(jnp.float32)).astype(jnp.bfloat16)
    line_back = lax.ppermute(line_part, "ctx", flip(to_line))
    total = own_part + side_back.astype(jnp.float32) + line_back.astype(jnp.float32)
    total = total.astype(jnp.bfloat16)
    return attended, grad_query, total[:, :dim], total[:, dim:]


def solution(mesh):
    return jax.shard_map(
        body,
        mesh=mesh,
        in_specs=(P("ctx", "head"), P("ctx", "head"), P("ctx", "head"), P(), P("ctx", "head")),
        out_specs=(P("ctx", "head"), P("ctx", "head"), P("ctx", "head"), P("ctx", "head")),
        check_vma=False,
    )
```

time: 66.1 us -> 35.9 us (0.54)
  the two profiles are of different devices: /device:TPU:21 before, /device:TPU:0 now
where the time goes in v1:
time: 35.9 us; the launch traced here: 35.7 us
  waiting for transfers between devices  13.5 us (38%)
  Pallas kernels  12.4 us (35%)
  starting transfers between devices  5.4 us (15%)
  local copies, waits for them, and re-layouts  3.66 us (10%)
  between operations  0.68 us (2%)
    pallas_call x1, Pallas kernels, attend(): pl.pallas_call(attend_kernel, out_shape=(jax.ShapeDtypeStruct(queries.sha...  12.4 us
    ppermute x1, waiting for transfers between devices, body(): line = lax.ppermute(own, 'ctx', to_line)  7.3 us
    ppermute x1, waiting for transfers between devices, body(): side_back = lax.ppermute(side_part, 'ctx', flip(to_side))  3.07 us
    ppermute x1, starting transfers between devices, body(): line = lax.ppermute(own, 'ctx', to_line)  3.02 us
    unnamed x9, local copies, waits for them, and re-layouts  2.98 us
    ppermute x1, starting transfers between devices, body(): side_back = lax.ppermute(side_part, 'ctx', flip(to_side))  2.03 us
    ppermute x1, waiting for transfers between devices, body(): line_back = lax.ppermute(line_part, 'ctx', flip(to_line))  1.75 us
    ppermute x1, waiting for transfers between devices, body(): mate = lax.ppermute(line, 'ctx', to_mate)  1.34 us
  transfers between devices with their start and end apart: 6, of which 4 were waited for; matrix products, arithmetic and copies ran while one was open for 0% of the time, Pallas kernels for 0%

profile of v1, /device:TPU:0, one launch (start us, length us, event | category | flops | bytes accessed | tf_op | source)
XLA Modules:
  0.0 35.7 jit_solution(6605477554227235342)
XLA Ops:
  0.6 0.0 copy-start.3
  0.6 0.9 %constant_dynamic-update-slice_fusion.1 = bf16[256,256]{1,0:T(8,128)(2,1)S(1)} fusion(bf16[256,128]{1,0:T(8,128)(2,1)} %param.6), kind=kLoop, calls=%fused_computation.3 | loop fusion | bytes 131072
  1.5 0.0 copy-done.3
  1.5 0.0 copy-start.2
  1.6 3.0 %collective-permute-start = (bf16[256,256]{1,0:T(8,128)(2,1)S(1)}, bf16[256,256]{1,0:T(8,128)(2,1)S(1)}, u32[]{:S(2)}, u32[]{:S(2)}) collective-permute-start(bf16[256,256]{1,0:T(8,128)(2,1)S(1)} %constant_dynamic-update-slice_fusion.own_ref), channel_id=1, source_target_pairs={{0,4},{2,6},{4,8},{6,10},{8,12},{10,14},{12,16},{14,18},{16,20},{1... | collective-permute-start | bytes 393224 | tf_op jit(solution)/shard_map/ppermute | solution.py:133
  4.6 0.0 collective-permute-start.2
  4.6 7.3 %collective-permute-done.line_ref = bf16[256,256]{1,0:T(8,128)(2,1)S(1)} collective-permute-done((bf16[256,256]{1,0:T(8,128)(2,1)S(1)}, bf16[256,256]{1,0:T(8,128)(2,1)S(1)}, u32[]{:S(2)}, u32[]{:S(2)}) %collective-permute-start) | collective-permute-done | bytes 131104 | tf_op jit(solution)/shard_map/ppermute | solution.py:133
  11.9 0.0 collective-permute-start.1
  11.9 0.0 collective-permute-done.2.side_ref
  11.9 1.3 %collective-permute-done.1.mate_ref = bf16[256,256]{1,0:T(8,128)(2,1)S(1)} collective-permute-done((bf16[256,256]{1,0:T(8,128)(2,1)S(1)}, bf16[256,256]{1,0:T(8,128)(2,1)S(1)}, u32[]{:S(2)}, u32[]{:S(2)}) %collective-permute-start.1) | collective-permute-done | bytes 131104 | tf_op jit(solution)/shard_map/ppermute | solution.py:135
  13.2 0.0 copy-done.2
  13.2 0.0 copy-start
  13.3 1.0 %copy-done = bf16[256,1024]{1,0:T(8,128)(2,1)S(1)} copy-done((bf16[256,1024]{1,0:T(8,128)(2,1)S(1)}, bf16[256,1024]{1,0:T(8,128)(2,1)}, u32[]{:S(2)}) %copy-start) | copy-done | bytes 524312
  14.3 0.0 copy-start.1
  14.3 1.0 %copy-done.1 = bf16[256,1024]{1,0:T(8,128)(2,1)S(1)} copy-done((bf16[256,1024]{1,0:T(8,128)(2,1)S(1)}, bf16[256,1024]{1,0:T(8,128)(2,1)}, u32[]{:S(2)}) %copy-start.1) | copy-done | bytes 524312
  15.3 12.4 %shard_map.84 = (bf16[256,1024]{1,0:T(8,128)(2,1)}, bf16[256,1024]{1,0:T(8,128)(2,1)}, f32[256,256]{1,0:T(8,128)S(1)}, bf16[256,256]{1,0:T(8,128)(2,1)S(1)}, f32...) custom-call(s32[32,128]{1,0:T(8,128)S(1)} %bitcast.1, bf16[256,1024]{1,0:T(8,128)(2,1)S(1)} %copy-done, ...), custom_call_target="tpu_custom_call" | custom-call | tf_op jit(solution)/shard_map/pallas_call | solution.py:102
  27.7 0.1 collective-permute-start.4
  27.9 2.0 %collective-permute-start.3 = (bf16[256,256]{1,0:T(8,128)(2,1)S(1)}, bf16[256,256]{1,0:T(8,128)(2,1)S(1)}, u32[]{:S(2)}, u32[]{:S(2)}) collective-permute-start(bf16[256,256]{1,0:T(8,128)(2,1)S(1)} %get-tuple-element.13), channel_id=1, source_target_pairs={{2,0},{8,2},{6,4},{12,6},{10,8},{16,10},{14,12},{20,14},{18,16},{2... | collective-permute-start | bytes 393224 | tf_op jit(solution)/shard_map/ppermute | solution.py:140
  29.9 0.0 collective-permute-done.4
  29.9 0.2 collective-permute-start.5
  30.1 3.1 %collective-permute-done.3 = bf16[256,256]{1,0:T(8,128)(2,1)S(1)} collective-permute-done((bf16[256,256]{1,0:T(8,128)(2,1)S(1)}, bf16[256,256]{1,0:T(8,128)(2,1)S(1)}, u32[]{:S(2)}, u32[]{:S(2)}) %collective-permute-start.3) | collective-permute-done | bytes 131104 | tf_op jit(solution)/shard_map/ppermute | solution.py:140
  33.2 1.8 %collective-permute-done.5 = bf16[256,256]{1,0:T(8,128)(2,1)S(1)} collective-permute-done((bf16[256,256]{1,0:T(8,128)(2,1)S(1)}, bf16[256,256]{1,0:T(8,128)(2,1)S(1)}, u32[]{:S(2)}, u32[]{:S(2)}) %collective-permute-start.5) | collective-permute-done | bytes 131104 | tf_op jit(solution)/shard_map/ppermute | solution.py:143
  35.0 0.7 %fusion = (bf16[256,128]{1,0:T(8,128)(2,1)}, bf16[256,128]{1,0:T(8,128)(2,1)}) fusion(bf16[256,256]{1,0:T(8,128)(2,1)S(1)} %add_convert_fusion), kind=kLoop, calls=%fused_computation.4 | loop fusion | bytes 262144 | tf_op jit(solution)/shard_map/slice | solution.py:146
  (3 shorter events, 0.1 us)
Async XLA Ops:
  0.6 0.9 %copy-start.3 = (bf16[256,128]{1,0:T(8,128)(2,1)S(1)}, bf16[256,128]{1,0:T(8,128)(2,1)}, u32[]{:S(2)}) copy-start(bf16[256,128]{1,0:T(8,128)(2,1)} %param.7) | copy-start | bytes 196612
  1.5 11.7 %copy-start.2 = (s32[4096]{0:T(1024)S(1)}, s32[4096]{0:T(1024)}, u32[]{:S(2)}) copy-start(s32[4096]{0:T(1024)} %param.8) | copy-start | bytes 49156
  1.6 10.3 %collective-permute-start = (bf16[256,256]{1,0:T(8,128)(2,1)S(1)}, bf16[256,256]{1,0:T(8,128)(2,1)S(1)}, u32[]{:S(2)}, u32[]{:S(2)}) collective-permute-start(bf16[256,256]{1,0:T(8,128)(2,1)S(1)} %constant_dynamic-update-slice_fusion.own_ref), channel_id=1, source_target_pairs={{0,4},{2,6},{4,8},{6,10},{8,12},{10,14},{12,16},{14,18},{16,20},{1... | collective-permute-start | bytes 393224 | tf_op jit(solution)/shard_map/ppermute | solution.py:133
  4.6 7.3 %collective-permute-start.2 = (bf16[256,256]{1,0:T(8,128)(2,1)S(1)}, bf16[256,256]{1,0:T(8,128)(2,1)S(1)}, u32[]{:S(2)}, u32[]{:S(2)}) collective-permute-start(bf16[256,256]{1,0:T(8,128)(2,1)S(1)} %constant_dynamic-update-slice_fusion.own_ref), channel_id=1, source_target_pairs={{0,2},{2,8},{4,6},{6,12},{8,10},{10,16},{12,14},{14,20},{16,18},{1... | collective-permute-start | bytes 393224 | tf_op jit(solution)/shard_map/ppermute | solution.py:134
  11.9 1.3 %collective-permute-start.1 = (bf16[256,256]{1,0:T(8,128)(2,1)S(1)}, bf16[256,256]{1,0:T(8,128)(2,1)S(1)}, u32[]{:S(2)}, u32[]{:S(2)}) collective-permute-start(bf16[256,256]{1,0:T(8,128)(2,1)S(1)} %collective-permute-done.line_ref), channel_id=1, source_target_pairs={{0,2},{2,0},{4,6},{6,4},{8,10},{10,8},{12,14},{14,12},{16,18},{18,... | collective-permute-start | bytes 393224 | tf_op jit(solution)/shard_map/ppermute | solution.py:135
  13.2 1.0 %copy-start = (bf16[256,1024]{1,0:T(8,128)(2,1)S(1)}, bf16[256,1024]{1,0:T(8,128)(2,1)}, u32[]{:S(2)}) copy-start(bf16[256,1024]{1,0:T(8,128)(2,1)} %q_ref.1) | copy-start | bytes 1572868
  14.3 1.0 %copy-start.1 = (bf16[256,1024]{1,0:T(8,128)(2,1)S(1)}, bf16[256,1024]{1,0:T(8,128)(2,1)}, u32[]{:S(2)}) copy-start(bf16[256,1024]{1,0:T(8,128)(2,1)} %g_ref.1) | copy-start | bytes 1572868
  27.7 2.2 %collective-permute-start.4 = (bf16[256,256]{1,0:T(8,128)(2,1)S(1)}, bf16[256,256]{1,0:T(8,128)(2,1)S(1)}, u32[]{:S(2)}, u32[]{:S(2)}) collective-permute-start(bf16[256,256]{1,0:T(8,128)(2,1)S(1)} %get-tuple-element.15), channel_id=1, source_target_pairs={{0,2},{2,0},{4,6},{6,4},{8,10},{10,8},{12,14},{14,12},{16,18},{18,... | collective-permute-start | bytes 393224 | tf_op jit(solution)/shard_map/ppermute | solution.py:141
  27.9 5.3 %collective-permute-start.3 = (bf16[256,256]{1,0:T(8,128)(2,1)S(1)}, bf16[256,256]{1,0:T(8,128)(2,1)S(1)}, u32[]{:S(2)}, u32[]{:S(2)}) collective-permute-start(bf16[256,256]{1,0:T(8,128)(2,1)S(1)} %get-tuple-element.13), channel_id=1, source_target_pairs={{2,0},{8,2},{6,4},{12,6},{10,8},{16,10},{14,12},{20,14},{18,16},{2... | collective-permute-start | bytes 393224 | tf_op jit(solution)/shard_map/ppermute | solution.py:140
  29.9 5.0 %collective-permute-start.5 = (bf16[256,256]{1,0:T(8,128)(2,1)S(1)}, bf16[256,256]{1,0:T(8,128)(2,1)S(1)}, u32[]{:S(2)}, u32[]{:S(2)}) collective-permute-start(bf16[256,256]{1,0:T(8,128)(2,1)S(1)} %add_convert_fusion.1), channel_id=1, source_target_pairs={{4,0},{6,2},{8,4},{10,6},{12,8},{14,10},{16,12},{18,14},{20,16},{2... | collective-permute-start | bytes 393224 | tf_op jit(solution)/shard_map/ppermute | solution.py:143

commit v2 on v1

v2 whole, which is shorter than its diff:
```python
import jax
import jax.numpy as jnp
from jax import lax
from jax.experimental import pallas as pl
from jax.experimental.pallas import tpu as pltpu
from jax.sharding import PartitionSpec as P

LANES = 128
LOG2_E = 1.4426950408889634
MASKED = -1e30

OWN, MATE, LINE, SIDE = range(4)


def nt(a, b):
    return lax.dot_general(a, b, (((1,), (1,)), ((), ())), preferred_element_type=jnp.float32)


def nn(a, b):
    return lax.dot_general(a, b, (((1,), (0,)), ((), ())), preferred_element_type=jnp.float32)


def row_sums(rows):
    high = rows.astype(jnp.bfloat16)
    low = (rows - high.astype(jnp.float32)).astype(jnp.bfloat16)
    ones = jnp.ones((8, rows.shape[1]), jnp.bfloat16)
    return (nt(ones, high) + nt(ones, low))[:1]


def mask_bias(role, doc_ref, bias):
    rows = bias.shape[0]
    steps = rows // LANES
    here, count = lax.axis_index("ctx"), lax.axis_size("ctx")
    odd = lax.rem(here, 2)
    block = here - (0, 1 + 2 * odd, 2, 3 - 2 * odd)[role]
    at = lax.rem(block + count, count) * steps
    own_doc = jnp.concatenate([doc_ref[pl.ds(here * steps + i, 1), :] for i in range(steps)], axis=1)
    for i in range(steps):
        row = jnp.where(block >= 0, doc_ref[pl.ds(at + i, 1), :], -1)
        column = jnp.transpose(jnp.broadcast_to(row, (LANES, LANES)).astype(jnp.float32)).astype(jnp.int32)
        same = jnp.concatenate([column] * steps, axis=1) == own_doc
        if role == OWN:
            key_at = lax.broadcasted_iota(jnp.int32, (LANES, rows), 0) + i * LANES
            same = same & (key_at <= lax.broadcasted_iota(jnp.int32, (LANES, rows), 1))
        bias[i * LANES : (i + 1) * LANES, :] = jnp.where(same, 0.0, MASKED)


def forward(role, doc_ref, q_ref, kv_ref, e_ref, stat_ref, out_ref, bias, s_ref, vt_ref, ready=lambda h: None):
    dim = kv_ref.shape[1] // 2
    heads = q_ref.shape[1] // dim
    factor = dim**-0.5 * LOG2_E
    mask_bias(role, doc_ref, bias)
    vt_ref[...] = jnp.transpose(kv_ref[:, dim:])
    for h in range(heads):
        ready(h)
        s = nt(kv_ref[:, :dim], q_ref[:, h * dim : (h + 1) * dim]) + bias[...]
        s_ref[h] = s
        stat_ref[h : h + 1, :] = jnp.max(s, axis=0, keepdims=True)
    for h in range(heads):
        e = jnp.exp2((s_ref[h] - stat_ref[h : h + 1, :]) * factor)
        e_ref[h] = e.astype(jnp.bfloat16)
        stat_ref[heads + h : heads + h + 1, :] = jnp.sum(e, axis=0, keepdims=True)
    for h in range(heads):
        out_ref[h] = nn(vt_ref[...], e_ref[h])


def backward(q_ref, g_ref, kv_ref, e_ref, scale_ref, delta_ref, part_ref, gq_in, gq_out, kt_ref, p_ref, ds_ref):
    dim = kv_ref.shape[1] // 2
    heads = q_ref.shape[1] // dim
    cols = [slice(h * dim, (h + 1) * dim) for h in range(heads)]
    kt_ref[...] = jnp.transpose(kv_ref[:, :dim])
    for h in range(heads):
        probs = e_ref[h].astype(jnp.float32) * scale_ref[h : h + 1, :]
        p_ref[h] = probs.astype(jnp.bfloat16)
        ds_ref[h] = (probs * (nt(kv_ref[:, dim:], g_ref[:, cols[h]]) - delta_ref[h : h + 1, :])).astype(jnp.bfloat16)
    grad_v = sum(nn(p_ref[h], g_ref[:, cols[h]]) for h in range(heads))
    part_ref[:, dim:] = grad_v.astype(part_ref.dtype)
    grad_k = sum(nn(ds_ref[h], q_ref[:, cols[h]]) for h in range(heads))
    part_ref[:, :dim] = (grad_k * dim**-0.5).astype(part_ref.dtype)
    for h in range(heads):
        grad_q = nn(kt_ref[...], ds_ref[h])
        gq_out(h, grad_q if gq_in is None else gq_in[h] + grad_q)


def store_into(ref):
    def put(h, value):
        ref[h] = value

    return put


def pack_kernel(k_ref, v_ref, kv_ref, sems):
    dim = k_ref.shape[1]
    copies = [
        pltpu.make_async_copy(ref, kv_ref.at[:, i * dim : (i + 1) * dim], sems.at[i]) for i, ref in enumerate((k_ref, v_ref))
    ]
    for copy in copies:
        copy.start()
    for copy in copies:
        copy.wait()


def own_kernel(doc_ref, q_in, g_in, kv_ref, q_ref, g_ref, e_ref, stat_ref, out_ref, bias, s_ref, vt_ref, sems):
    dim = kv_ref.shape[1] // 2
    heads = q_in.shape[1] // dim
    cols = [slice(h * dim, (h + 1) * dim) for h in range(heads)]
    q_copies = [pltpu.make_async_copy(q_in.at[:, c], q_ref.at[:, c], sems.at[0, h]) for h, c in enumerate(cols)]
    g_copies = [pltpu.make_async_copy(g_in.at[:, c], g_ref.at[:, c], sems.at[1, h]) for h, c in enumerate(cols)]
    for copy in q_copies + g_copies:
        copy.start()
    forward(OWN, doc_ref, q_ref, kv_ref, e_ref, stat_ref, out_ref, bias, s_ref, vt_ref, lambda h: q_copies[h].wait())
    for copy in g_copies:
        copy.wait()


def rest_kernel(
    doc_ref, q_ref, g_ref, mate_ref, own_stat, own_o, line_stat, line_o, side_stat, side_o,
    att_ref, mate_part, gq_part, scale_ref, delta_ref,
    bias, s_ref, vt_ref, mate_e, mate_stat, mate_o, kt_ref, p_ref, ds_ref, att_buf, sems,
):
    dim = mate_ref.shape[1] // 2
    heads = q_ref.shape[1] // dim
    factor = dim**-0.5 * LOG2_E
    forward(MATE, doc_ref, q_ref, mate_ref, mate_e, mate_stat, mate_o, bias, s_ref, vt_ref)
    stats = (own_stat, mate_stat, line_stat, side_stat)
    tops = [ref[:heads, :] for ref in stats]
    top = jnp.maximum(jnp.maximum(tops[0], tops[1]), jnp.maximum(tops[2], tops[3]))
    parts = [jnp.exp2((t - top) * factor) for t in tops]
    inverse = 1.0 / sum(p * ref[heads:, :] for p, ref in zip(parts, stats))
    for b in range(4):
        scale_ref[b] = parts[b] * inverse
    copies = []
    for h in range(heads):
        cols = slice(h * dim, (h + 1) * dim)
        out = sum(ref[h] * scale_ref[b, h : h + 1, :] for b, ref in enumerate((own_o, mate_o, line_o, side_o)))
        out = jnp.transpose(out)
        att_buf[:, cols] = out.astype(jnp.bfloat16)
        copies.append(pltpu.make_async_copy(att_buf.at[:, cols], att_ref.at[:, cols], sems.at[h]))
        copies[h].start()
        delta_ref[h : h + 1, :] = row_sums(out * g_ref[:, cols].astype(jnp.float32))
    backward(
        q_ref, g_ref, mate_ref, mate_e, scale_ref.at[MATE], delta_ref, mate_part, None, store_into(gq_part), kt_ref, p_ref, ds_ref
    )
    for copy in copies:
        copy.wait()


def later_kernel(role, q_ref, g_ref, kv_ref, e_ref, scale_ref, delta_ref, gq_in, part_ref, gq_ref, kt_ref, p_ref, ds_ref):
    backward(
        q_ref, g_ref, kv_ref, e_ref, scale_ref.at[role], delta_ref, part_ref, gq_in, store_into(gq_ref), kt_ref, p_ref, ds_ref
    )


def last_kernel(
    role, q_ref, g_ref, kv_ref, e_ref, scale_ref, delta_ref, gq_in, part_ref, gq_ref, kt_ref, p_ref, ds_ref, buf, sems
):
    dim = kv_ref.shape[1] // 2
    copies = []

    def put(h, value):
        cols = slice(h * dim, (h + 1) * dim)
        buf[:, cols] = jnp.transpose(value * dim**-0.5).astype(jnp.bfloat16)
        copies.append(pltpu.make_async_copy(buf.at[:, cols], gq_ref.at[:, cols], sems.at[h]))
        copies[h].start()

    backward(q_ref, g_ref, kv_ref, e_ref, scale_ref.at[role], delta_ref, part_ref, gq_in, put, kt_ref, p_ref, ds_ref)
    for copy in copies:
        copy.wait()


def call(name, kernel, args, outs, scratch, flops, far_in=(), far_out=()):
    near, far = pl.BlockSpec(memory_space=pltpu.VMEM), pl.BlockSpec(memory_space=pltpu.HBM)
    args = [pltpu.with_memory_space_constraint(a, pltpu.HBM) if i in far_in else a for i, a in enumerate(args)]
    return pl.pallas_call(
        kernel,
        name=name,
        out_shape=outs,
        in_specs=[far if i in far_in else near for i in range(len(args))],
        out_specs=[far if i in far_out else near for i in range(len(outs))],
        scratch_shapes=scratch,
        cost_estimate=pl.CostEstimate(flops=flops, bytes_accessed=1 << 20, transcendentals=0),
        compiler_params=pltpu.CompilerParams(vmem_limit_bytes=16 << 20),
    )(*args)


def body(queries, key_vectors, value_vectors, doc_ids, grad_out):
    rows, dim = key_vectors.shape
    heads = queries.shape[1] // dim
    count = lax.axis_size("ctx")
    to_mate = [(i, i ^ 1) for i in range(count)]
    to_line = [(i, (i + 2) % count) for i in range(count)]
    to_side = [(i, (i + 1 + 2 * (i % 2)) % count) for i in range(count)]
    flip = lambda pairs: [(b, a) for a, b in pairs]
    f32, bf16 = jnp.float32, jnp.bfloat16
    shape = jax.ShapeDtypeStruct
    e_shape, stat_shape, out_shape = shape((heads, rows, rows), bf16), shape((2 * heads, rows), f32), shape((heads, dim, rows), f32)
    pair, pair_sent = shape((rows, 2 * dim), f32), shape((rows, 2 * dim), bf16)
    wide = shape(queries.shape, bf16)
    buffer = lambda like: pltpu.VMEM(like.shape, like.dtype)
    flat = pltpu.VMEM((dim, rows), bf16)
    ahead = [pltpu.VMEM((rows, rows), f32), pltpu.VMEM((heads, rows, rows), f32), flat]
    back = [flat, buffer(e_shape), buffer(e_shape)]
    work = 16 * heads * rows * rows * dim

    docs = doc_ids.reshape(-1, LANES)
    own = call(
        "pack", pack_kernel, (key_vectors, value_vectors), (pair_sent,), [pltpu.SemaphoreType.DMA((2,))], 0, (0, 1)
    )[0]
    line = lax.ppermute(own, "ctx", to_line)
    side = lax.ppermute(own, "ctx", to_side)
    q, g, own_e, own_stat, own_o = call(
        "own_forward", own_kernel, (docs, queries, grad_out, own), (wide, wide, e_shape, stat_shape, out_shape),
        [*ahead, pltpu.SemaphoreType.DMA((2, heads))], 2 * work, (1, 2),
    )
    line, own_stat = lax.optimization_barrier((line, own_stat))
    mate = lax.ppermute(line, "ctx", to_mate)

    def first(name, role, kv):
        return call(
            name, lambda *refs: forward(role, *refs), (docs, q, kv), (e_shape, stat_shape, out_shape), ahead, 2 * work
        )

    line_e, line_stat, line_o = first("line_forward", LINE, line)
    side_e, side_stat, side_o = first("side_forward", SIDE, side)
    attended, mate_part, gq, scales, delta = call(
        "rest_forward", rest_kernel,
        (docs, q, g, mate, own_stat, own_o, line_stat, line_o, side_stat, side_o),
        (wide, pair_sent, out_shape, shape((4, heads, rows), f32), shape((heads, rows), f32)),
        [*ahead, buffer(e_shape), buffer(stat_shape), buffer(out_shape), *back, buffer(wide), pltpu.SemaphoreType.DMA((heads,))],
        6 * work, (), (0,),
    )
    mate_back = lax.ppermute(mate_part, "ctx", to_mate)

    def later(name, kernel, role, kv, e, gq, outs, extra=(), far_out=()):
        return call(
            name, lambda *refs: kernel(role, *refs), (q, g, kv, e, scales, delta, gq), outs, [*back, *extra], 4 * work,
            (), far_out,
        )

    line_part, gq = later("line_backward", later_kernel, LINE, line, line_e, gq, (pair, out_shape))
    line_part = (line_part + mate_back.astype(f32)).astype(bf16)
    line_part, gq = lax.optimization_barrier((line_part, gq))
    line_back = lax.ppermute(line_part, "ctx", flip(to_line))
    side_part, gq = later("side_backward", later_kernel, SIDE, side, side_e, gq, (pair_sent, out_shape))
    side_back = lax.ppermute(side_part, "ctx", flip(to_side))
    own_part, grad_query = later(
        "own_backward", last_kernel, OWN, own, own_e, gq, (pair, wide), [buffer(wide), pltpu.SemaphoreType.DMA((heads,))], (1,)
    )
    total = (own_part + side_back.astype(f32) + line_back.astype(f32)).astype(bf16)
    return attended, grad_query, total[:, :dim], total[:, dim:]


def solution(mesh):
    return jax.shard_map(
        body,
        mesh=mesh,
        in_specs=(P("ctx", "head"), P("ctx", "head"), P("ctx", "head"), P(), P("ctx", "head")),
        out_specs=(P("ctx", "head"), P("ctx", "head"), P("ctx", "head"), P("ctx", "head")),
        check_vma=False,
    )
```

time: 35.9 us -> 28.6 us (0.80)
  waiting for transfers between devices: 13.5 us -> 6.96 us
  local copies, waits for them, and re-layouts: 3.66 us -> 0.67 us
  Pallas kernels: 12.4 us -> 14 us
  starting transfers between devices: 5.4 us -> 5.91 us
    ppermute x1, waiting for transfers between devices: 7.3 us -> 4 us  [body(): line = lax.ppermute(own, 'ctx', to_line)]
    unnamed x9 -> x2, local copies, waits for them, and re-layouts: 2.98 us -> 0.01 us
    ppermute x1, waiting for transfers between devices: 3.07 us -> 0.45 us  [body(): side_back = lax.ppermute(side_part, 'ctx', flip(to_side))]
    pallas_call x1 -> x8, Pallas kernels: 12.4 us -> 14 us  [call(): pl.pallas_call(kernel, name=name, out_shape=outs, in_specs=[far if i in f...]
    ppermute x1, waiting for transfers between devices: 1.34 us -> 0.01 us  [body(): mate = lax.ppermute(line, 'ctx', to_mate)]
    ppermute x1, starting transfers between devices: 0.01 us -> 0.88 us  [body(): mate = lax.ppermute(line, 'ctx', to_mate)]
    ppermute x1, waiting for transfers between devices: 1.75 us -> 2.42 us  [body(): line_back = lax.ppermute(line_part, 'ctx', flip(to_line))]
    ppermute x1, starting transfers between devices: 0.01 us -> 0.5 us  [body(): side = lax.ppermute(own, 'ctx', to_side)]
  transfers between devices with their start and end apart: 6 -> 6, of which waited for: 4 -> 4; matrix products, arithmetic and copies ran while one was open for 0% -> 0% of each run, Pallas kernels for 0% -> 31%
where the time goes in v2:
time: 28.6 us; the launch traced here: 28.4 us
  Pallas kernels  14 us (49%)
  waiting for transfers between devices  6.96 us (24%)
  starting transfers between devices  5.91 us (21%)
  between operations  0.74 us (3%)
  local copies, waits for them, and re-layouts  0.67 us (2%)
    pallas_call x8, Pallas kernels, call(): pl.pallas_call(kernel, name=name, out_shape=outs, in_specs=[far if i in f...  14 us
    ppermute x1, waiting for transfers between devices, body(): line = lax.ppermute(own, 'ctx', to_line)  4 us
    ppermute x1, starting transfers between devices, body(): line = lax.ppermute(own, 'ctx', to_line)  2.58 us
    ppermute x1, waiting for transfers between devices, body(): line_back = lax.ppermute(line_part, 'ctx', flip(to_line))  2.42 us
    ppermute x1, starting transfers between devices, body(): side_back = lax.ppermute(side_part, 'ctx', flip(to_side))  1.87 us
    ppermute x1, starting transfers between devices, body(): mate = lax.ppermute(line, 'ctx', to_mate)  0.88 us
    slice x1, local copies, waits for them, and re-layouts, body(): return (attended, grad_query, total[:, :dim], total[:, dim:])  0.66 us
  transfers between devices with their start and end apart: 6, of which 4 were waited for; matrix products, arithmetic and copies ran while one was open for 0% of the time, Pallas kernels for 31%

profile of v2, /device:TPU:0, one launch (start us, length us, event | category | flops | bytes accessed | tf_op | source)
XLA Modules:
  0.0 28.4 jit_solution(5158495067457612719)
XLA Ops:
  0.6 0.0 copy-start
  0.6 0.9 %pack.1.kv_ref.refs_2_ = bf16[256,256]{1,0:T(8,128)(2,1)S(1)} custom-call(bf16[256,128]{1,0:T(8,128)(2,1)} %k_ref.1, bf16[256,128]{1,0:T(8,128)(2,1)} %v_ref.1), custom_call_target="tpu_custom_call" | custom-call | bytes 1048576 | tf_op jit(solution)/shard_map/pack/pallas_call | solution.py:174
  1.5 0.5 %collective-permute-start.2 = (bf16[256,256]{1,0:T(8,128)(2,1)S(1)}, bf16[256,256]{1,0:T(8,128)(2,1)S(1)}, u32[]{:S(2)}, u32[]{:S(2)}) collective-permute-start(bf16[256,256]{1,0:T(8,128)(2,1)S(1)} %pack.1.kv_ref.refs_2_), channel_id=1, source_target_pairs={{0,2},{2,8},{4,6},{6,12},{8,10},{10,16},{12,14},{14,20},{16,18},{1... | collective-permute-start | bytes 393224 | tf_op jit(solution)/shard_map/ppermute | solution.py:210
  2.0 2.6 %collective-permute-start = (bf16[256,256]{1,0:T(8,128)(2,1)S(1)}, bf16[256,256]{1,0:T(8,128)(2,1)S(1)}, u32[]{:S(2)}, u32[]{:S(2)}) collective-permute-start(bf16[256,256]{1,0:T(8,128)(2,1)S(1)} %pack.1.kv_ref.refs_2_), channel_id=1, source_target_pairs={{0,4},{2,6},{4,8},{6,10},{8,12},{10,14},{12,16},{14,18},{16,20},{1... | collective-permute-start | bytes 393224 | tf_op jit(solution)/shard_map/ppermute | solution.py:209
  4.6 0.0 copy-done
  4.6 3.3 %own_forward.1 = (bf16[256,1024]{1,0:T(8,128)(2,1)S(1)}, bf16[256,1024]{1,0:T(8,128)(2,1)S(1)}, bf16[8,256,256]{2,1,0:T(8,128)(2,1)S(1)}, f32[16,256]{1,0:T(8,128)S(1)}, f32[8,128,256]{2,1,0:T(8,128)S(1)}) custom-call(s32[32,128]{1,0:T(8,128)S(1)} %bitcast.1, bf16[256,1024]{1,0:T(8,128)(2,1)} %q_in.1, bf16[256,1024]{1,0:T(8,128)(2,1)} %g_in.1, ...), custom_call_target="tpu_custom_call" | custom-call | flops 2147483648 | bytes 1048576 | tf_op jit(solution)/shard_map/own_forward/pallas_call | solution.py:174
  7.9 4.0 %collective-permute-done.refs_2_ = bf16[256,256]{1,0:T(8,128)(2,1)S(1)} collective-permute-done((bf16[256,256]{1,0:T(8,128)(2,1)S(1)}, bf16[256,256]{1,0:T(8,128)(2,1)S(1)}, u32[]{:S(2)}, u32[]{:S(2)}) %collective-permute-start) | collective-permute-done | bytes 131104 | tf_op jit(solution)/shard_map/ppermute | solution.py:209
  11.9 0.9 %collective-permute-start.1 = (bf16[256,256]{1,0:T(8,128)(2,1)S(1)}, bf16[256,256]{1,0:T(8,128)(2,1)S(1)}, u32[]{:S(2)}, u32[]{:S(2)}) collective-permute-start(bf16[256,256]{1,0:T(8,128)(2,1)S(1)} %collective-permute-done.refs_2_), channel_id=1, source_target_pairs={{0,2},{2,0},{4,6},{6,4},{8,10},{10,8},{12,14},{14,12},{16,18},{18,... | collective-permute-start | bytes 393224 | tf_op jit(solution)/shard_map/ppermute | solution.py:216
  12.8 1.2 %line_forward.1 = (bf16[8,256,256]{2,1,0:T(8,128)(2,1)S(1)}, f32[16,256]{1,0:T(8,128)S(1)}, f32[8,128,256]{2,1,0:T(8,128)S(1)}) custom-call(s32[32,128]{1,0:T(8,128)S(1)} %bitcast.2, bf16[256,1024]{1,0:T(8,128)(2,1)S(1)} %get-tuple-element.30.refs_1_.q_ref.refs_0_, bf16[256,256]{1,0:T(8,128)(2,1)S(1)} %collective-permute-done.refs_2_), custom_call_target="tpu_custom_call" | custom-call | flops 2147483648 | bytes 1048576 | tf_op jit(solution)/shard_map/line_forward/pallas_call | solution.py:174
  14.0 0.0 collective-permute-done.2.refs_2_
  14.0 1.1 %side_forward.1 = (bf16[8,256,256]{2,1,0:T(8,128)(2,1)S(1)}, f32[16,256]{1,0:T(8,128)S(1)}, f32[8,128,256]{2,1,0:T(8,128)S(1)}) custom-call(s32[32,128]{1,0:T(8,128)S(1)} %bitcast.3, bf16[256,1024]{1,0:T(8,128)(2,1)S(1)} %get-tuple-element.30.refs_1_.q_ref.refs_0_, bf16[256,256]{1,0:T(8,128)(2,1)S(1)} %collective-permute-done.2.refs_2_), custom_call_target="tpu_custom_call" | custom-call | flops 2147483648 | bytes 1048576 | tf_op jit(solution)/shard_map/side_forward/pallas_call | solution.py:174
  15.2 0.0 collective-permute-done.1.mate_ref
  15.2 2.9 %rest_forward.1 = (bf16[256,1024]{1,0:T(8,128)(2,1)}, bf16[256,256]{1,0:T(8,128)(2,1)S(1)}, f32[8,128,256]{2,1,0:T(8,128)S(1)}, f32[4,8,256]{2,1,0:T(8,128)S(1)}, f32[8,256]{1,0:T(8,128)S(1)}) custom-call(s32[32,128]{1,0:T(8,128)S(1)} %bitcast.4, bf16[256,1024]{1,0:T(8,128)(2,1)S(1)} %get-tuple-element.30.refs_1_.q_ref.refs_0_, ...), custom_call_target="tpu_custom_call" | custom-call | flops 6442450944 | bytes 1048576 | tf_op jit(solution)/shard_map/rest_forward/pallas_call | solution.py:174
  18.1 0.1 collective-permute-start.3
  18.2 1.3 %line_backward.1 = (f32[256,256]{1,0:T(8,128)S(1)}, f32[8,128,256]{2,1,0:T(8,128)S(1)}) custom-call(bf16[256,1024]{1,0:T(8,128)(2,1)S(1)} %get-tuple-element.30.refs_1_.q_ref.refs_0_, bf16[256,1024]{1,0:T(8,128)(2,1)S(1)} %get-tuple-element.31.g_ref.refs_1_, bf16[256,256]{1,0:T(8,128)(2,1)S(1)} %collective-permute-done.refs_2_, ...), custom_call_target="tpu_custom_call" | custom-call | flops 4294967296 | bytes 1048576 | tf_op jit(solution)/shard_map/line_backward/pallas_call | solution.py:174
  19.4 0.1 collective-permute-done.3
  19.6 1.2 %side_backward.1 = (bf16[256,256]{1,0:T(8,128)(2,1)S(1)}, f32[8,128,256]{2,1,0:T(8,128)S(1)}) custom-call(bf16[256,1024]{1,0:T(8,128)(2,1)S(1)} %get-tuple-element.30.refs_1_.q_ref.refs_0_, bf16[256,1024]{1,0:T(8,128)(2,1)S(1)} %get-tuple-element.31.g_ref.refs_1_, bf16[256,256]{1,0:T(8,128)(2,1)S(1)} %collective-permute-done.2.refs_2_, ...), custom_call_target="tpu_custom_call" | custom-call | flops 4294967296 | bytes 1048576 | tf_op jit(solution)/shard_map/side_backward/pallas_call | solution.py:174
  20.8 1.9 %collective-permute-start.4 = (bf16[256,256]{1,0:T(8,128)(2,1)S(1)}, bf16[256,256]{1,0:T(8,128)(2,1)S(1)}, u32[]{:S(2)}, u32[]{:S(2)}) collective-permute-start(bf16[256,256]{1,0:T(8,128)(2,1)S(1)} %get-tuple-element.54), channel_id=1, source_target_pairs={{2,0},{8,2},{6,4},{12,6},{10,8},{16,10},{14,12},{20,14},{18,16},{2... | collective-permute-start | bytes 393224 | tf_op jit(solution)/shard_map/ppermute | solution.py:245
  22.7 0.0 collective-permute-start.5
  22.7 2.1 %own_backward.1 = (f32[256,256]{1,0:T(8,128)S(1)}, bf16[256,1024]{1,0:T(8,128)(2,1)}) custom-call(bf16[256,1024]{1,0:T(8,128)(2,1)S(1)} %get-tuple-element.30.refs_1_.q_ref.refs_0_, bf16[256,1024]{1,0:T(8,128)(2,1)S(1)} %get-tuple-element.31.g_ref.refs_1_, bf16[256,256]{1,0:T(8,128)(2,1)S(1)} %pack.1.kv_ref.refs_2_, ...), custom_call_target="tpu_custom_call" | custom-call | flops 4294967296 | bytes 1048576 | tf_op jit(solution)/shard_map/own_backward/pallas_call | solution.py:174
  24.8 0.5 %collective-permute-done.4 = bf16[256,256]{1,0:T(8,128)(2,1)S(1)} collective-permute-done((bf16[256,256]{1,0:T(8,128)(2,1)S(1)}, bf16[256,256]{1,0:T(8,128)(2,1)S(1)}, u32[]{:S(2)}, u32[]{:S(2)}) %collective-permute-start.4) | collective-permute-done | bytes 131104 | tf_op jit(solution)/shard_map/ppermute | solution.py:245
  25.2 2.4 %collective-permute-done.5 = bf16[256,256]{1,0:T(8,128)(2,1)S(1)} collective-permute-done((bf16[256,256]{1,0:T(8,128)(2,1)S(1)}, bf16[256,256]{1,0:T(8,128)(2,1)S(1)}, u32[]{:S(2)}, u32[]{:S(2)}) %collective-permute-start.5) | collective-permute-done | bytes 131104 | tf_op jit(solution)/shard_map/ppermute | solution.py:243
  27.7 0.7 %fusion = (bf16[256,128]{1,0:T(8,128)(2,1)}, bf16[256,128]{1,0:T(8,128)(2,1)}) fusion(bf16[256,256]{1,0:T(8,128)(2,1)S(1)} %add_convert_fusion), kind=kLoop, calls=%fused_computation.2 | loop fusion | bytes 262144 | tf_op jit(solution)/shard_map/slice | solution.py:250
  (2 shorter events, 0.1 us)
Async XLA Ops:
  0.6 4.0 %copy-start = (s32[4096]{0:T(1024)S(1)}, s32[4096]{0:T(1024)}, u32[]{:S(2)}) copy-start(s32[4096]{0:T(1024)} %param.8) | copy-start | bytes 49156
  1.5 12.4 %collective-permute-start.2 = (bf16[256,256]{1,0:T(8,128)(2,1)S(1)}, bf16[256,256]{1,0:T(8,128)(2,1)S(1)}, u32[]{:S(2)}, u32[]{:S(2)}) collective-permute-start(bf16[256,256]{1,0:T(8,128)(2,1)S(1)} %pack.1.kv_ref.refs_2_), channel_id=1, source_target_pairs={{0,2},{2,8},{4,6},{6,12},{8,10},{10,16},{12,14},{14,20},{16,18},{1... | collective-permute-start | bytes 393224 | tf_op jit(solution)/shard_map/ppermute | solution.py:210
  2.0 9.9 %collective-permute-start = (bf16[256,256]{1,0:T(8,128)(2,1)S(1)}, bf16[256,256]{1,0:T(8,128)(2,1)S(1)}, u32[]{:S(2)}, u32[]{:S(2)}) collective-permute-start(bf16[256,256]{1,0:T(8,128)(2,1)S(1)} %pack.1.kv_ref.refs_2_), channel_id=1, source_target_pairs={{0,4},{2,6},{4,8},{6,10},{8,12},{10,14},{12,16},{14,18},{16,20},{1... | collective-permute-start | bytes 393224 | tf_op jit(solution)/shard_map/ppermute | solution.py:209
  11.9 3.2 %collective-permute-start.1 = (bf16[256,256]{1,0:T(8,128)(2,1)S(1)}, bf16[256,256]{1,0:T(8,128)(2,1)S(1)}, u32[]{:S(2)}, u32[]{:S(2)}) collective-permute-start(bf16[256,256]{1,0:T(8,128)(2,1)S(1)} %collective-permute-done.refs_2_), channel_id=1, source_target_pairs={{0,2},{2,0},{4,6},{6,4},{8,10},{10,8},{12,14},{14,12},{16,18},{18,... | collective-permute-start | bytes 393224 | tf_op jit(solution)/shard_map/ppermute | solution.py:216
  18.1 1.4 %collective-permute-start.3 = (bf16[256,256]{1,0:T(8,128)(2,1)S(1)}, bf16[256,256]{1,0:T(8,128)(2,1)S(1)}, u32[]{:S(2)}, u32[]{:S(2)}) collective-permute-start(bf16[256,256]{1,0:T(8,128)(2,1)S(1)} %get-tuple-element.48), channel_id=1, source_target_pairs={{0,2},{2,0},{4,6},{6,4},{8,10},{10,8},{12,14},{14,12},{16,18},{18,... | collective-permute-start | bytes 393224 | tf_op jit(solution)/shard_map/ppermute | solution.py:232
  20.8 4.4 %collective-permute-start.4 = (bf16[256,256]{1,0:T(8,128)(2,1)S(1)}, bf16[256,256]{1,0:T(8,128)(2,1)S(1)}, u32[]{:S(2)}, u32[]{:S(2)}) collective-permute-start(bf16[256,256]{1,0:T(8,128)(2,1)S(1)} %get-tuple-element.54), channel_id=1, source_target_pairs={{2,0},{8,2},{6,4},{12,6},{10,8},{16,10},{14,12},{20,14},{18,16},{2... | collective-permute-start | bytes 393224 | tf_op jit(solution)/shard_map/ppermute | solution.py:245
  22.7 5.0 %collective-permute-start.5 = (bf16[256,256]{1,0:T(8,128)(2,1)S(1)}, bf16[256,256]{1,0:T(8,128)(2,1)S(1)}, u32[]{:S(2)}, u32[]{:S(2)}) collective-permute-start(bf16[256,256]{1,0:T(8,128)(2,1)S(1)} %add_convert_fusion.1), channel_id=1, source_target_pairs={{4,0},{6,2},{8,4},{10,6},{12,8},{14,10},{16,12},{18,14},{20,16},{2... | collective-permute-start | bytes 393224 | tf_op jit(solution)/shard_map/ppermute | solution.py:243

commit v3 on v2

--- a/solution.py
+++ b/solution.py
@@ -73,13 +73,13 @@
         probs = e_ref[h].astype(jnp.float32) * scale_ref[h : h + 1, :]
         p_ref[h] = probs.astype(jnp.bfloat16)
         ds_ref[h] = (probs * (nt(kv_ref[:, dim:], g_ref[:, cols[h]]) - delta_ref[h : h + 1, :])).astype(jnp.bfloat16)
+    for h in range(heads):
+        grad_q = nn(kt_ref[...], ds_ref[h])
+        gq_out(h, grad_q if gq_in is None else gq_in[h] + grad_q)
     grad_v = sum(nn(p_ref[h], g_ref[:, cols[h]]) for h in range(heads))
     part_ref[:, dim:] = grad_v.astype(part_ref.dtype)
     grad_k = sum(nn(ds_ref[h], q_ref[:, cols[h]]) for h in range(heads))
     part_ref[:, :dim] = (grad_k * dim**-0.5).astype(part_ref.dtype)
-    for h in range(heads):
-        grad_q = nn(kt_ref[...], ds_ref[h])
-        gq_out(h, grad_q if gq_in is None else gq_in[h] + grad_q)
 
 
 def store_into(ref):
@@ -100,17 +100,8 @@
         copy.wait()
 
 
-def own_kernel(doc_ref, q_in, g_in, kv_ref, q_ref, g_ref, e_ref, stat_ref, out_ref, bias, s_ref, vt_ref, sems):
-    dim = kv_ref.shape[1] // 2
-    heads = q_in.shape[1] // dim
-    cols = [slice(h * dim, (h + 1) * dim) for h in range(heads)]
-    q_copies = [pltpu.make_async_copy(q_in.at[:, c], q_ref.at[:, c], sems.at[0, h]) for h, c in enumerate(cols)]
-    g_copies = [pltpu.make_async_copy(g_in.at[:, c], g_ref.at[:, c], sems.at[1, h]) for h, c in enumerate(cols)]
-    for copy in q_copies + g_copies:
-        copy.start()
-    forward(OWN, doc_ref, q_ref, kv_ref, e_ref, stat_ref, out_ref, bias, s_ref, vt_ref, lambda h: q_copies[h].wait())
-    for copy in g_copies:
-        copy.wait()
+def settle_kernel(in_ref, out_ref):
+    out_ref[:16, :] = in_ref[:16, :]
 
 
 def rest_kernel(
@@ -168,7 +159,7 @@
         copy.wait()
 
 
-def call(name, kernel, args, outs, scratch, flops, far_in=(), far_out=()):
+def call(name, kernel, args, outs, scratch, flops, far_in=(), far_out=(), aliases=None):
     near, far = pl.BlockSpec(memory_space=pltpu.VMEM), pl.BlockSpec(memory_space=pltpu.HBM)
     args = [pltpu.with_memory_space_constraint(a, pltpu.HBM) if i in far_in else a for i, a in enumerate(args)]
     return pl.pallas_call(
@@ -178,7 +169,8 @@
         in_specs=[far if i in far_in else near for i in range(len(args))],
         out_specs=[far if i in far_out else near for i in range(len(outs))],
         scratch_shapes=scratch,
-        cost_estimate=pl.CostEstimate(flops=flops, bytes_accessed=1 << 20, transcendentals=0),
+        input_output_aliases=aliases or {},
+        cost_estimate=pl.CostEstimate(flops=flops, bytes_accessed=0, transcendentals=0),
         compiler_params=pltpu.CompilerParams(vmem_limit_bytes=16 << 20),
     )(*args)
 
@@ -200,25 +192,25 @@
     flat = pltpu.VMEM((dim, rows), bf16)
     ahead = [pltpu.VMEM((rows, rows), f32), pltpu.VMEM((heads, rows, rows), f32), flat]
     back = [flat, buffer(e_shape), buffer(e_shape)]
-    work = 16 * heads * rows * rows * dim
+    work = heads * rows
 
     docs = doc_ids.reshape(-1, LANES)
     own = call(
         "pack", pack_kernel, (key_vectors, value_vectors), (pair_sent,), [pltpu.SemaphoreType.DMA((2,))], 0, (0, 1)
     )[0]
+    own = call("settle", settle_kernel, (own,), (pair_sent,), [], 1 << 33, (), (), {0: 0})[0]
     line = lax.ppermute(own, "ctx", to_line)
     side = lax.ppermute(own, "ctx", to_side)
-    q, g, own_e, own_stat, own_o = call(
-        "own_forward", own_kernel, (docs, queries, grad_out, own), (wide, wide, e_shape, stat_shape, out_shape),
-        [*ahead, pltpu.SemaphoreType.DMA((2, heads))], 2 * work, (1, 2),
-    )
-    line, own_stat = lax.optimization_barrier((line, own_stat))
-    mate = lax.ppermute(line, "ctx", to_mate)
+    q, g = queries, grad_out
 
     def first(name, role, kv):
         return call(
             name, lambda *refs: forward(role, *refs), (docs, q, kv), (e_shape, stat_shape, out_shape), ahead, 2 * work
         )
+
+    own_e, own_stat, own_o = first("own_forward", OWN, own)
+    line, own_stat = lax.optimization_barrier((line, own_stat))
+    mate = lax.ppermute(line, "ctx", to_mate)
 
     line_e, line_stat, line_o = first("line_forward", LINE, line)
     side_e, side_stat, side_o = first("side_forward", SIDE, side)
@@ -240,13 +232,14 @@
     line_part, gq = later("line_backward", later_kernel, LINE, line, line_e, gq, (pair, out_shape))
     line_part = (line_part + mate_back.astype(f32)).astype(bf16)
     line_part, gq = lax.optimization_barrier((line_part, gq))
-    line_back = lax.ppermute(line_part, "ctx", flip(to_line))
     side_part, gq = later("side_backward", later_kernel, SIDE, side, side_e, gq, (pair_sent, out_shape))
     side_back = lax.ppermute(side_part, "ctx", flip(to_side))
+    line_back = lax.ppermute(line_part, "ctx", flip(to_line))
     own_part, grad_query = later(
         "own_backward", last_kernel, OWN, own, own_e, gq, (pair, wide), [buffer(wide), pltpu.SemaphoreType.DMA((heads,))], (1,)
     )
-    total = (own_part + side_back.astype(f32) + line_back.astype(f32)).astype(bf16)
+    total = lax.optimization_barrier(own_part + line_back.astype(f32))
+    total = (total + side_back.astype(f32)).astype(bf16)
     return attended, grad_query, total[:, :dim], total[:, dim:]
 
 

time: 28.6 us -> 26.3 us (0.920)
  the two profiles are of different devices: /device:TPU:0 before, /device:TPU:1 now
where the time goes in v3:
time: 26.3 us; the launch traced here: 26.1 us
  Pallas kernels  11.9 us (45%)
  starting transfers between devices  7.88 us (30%)
  waiting for transfers between devices  4.74 us (18%)
  between operations  0.76 us (3%)
  local copies, waits for them, and re-layouts  0.68 us (3%)
    pallas_call x9, Pallas kernels, call(): pl.pallas_call(kernel, name=name, out_shape=outs, in_specs=[far if i in f...  11.9 us
    ppermute x1, waiting for transfers between devices, body(): line = lax.ppermute(own, 'ctx', to_line)  2.99 us
    ppermute x1, starting transfers between devices, body(): side = lax.ppermute(own, 'ctx', to_side)  2.14 us
    ppermute x1, starting transfers between devices, body(): line = lax.ppermute(own, 'ctx', to_line)  2.12 us
    ppermute x1, starting transfers between devices, body(): mate = lax.ppermute(line, 'ctx', to_mate)  2 us
    ppermute x1, waiting for transfers between devices, body(): side_back = lax.ppermute(side_part, 'ctx', flip(to_side))  1.72 us
    ppermute x1, starting transfers between devices, body(): line_back = lax.ppermute(line_part, 'ctx', flip(to_line))  0.91 us
    slice x1, local copies, waits for them, and re-layouts, body(): return (attended, grad_query, total[:, :dim], total[:, dim:])  0.66 us
  transfers between devices with their start and end apart: 6, of which 2 were waited for; matrix products, arithmetic and copies ran while one was open for 0% of the time, Pallas kernels for 31%

profile of v3, /device:TPU:1, one launch (start us, length us, event | category | flops | bytes accessed | tf_op | source)
XLA Modules:
  0.0 26.1 jit_solution(1423069954595242541)
XLA Ops:
  0.6 0.9 %pack.1.in_ref = bf16[256,256]{1,0:T(8,128)(2,1)S(1)} custom-call(bf16[256,128]{1,0:T(8,128)(2,1)} %k_ref.1, bf16[256,128]{1,0:T(8,128)(2,1)} %v_ref.1), custom_call_target="tpu_custom_call" | custom-call | tf_op jit(solution)/shard_map/pack/pallas_call | solution.py:165
  1.5 0.0 copy-start
  1.5 0.0 copy-start.2
  1.6 2.1 %collective-permute-start = (bf16[256,256]{1,0:T(8,128)(2,1)S(1)}, bf16[256,256]{1,0:T(8,128)(2,1)S(1)}, u32[]{:S(2)}, u32[]{:S(2)}) collective-permute-start(bf16[256,256]{1,0:T(8,128)(2,1)S(1)} %settle.1.refs_2_), channel_id=1, source_target_pairs={{0,4},{2,6},{4,8},{6,10},{8,12},{10,14},{12,16},{14,18},{16,20},{1... | collective-permute-start | bytes 393224 | tf_op jit(solution)/shard_map/ppermute | solution.py:202
  3.7 2.1 %collective-permute-start.2 = (bf16[256,256]{1,0:T(8,128)(2,1)S(1)}, bf16[256,256]{1,0:T(8,128)(2,1)S(1)}, u32[]{:S(2)}, u32[]{:S(2)}) collective-permute-start(bf16[256,256]{1,0:T(8,128)(2,1)S(1)} %settle.1.refs_2_), channel_id=1, source_target_pairs={{0,2},{2,8},{4,6},{6,12},{8,10},{10,16},{12,14},{14,20},{16,18},{1... | collective-permute-start | bytes 393224 | tf_op jit(solution)/shard_map/ppermute | solution.py:203
  5.8 0.0 copy-done
  5.8 0.0 copy-done.2
  5.8 1.1 %own_forward.1 = (bf16[8,256,256]{2,1,0:T(8,128)(2,1)S(1)}, f32[16,256]{1,0:T(8,128)S(1)}, f32[8,128,256]{2,1,0:T(8,128)S(1)}) custom-call(s32[32,128]{1,0:T(8,128)S(1)} %bitcast.1, bf16[256,1024]{1,0:T(8,128)(2,1)S(1)} %copy-done, bf16[256,256]{1,0:T(8,128)(2,1)S(1)} %settle.1.refs_2_), custom_call_target="tpu_custom_call" | custom-call | flops 4096 | tf_op jit(solution)/shard_map/own_forward/pallas_call | solution.py:165
  7.0 3.0 %collective-permute-done.refs_2_ = bf16[256,256]{1,0:T(8,128)(2,1)S(1)} collective-permute-done((bf16[256,256]{1,0:T(8,128)(2,1)S(1)}, bf16[256,256]{1,0:T(8,128)(2,1)S(1)}, u32[]{:S(2)}, u32[]{:S(2)}) %collective-permute-start) | collective-permute-done | bytes 131104 | tf_op jit(solution)/shard_map/ppermute | solution.py:202
  9.9 0.0 copy-start.1
  9.9 2.0 %collective-permute-start.1 = (bf16[256,256]{1,0:T(8,128)(2,1)S(1)}, bf16[256,256]{1,0:T(8,128)(2,1)S(1)}, u32[]{:S(2)}, u32[]{:S(2)}) collective-permute-start(bf16[256,256]{1,0:T(8,128)(2,1)S(1)} %collective-permute-done.refs_2_), channel_id=1, source_target_pairs={{0,2},{2,0},{4,6},{6,4},{8,10},{10,8},{12,14},{14,12},{16,18},{18,... | collective-permute-start | bytes 393224 | tf_op jit(solution)/shard_map/ppermute | solution.py:213
  11.9 1.1 %line_forward.1 = (bf16[8,256,256]{2,1,0:T(8,128)(2,1)S(1)}, f32[16,256]{1,0:T(8,128)S(1)}, f32[8,128,256]{2,1,0:T(8,128)S(1)}) custom-call(s32[32,128]{1,0:T(8,128)S(1)} %bitcast.2, bf16[256,1024]{1,0:T(8,128)(2,1)S(1)} %copy-done, bf16[256,256]{1,0:T(8,128)(2,1)S(1)} %collective-permute-done.refs_2_), custom_call_target="tpu_custom_call" | custom-call | flops 4096 | tf_op jit(solution)/shard_map/line_forward/pallas_call | solution.py:165
  13.1 0.0 collective-permute-done.2.refs_2_
  13.1 1.1 %side_forward.1 = (bf16[8,256,256]{2,1,0:T(8,128)(2,1)S(1)}, f32[16,256]{1,0:T(8,128)S(1)}, f32[8,128,256]{2,1,0:T(8,128)S(1)}) custom-call(s32[32,128]{1,0:T(8,128)S(1)} %bitcast.3, bf16[256,1024]{1,0:T(8,128)(2,1)S(1)} %copy-done, bf16[256,256]{1,0:T(8,128)(2,1)S(1)} %collective-permute-done.2.refs_2_), custom_call_target="tpu_custom_call" | custom-call | flops 4096 | tf_op jit(solution)/shard_map/side_forward/pallas_call | solution.py:165
  14.2 0.0 collective-permute-done.1.mate_ref
  14.3 0.0 copy-done.1
  14.3 3.0 %rest_forward.1 = (bf16[256,1024]{1,0:T(8,128)(2,1)}, bf16[256,256]{1,0:T(8,128)(2,1)S(1)}, f32[8,128,256]{2,1,0:T(8,128)S(1)}, f32[4,8,256]{2,1,0:T(8,128)S(1)}, f32[8,256]{1,0:T(8,128)S(1)}) custom-call(s32[32,128]{1,0:T(8,128)S(1)} %bitcast.4, bf16[256,1024]{1,0:T(8,128)(2,1)S(1)} %copy-done, bf16[256,1024]{1,0:T(8,128)(2,1)S(1)} %copy-done.1, ...), custom_call_target="tpu_custom_call" | custom-call | flops 12288 | tf_op jit(solution)/shard_map/rest_forward/pallas_call | solution.py:165
  17.3 0.1 collective-permute-start.3
  17.4 1.3 %line_backward.1 = (f32[256,256]{1,0:T(8,128)S(1)}, f32[8,128,256]{2,1,0:T(8,128)S(1)}) custom-call(bf16[256,1024]{1,0:T(8,128)(2,1)S(1)} %copy-done, bf16[256,1024]{1,0:T(8,128)(2,1)S(1)} %copy-done.1, bf16[256,256]{1,0:T(8,128)(2,1)S(1)} %collective-permute-done.refs_2_, bf16[8,256,256]{2,1,0:T(8,128)(2,1)S(1)} %get-tuple-element.41.refs_3_, ...), custom_call_target="tpu_custom_call" | custom-call | flops 8192 | tf_op jit(solution)/shard_map/line_backward/pallas_call | solution.py:165
  18.7 0.0 collective-permute-done.3
  18.8 0.9 %collective-permute-start.4 = (bf16[256,256]{1,0:T(8,128)(2,1)S(1)}, bf16[256,256]{1,0:T(8,128)(2,1)S(1)}, u32[]{:S(2)}, u32[]{:S(2)}) collective-permute-start(bf16[256,256]{1,0:T(8,128)(2,1)S(1)} %add_convert_fusion.1), channel_id=1, source_target_pairs={{4,0},{6,2},{8,4},{10,6},{12,8},{14,10},{16,12},{18,14},{20,16},{2... | collective-permute-start | bytes 393224 | tf_op jit(solution)/shard_map/ppermute | solution.py:237
  19.7 1.3 %side_backward.1 = (bf16[256,256]{1,0:T(8,128)(2,1)S(1)}, f32[8,128,256]{2,1,0:T(8,128)S(1)}) custom-call(bf16[256,1024]{1,0:T(8,128)(2,1)S(1)} %copy-done, bf16[256,1024]{1,0:T(8,128)(2,1)S(1)} %copy-done.1, bf16[256,256]{1,0:T(8,128)(2,1)S(1)} %collective-permute-done.2.refs_2_, bf16[8,256,256]{2,1,0:T(8,128)(2,1)S(1)} %get-tuple-element.40.refs_3_, ...), custom_call_target="tpu_custom_call" | custom-call | flops 8192 | tf_op jit(solution)/shard_map/side_backward/pallas_call | solution.py:165
  21.0 0.6 %collective-permute-start.5 = (bf16[256,256]{1,0:T(8,128)(2,1)S(1)}, bf16[256,256]{1,0:T(8,128)(2,1)S(1)}, u32[]{:S(2)}, u32[]{:S(2)}) collective-permute-start(bf16[256,256]{1,0:T(8,128)(2,1)S(1)} %get-tuple-element.51), channel_id=1, source_target_pairs={{2,0},{8,2},{6,4},{12,6},{10,8},{16,10},{14,12},{20,14},{18,16},{2... | collective-permute-start | bytes 393224 | tf_op jit(solution)/shard_map/ppermute | solution.py:236
  21.6 2.0 %own_backward.1 = (f32[256,256]{1,0:T(8,128)S(1)}, bf16[256,1024]{1,0:T(8,128)(2,1)}) custom-call(bf16[256,1024]{1,0:T(8,128)(2,1)S(1)} %copy-done, bf16[256,1024]{1,0:T(8,128)(2,1)S(1)} %copy-done.1, bf16[256,256]{1,0:T(8,128)(2,1)S(1)} %settle.1.refs_2_, bf16[8,256,256]{2,1,0:T(8,128)(2,1)S(1)} %get-tuple-element.37.refs_3_, ...), custom_call_target="tpu_custom_call" | custom-call | flops 8192 | tf_op jit(solution)/shard_map/own_backward/pallas_call | solution.py:165
  23.7 0.0 collective-permute-done.4
  23.7 1.7 %collective-permute-done.5 = bf16[256,256]{1,0:T(8,128)(2,1)S(1)} collective-permute-done((bf16[256,256]{1,0:T(8,128)(2,1)S(1)}, bf16[256,256]{1,0:T(8,128)(2,1)S(1)}, u32[]{:S(2)}, u32[]{:S(2)}) %collective-permute-start.5) | collective-permute-done | bytes 131104 | tf_op jit(solution)/shard_map/ppermute | solution.py:236
  25.5 0.7 %fusion = (bf16[256,128]{1,0:T(8,128)(2,1)}, bf16[256,128]{1,0:T(8,128)(2,1)}) fusion(bf16[256,256]{1,0:T(8,128)(2,1)S(1)} %add_convert_fusion), kind=kLoop, calls=%fused_computation.3 | loop fusion | bytes 262144 | tf_op jit(solution)/shard_map/slice | solution.py:243
  (4 shorter events, 0.1 us)
Async XLA Ops:
  1.5 4.3 %copy-start = (bf16[256,1024]{1,0:T(8,128)(2,1)S(1)}, bf16[256,1024]{1,0:T(8,128)(2,1)}, u32[]{:S(2)}) copy-start(bf16[256,1024]{1,0:T(8,128)(2,1)} %refs_0_.5) | copy-start | bytes 1572868
  1.5 4.3 %copy-start.2 = (s32[4096]{0:T(1024)S(1)}, s32[4096]{0:T(1024)}, u32[]{:S(2)}) copy-start(s32[4096]{0:T(1024)} %param.8) | copy-start | bytes 49156
  1.6 8.4 %collective-permute-start = (bf16[256,256]{1,0:T(8,128)(2,1)S(1)}, bf16[256,256]{1,0:T(8,128)(2,1)S(1)}, u32[]{:S(2)}, u32[]{:S(2)}) collective-permute-start(bf16[256,256]{1,0:T(8,128)(2,1)S(1)} %settle.1.refs_2_), channel_id=1, source_target_pairs={{0,4},{2,6},{4,8},{6,10},{8,12},{10,14},{12,16},{14,18},{16,20},{1... | collective-permute-start | bytes 393224 | tf_op jit(solution)/shard_map/ppermute | solution.py:202
  3.7 9.4 %collective-permute-start.2 = (bf16[256,256]{1,0:T(8,128)(2,1)S(1)}, bf16[256,256]{1,0:T(8,128)(2,1)S(1)}, u32[]{:S(2)}, u32[]{:S(2)}) collective-permute-start(bf16[256,256]{1,0:T(8,128)(2,1)S(1)} %settle.1.refs_2_), channel_id=1, source_target_pairs={{0,2},{2,8},{4,6},{6,12},{8,10},{10,16},{12,14},{14,20},{16,18},{1... | collective-permute-start | bytes 393224 | tf_op jit(solution)/shard_map/ppermute | solution.py:203
  9.9 4.3 %copy-start.1 = (bf16[256,1024]{1,0:T(8,128)(2,1)S(1)}, bf16[256,1024]{1,0:T(8,128)(2,1)}, u32[]{:S(2)}) copy-start(bf16[256,1024]{1,0:T(8,128)(2,1)} %refs_1_.11) | copy-start | bytes 1572868
  9.9 4.3 %collective-permute-start.1 = (bf16[256,256]{1,0:T(8,128)(2,1)S(1)}, bf16[256,256]{1,0:T(8,128)(2,1)S(1)}, u32[]{:S(2)}, u32[]{:S(2)}) collective-permute-start(bf16[256,256]{1,0:T(8,128)(2,1)S(1)} %collective-permute-done.refs_2_), channel_id=1, source_target_pairs={{0,2},{2,0},{4,6},{6,4},{8,10},{10,8},{12,14},{14,12},{16,18},{18,... | collective-permute-start | bytes 393224 | tf_op jit(solution)/shard_map/ppermute | solution.py:213
  17.3 1.4 %collective-permute-start.3 = (bf16[256,256]{1,0:T(8,128)(2,1)S(1)}, bf16[256,256]{1,0:T(8,128)(2,1)S(1)}, u32[]{:S(2)}, u32[]{:S(2)}) collective-permute-start(bf16[256,256]{1,0:T(8,128)(2,1)S(1)} %get-tuple-element.44), channel_id=1, source_target_pairs={{0,2},{2,0},{4,6},{6,4},{8,10},{10,8},{12,14},{14,12},{16,18},{18,... | collective-permute-start | bytes 393224 | tf_op jit(solution)/shard_map/ppermute | solution.py:224
  18.8 4.9 %collective-permute-start.4 = (bf16[256,256]{1,0:T(8,128)(2,1)S(1)}, bf16[256,256]{1,0:T(8,128)(2,1)S(1)}, u32[]{:S(2)}, u32[]{:S(2)}) collective-permute-start(bf16[256,256]{1,0:T(8,128)(2,1)S(1)} %add_convert_fusion.1), channel_id=1, source_target_pairs={{4,0},{6,2},{8,4},{10,6},{12,8},{14,10},{16,12},{18,14},{20,16},{2... | collective-permute-start | bytes 393224 | tf_op jit(solution)/shard_map/ppermute | solution.py:237
  21.0 4.4 %collective-permute-start.5 = (bf16[256,256]{1,0:T(8,128)(2,1)S(1)}, bf16[256,256]{1,0:T(8,128)(2,1)S(1)}, u32[]{:S(2)}, u32[]{:S(2)}) collective-permute-start(bf16[256,256]{1,0:T(8,128)(2,1)S(1)} %get-tuple-element.51), channel_id=1, source_target_pairs={{2,0},{8,2},{6,4},{12,6},{10,8},{16,10},{14,12},{20,14},{18,16},{2... | collective-permute-start | bytes 393224 | tf_op jit(solution)/shard_map/ppermute | solution.py:236

commit v4 on v3

v4 whole, which is shorter than its diff:
```python
import jax
import jax.numpy as jnp
from jax import lax
from jax.experimental import pallas as pl
from jax.experimental.pallas import tpu as pltpu
from jax.sharding import PartitionSpec as P

LANES = 128
LOG2_E = 1.4426950408889634
MASKED = -1e30

OWN, MATE, LINE, SIDE = range(4)


def nt(a, b):
    return lax.dot_general(a, b, (((1,), (1,)), ((), ())), preferred_element_type=jnp.float32)


def nn(a, b):
    return lax.dot_general(a, b, (((1,), (0,)), ((), ())), preferred_element_type=jnp.float32)


def place(role, rows):
    here, count = lax.axis_index("ctx"), lax.axis_size("ctx")
    odd = lax.rem(here, 2)
    block = here - (0, 1 + 2 * odd, 2, 3 - 2 * odd)[role]
    steps = rows // LANES
    return here * steps, lax.rem(block + count, count) * steps, block >= 0


def is_seen(role, doc_ref, rows):
    mine, at, valid = place(role, rows)
    first = jnp.min(doc_ref[pl.ds(mine, 1), :].astype(jnp.float32))
    last = jnp.max(doc_ref[pl.ds(at + rows // LANES - 1, 1), :].astype(jnp.float32))
    return valid & (first == last)


def mask_bias(role, doc_ref, bias):
    rows = bias.shape[0]
    steps = rows // LANES
    mine, at, valid = place(role, rows)
    own_doc = jnp.concatenate([doc_ref[pl.ds(mine + i, 1), :] for i in range(steps)], axis=1)
    for i in range(steps):
        row = jnp.where(valid, doc_ref[pl.ds(at + i, 1), :], -1)
        column = jnp.transpose(jnp.broadcast_to(row, (LANES, LANES)).astype(jnp.float32)).astype(jnp.int32)
        same = jnp.concatenate([column] * steps, axis=1) == own_doc
        if role == OWN:
            key_at = lax.broadcasted_iota(jnp.int32, (LANES, rows), 0) + i * LANES
            same = same & (key_at <= lax.broadcasted_iota(jnp.int32, (LANES, rows), 1))
        bias[i * LANES : (i + 1) * LANES, :] = jnp.where(same, 0.0, MASKED)


def forward(q_ref, kv_ref, bias, e_ref, stat_ref, out_ref, s_ref, vt_ref):
    dim = kv_ref.shape[1] // 2
    heads = q_ref.shape[1] // dim
    factor = dim**-0.5 * LOG2_E
    vt_ref[...] = jnp.transpose(kv_ref[:, dim:])
    for h in range(heads):
        s = nt(kv_ref[:, :dim], q_ref[:, h * dim : (h + 1) * dim]) + bias[...]
        s_ref[h] = s
        stat_ref[h : h + 1, :] = jnp.max(s, axis=0, keepdims=True)
    for h in range(heads):
        e = jnp.exp2((s_ref[h] - stat_ref[h : h + 1, :]) * factor)
        e_ref[h] = e.astype(jnp.bfloat16)
        stat_ref[heads + h : heads + h + 1, :] = jnp.sum(e, axis=0, keepdims=True)
    for h in range(heads):
        out_ref[h] = nn(vt_ref[...], e_ref[h])


def forward_unseen(stat_ref, out_ref):
    heads = out_ref.shape[0]
    stat_ref[:heads, :] = jnp.full((heads, stat_ref.shape[1]), MASKED, jnp.float32)
    stat_ref[heads:, :] = jnp.zeros((heads, stat_ref.shape[1]), jnp.float32)
    out_ref[...] = jnp.zeros(out_ref.shape, out_ref.dtype)


def backward_queries(g_ref, kv_ref, e_ref, scale_ref, delta_ref, gq_out, kt_ref, p_ref, ds_ref, dp=None):
    dim = kv_ref.shape[1] // 2
    heads = g_ref.shape[1] // dim
    kt_ref[...] = jnp.transpose(kv_ref[:, :dim])
    for h in range(heads):
        probs = e_ref[h].astype(jnp.float32) * scale_ref[h : h + 1, :]
        p_ref[h] = probs.astype(jnp.bfloat16)
        grad_p = nt(kv_ref[:, dim:], g_ref[:, h * dim : (h + 1) * dim]) if dp is None else dp[h]
        ds_ref[h] = (probs * (grad_p - delta_ref[h : h + 1, :])).astype(jnp.bfloat16)
    for h in range(heads):
        gq_out(h, nn(kt_ref[...], ds_ref[h]))


def backward_keys(q_ref, g_ref, p_ref, ds_ref, part_ref):
    dim = part_ref.shape[1] // 2
    cols = [slice(h * dim, (h + 1) * dim) for h in range(q_ref.shape[1] // dim)]
    grad_v = sum(nn(p_ref[h], g_ref[:, c]) for h, c in enumerate(cols))
    part_ref[:, dim:] = grad_v.astype(part_ref.dtype)
    grad_k = sum(nn(ds_ref[h], q_ref[:, c]) for h, c in enumerate(cols))
    part_ref[:, :dim] = (grad_k * dim**-0.5).astype(part_ref.dtype)


def backward_unseen(part_ref, gq_in, gq_ref):
    part_ref[...] = jnp.zeros(part_ref.shape, part_ref.dtype)
    gq_ref[...] = jnp.zeros(gq_ref.shape, gq_ref.dtype) if gq_in is None else gq_in[...]


def pack_kernel(k_ref, v_ref, kv_ref, sems):
    dim = k_ref.shape[1]
    copies = [
        pltpu.make_async_copy(ref, kv_ref.at[:, i * dim : (i + 1) * dim], sems.at[i]) for i, ref in enumerate((k_ref, v_ref))
    ]
    for copy in copies:
        copy.start()
    for copy in copies:
        copy.wait()


def settle_kernel(in_ref, out_ref):
    out_ref[:16, :] = in_ref[:16, :]


def own_kernel(doc_ref, q_ref, g_ref, kv_ref, e_ref, stat_ref, out_ref, bias_ref, gt_ref, dp_ref, bias, s_ref, vt_ref):
    dim = kv_ref.shape[1] // 2
    heads = q_ref.shape[1] // dim
    mask_bias(OWN, doc_ref, bias)
    forward(q_ref, kv_ref, bias, e_ref, stat_ref, out_ref, s_ref, vt_ref)
    for role in (MATE, LINE, SIDE):
        mask_bias(role, doc_ref, bias_ref.at[role - 1])
    for h in range(heads):
        g = g_ref[:, h * dim : (h + 1) * dim]
        gt_ref[h] = jnp.transpose(g)
        dp_ref[h] = nt(kv_ref[:, dim:], g)


def next_kernel(role, doc_ref, q_ref, kv_ref, bias_ref, e_ref, stat_ref, out_ref, s_ref, vt_ref):
    seen = is_seen(role, doc_ref, kv_ref.shape[0])

    @pl.when(seen)
    def _():
        forward(q_ref, kv_ref, bias_ref.at[role - 1], e_ref, stat_ref, out_ref, s_ref, vt_ref)

    @pl.when(jnp.logical_not(seen))
    def _():
        forward_unseen(stat_ref, out_ref)


def next_backward(seen, q_ref, g_ref, kv_ref, e_ref, scale_ref, delta_ref, gq_in, part_ref, gq_ref, kt_ref, p_ref, ds_ref):
    @pl.when(seen)
    def _():
        def put(h, value):
            gq_ref[h] = value if gq_in is None else gq_in[h] + value

        backward_queries(g_ref, kv_ref, e_ref, scale_ref, delta_ref, put, kt_ref, p_ref, ds_ref)
        backward_keys(q_ref, g_ref, p_ref, ds_ref, part_ref)

    @pl.when(jnp.logical_not(seen))
    def _():
        backward_unseen(part_ref, gq_in, gq_ref)


def rest_kernel(
    doc_ref, q_ref, g_ref, mate_ref, bias_ref, gt_ref, own_stat, own_o, line_stat, line_o, side_stat, side_o,
    att_t, mate_part, gq_part, scale_ref, delta_ref,
    s_ref, vt_ref, mate_e, mate_stat, mate_o, kt_ref, p_ref, ds_ref,
):
    dim = mate_ref.shape[1] // 2
    heads = q_ref.shape[1] // dim
    factor = dim**-0.5 * LOG2_E
    next_kernel(MATE, doc_ref, q_ref, mate_ref, bias_ref, mate_e, mate_stat, mate_o, s_ref, vt_ref)
    stats = (own_stat, mate_stat, line_stat, side_stat)
    tops = [ref[:heads, :] for ref in stats]
    top = jnp.maximum(jnp.maximum(tops[0], tops[1]), jnp.maximum(tops[2], tops[3]))
    parts = [jnp.exp2((t - top) * factor) for t in tops]
    inverse = 1.0 / sum(p * ref[heads:, :] for p, ref in zip(parts, stats))
    for b in range(4):
        scale_ref[b] = parts[b] * inverse
    for h in range(heads):
        out = sum(ref[h] * scale_ref[b, h : h + 1, :] for b, ref in enumerate((own_o, mate_o, line_o, side_o)))
        att_t[h] = out.astype(jnp.bfloat16)
        delta_ref[h : h + 1, :] = jnp.sum(out * gt_ref[h].astype(jnp.float32), axis=0, keepdims=True)
    next_backward(
        is_seen(MATE, doc_ref, mate_ref.shape[0]), q_ref, g_ref, mate_ref, mate_e, scale_ref.at[MATE], delta_ref, None,
        mate_part, gq_part, kt_ref, p_ref, ds_ref,
    )


def line_kernel(
    doc_ref, q_ref, g_ref, kv_ref, e_ref, side_ref, side_e, scale_ref, delta_ref, gq_in,
    part_ref, side_part, gq_ref, kt_ref, p_ref, ds_ref,
):
    rows = kv_ref.shape[0]
    first_chip = lax.axis_index("ctx") < 2
    common = (q_ref, g_ref)

    @pl.when(jnp.logical_not(first_chip))
    def _():
        next_backward(
            is_seen(LINE, doc_ref, rows), *common, kv_ref, e_ref, scale_ref.at[LINE], delta_ref, gq_in,
            part_ref, gq_ref, kt_ref, p_ref, ds_ref,
        )

    @pl.when(first_chip)
    def _():
        part_ref[...] = jnp.zeros(part_ref.shape, part_ref.dtype)
        next_backward(
            is_seen(SIDE, doc_ref, rows), *common, side_ref, side_e, scale_ref.at[SIDE], delta_ref, gq_in,
            side_part, gq_ref, kt_ref, p_ref, ds_ref,
        )


def turn(h, value, buf):
    buf[:, h * value.shape[0] : (h + 1) * value.shape[0]] = jnp.transpose(value.astype(jnp.bfloat16))


def side_kernel(
    doc_ref, q_ref, g_ref, kv_ref, e_ref, scale_ref, delta_ref, gq_in, early_part, part_ref, gq_ref, kt_ref, p_ref, ds_ref
):
    first_chip = lax.axis_index("ctx") < 2

    @pl.when(jnp.logical_not(first_chip))
    def _():
        next_backward(
            is_seen(SIDE, doc_ref, kv_ref.shape[0]), q_ref, g_ref, kv_ref, e_ref, scale_ref.at[SIDE], delta_ref, gq_in,
            part_ref, gq_ref, kt_ref, p_ref, ds_ref,
        )

    @pl.when(first_chip)
    def _():
        part_ref[...] = early_part[...]
        gq_ref[...] = gq_in[...]


def last_kernel(
    q_ref, g_ref, kv_ref, e_ref, scale_ref, delta_ref, gq_in, dp_ref, att_t, part_ref, gq_ref, att_ref,
    kt_ref, p_ref, ds_ref, buf, att_buf, sems,
):
    factor = (kv_ref.shape[1] // 2) ** -0.5
    for h in range(att_t.shape[0]):
        turn(h, att_t[h], att_buf)
    att_copy = pltpu.make_async_copy(att_buf, att_ref, sems.at[0])
    gq_copy = pltpu.make_async_copy(buf, gq_ref, sems.at[1])
    att_copy.start()

    @pl.when(lax.axis_index("ctx") >= 0)
    def _():
        backward_queries(
            g_ref, kv_ref, e_ref, scale_ref.at[OWN], delta_ref, lambda h, v: turn(h, (gq_in[h] + v) * factor, buf),
            kt_ref, p_ref, ds_ref, dp_ref,
        )

    gq_copy.start()

    @pl.when(lax.axis_index("ctx") >= 0)
    def _():
        backward_keys(q_ref, g_ref, p_ref, ds_ref, part_ref)

    att_copy.wait()
    gq_copy.wait()


def line_add_kernel(line_ref, mate_ref, out_ref):
    out_ref[...] = (line_ref[...] + mate_ref[...].astype(jnp.float32)).astype(jnp.bfloat16)


def line_sum_kernel(own_ref, line_ref, out_ref):
    out_ref[...] = own_ref[...] + line_ref[...].astype(jnp.float32)


def side_sum_kernel(sum_ref, near_ref, far_ref, k_ref, v_ref):
    here, count = lax.axis_index("ctx"), lax.axis_size("ctx")
    dim = k_ref.shape[1]
    even = lax.rem(here, 2) == 0
    side = jnp.where(even, near_ref[...].astype(jnp.float32), far_ref[...].astype(jnp.float32))
    total = sum_ref[...] + jnp.where(even | (here + 3 < count), side, 0.0)
    k_ref[...] = total[:, :dim].astype(jnp.bfloat16)
    v_ref[...] = total[:, dim:].astype(jnp.bfloat16)


def call(name, kernel, args, outs, scratch, flops, far_in=(), far_out=(), aliases=None):
    near, far = pl.BlockSpec(memory_space=pltpu.VMEM), pl.BlockSpec(memory_space=pltpu.HBM)
    args = [pltpu.with_memory_space_constraint(a, pltpu.HBM) if i in far_in else a for i, a in enumerate(args)]
    return pl.pallas_call(
        kernel,
        name=name,
        out_shape=outs,
        in_specs=[far if i in far_in else near for i in range(len(args))],
        out_specs=[far if i in far_out else near for i in range(len(outs))],
        scratch_shapes=scratch,
        input_output_aliases=aliases or {},
        cost_estimate=pl.CostEstimate(flops=flops, bytes_accessed=0, transcendentals=0),
        compiler_params=pltpu.CompilerParams(vmem_limit_bytes=16 << 20),
    )(*args)


def three_back(count):
    to = {i: i - 3 for i in range(4, count, 2)}
    to.update({i: i + 3 for i in range(3, count - 3, 2)})
    to.update({0: 2, 1: 0, 2: 4, count - 3: count - 1, count - 1: count - 3})
    return list(to.items())


def body(queries, key_vectors, value_vectors, doc_ids, grad_out):
    rows, dim = key_vectors.shape
    heads = queries.shape[1] // dim
    count = lax.axis_size("ctx")
    to_mate = [(i, i ^ 1) for i in range(count)]
    to_line = [(i, (i + 2) % count) for i in range(count)]
    to_side = [(i, (i + 1 + 2 * (i % 2)) % count) for i in range(count)]
    flip = lambda pairs: [(b, a) for a, b in pairs]
    f32, bf16 = jnp.float32, jnp.bfloat16
    shape = jax.ShapeDtypeStruct
    e_shape, stat_shape, out_shape = shape((heads, rows, rows), bf16), shape((2 * heads, rows), f32), shape((heads, dim, rows), f32)
    pair, pair_sent = shape((rows, 2 * dim), f32), shape((rows, 2 * dim), bf16)
    wide = shape(queries.shape, bf16)
    buffer = lambda like: pltpu.VMEM(like.shape, like.dtype)
    flat = pltpu.VMEM((dim, rows), bf16)
    ahead = [pltpu.VMEM((heads, rows, rows), f32), flat]
    back = [flat, buffer(e_shape), buffer(e_shape)]
    work = heads * rows

    docs = doc_ids.reshape(-1, LANES)
    own = call(
        "pack", pack_kernel, (key_vectors, value_vectors), (pair_sent,), [pltpu.SemaphoreType.DMA((2,))], 0, (0, 1)
    )[0]
    own = call("settle", settle_kernel, (own,), (pair_sent,), [], 1 << 33, (), (), {0: 0})[0]
    line = lax.ppermute(own, "ctx", to_line)
    q, g = queries, grad_out
    own_e, own_stat, own_o, bias, gt, dp = call(
        "own_forward", own_kernel, (docs, q, g, own),
        (e_shape, stat_shape, out_shape, shape((3, rows, rows), f32), shape((heads, dim, rows), bf16), shape((heads, rows, rows), f32)),
        [pltpu.VMEM((rows, rows), f32), *ahead], work,
    )
    line, own_stat = lax.optimization_barrier((line, own_stat))
    side = lax.ppermute(own, "ctx", to_side)
    mate = lax.ppermute(line, "ctx", to_mate)

    def first(name, role, kv):
        return call(
            name, lambda *refs: next_kernel(role, *refs), (docs, q, kv, bias), (e_shape, stat_shape, out_shape), ahead, work
        )

    line_e, line_stat, line_o = first("line_forward", LINE, line)
    side_e, side_stat, side_o = first("side_forward", SIDE, side)
    attended_t, mate_part, gq, scales, delta = call(
        "rest_forward", rest_kernel,
        (docs, q, g, mate, bias, gt, own_stat, own_o, line_stat, line_o, side_stat, side_o),
        (shape((heads, dim, rows), bf16), pair_sent, out_shape, shape((4, heads, rows), f32), shape((heads, rows), f32)),
        [*ahead, buffer(e_shape), buffer(stat_shape), buffer(out_shape), *back],
        work,
    )
    mate_back = lax.ppermute(mate_part, "ctx", to_mate)
    line_part, early_part, gq = call(
        "line_backward", line_kernel, (docs, q, g, line, line_e, side, side_e, scales, delta, gq), (pair, pair_sent, out_shape),
        back, work,
    )
    line_part = call("line_add", line_add_kernel, (line_part, mate_back), (pair_sent,), [], 0)[0]
    line_part, gq = lax.optimization_barrier((line_part, gq))
    side_part, gq = call(
        "side_backward", side_kernel, (docs, q, g, side, side_e, scales, delta, gq, early_part), (pair_sent, out_shape), back, work
    )
    side_far = lax.ppermute(side_part, "ctx", three_back(count))
    side_near = lax.ppermute(side_part, "ctx", to_mate)
    line_back = lax.ppermute(line_part, "ctx", flip(to_line))
    own_part, grad_query, attended = call(
        "own_backward", last_kernel, (q, g, own, own_e, scales, delta, gq, dp, attended_t), (pair, wide, wide),
        [*back, buffer(wide), buffer(wide), pltpu.SemaphoreType.DMA((2,))], work, (), (1, 2),
    )
    total = call("line_sum", line_sum_kernel, (own_part, line_back), (pair,), [], work)[0]
    narrow = shape((rows, dim), bf16)
    grad_key, grad_value = call("side_sum", side_sum_kernel, (total, side_near, side_far), (narrow, narrow), [], 0)
    return attended, grad_query, grad_key, grad_value


def solution(mesh):
    return jax.shard_map(
        body,
        mesh=mesh,
        in_specs=(P("ctx", "head"), P("ctx", "head"), P("ctx", "head"), P(), P("ctx", "head")),
        out_specs=(P("ctx", "head"), P("ctx", "head"), P("ctx", "head"), P("ctx", "head")),
        check_vma=False,
    )
```

time: 26.3 us -> 24.8 us (0.943)
  Pallas kernels: 11.9 us -> 8.63 us
  starting transfers between devices: 7.88 us -> 9.64 us
  local copies, waits for them, and re-layouts: 0.68 us -> 0.02 us
  waiting for transfers between devices: 4.74 us -> 5.34 us
    pallas_call x9 -> x12, Pallas kernels: 11.9 us -> 8.63 us  [call(): pl.pallas_call(kernel, name=name, out_shape=outs, in_specs=[far if i in f...]
    ppermute x1, starting transfers between devices: 0.91 us -> 2.51 us  [body(): line_back = lax.ppermute(line_part, 'ctx', flip(to_line))]
    ppermute x1 -> x2, waiting for transfers between devices: 1.72 us -> 2.65 us  [the longest x1 2.65 us: body(): side_far = lax.ppermute(side_part, 'ctx', three_back(count))]
    slice x1 -> x0, local copies, waits for them, and re-layouts: 0.66 us -> none  [body(): return (attended, grad_query, total[:, :dim], total[:, dim:])]
    ppermute x1, waiting for transfers between devices: 2.99 us -> 2.68 us  [body(): line = lax.ppermute(own, 'ctx', to_line)]
    ppermute x1 -> x2, starting transfers between devices: 0.65 us -> 0.8 us  [the longest x1 0.73 us: body(): side_far = lax.ppermute(side_part, 'ctx', three_back(count))]
  transfers between devices with their start and end apart: 6 -> 7, of which waited for: 2 -> 2; matrix products, arithmetic and copies ran while one was open for 0% -> 0% of each run, Pallas kernels for 31% -> 26%
where the time goes in v4:
time: 24.8 us; the launch traced here: 24.4 us
  starting transfers between devices  9.64 us (39%)
  Pallas kernels  8.63 us (35%)
  waiting for transfers between devices  5.34 us (22%)
  between operations  0.78 us (3%)
    pallas_call x12, Pallas kernels, call(): pl.pallas_call(kernel, name=name, out_shape=outs, in_specs=[far if i in f...  8.63 us
    ppermute x1, waiting for transfers between devices, body(): line = lax.ppermute(own, 'ctx', to_line)  2.68 us
    ppermute x1, waiting for transfers between devices, body(): side_far = lax.ppermute(side_part, 'ctx', three_back(count))  2.65 us
    ppermute x1, starting transfers between devices, body(): line_back = lax.ppermute(line_part, 'ctx', flip(to_line))  2.51 us
    ppermute x1, starting transfers between devices, body(): side = lax.ppermute(own, 'ctx', to_side)  2.14 us
    ppermute x1, starting transfers between devices, body(): line = lax.ppermute(own, 'ctx', to_line)  2.12 us
    ppermute x1, starting transfers between devices, body(): mate = lax.ppermute(line, 'ctx', to_mate)  2 us
    ppermute x1, starting transfers between devices, body(): side_far = lax.ppermute(side_part, 'ctx', three_back(count))  0.73 us
  transfers between devices with their start and end apart: 7, of which 2 were waited for; matrix products, arithmetic and copies ran while one was open for 0% of the time, Pallas kernels for 26%

profile of v4, /device:TPU:1, one launch (start us, length us, event | category | flops | bytes accessed | tf_op | source)
XLA Modules:
  0.0 24.4 jit_solution(2697247943809035838)
XLA Ops:
  0.6 0.9 %pack.1.in_ref = bf16[256,256]{1,0:T(8,128)(2,1)S(1)} custom-call(bf16[256,128]{1,0:T(8,128)(2,1)} %k_ref.1, bf16[256,128]{1,0:T(8,128)(2,1)} %v_ref.1), custom_call_target="tpu_custom_call" | custom-call | tf_op jit(solution)/shard_map/pack/pallas_call | solution.py:279
  1.5 0.0 copy-start
  1.5 0.0 copy-start.1
  1.6 0.0 copy-start.2
  1.6 2.1 %collective-permute-start = (bf16[256,256]{1,0:T(8,128)(2,1)S(1)}, bf16[256,256]{1,0:T(8,128)(2,1)S(1)}, u32[]{:S(2)}, u32[]{:S(2)}) collective-permute-start(bf16[256,256]{1,0:T(8,128)(2,1)S(1)} %settle.1.kv_ref), channel_id=1, source_target_pairs={{0,4},{2,6},{4,8},{6,10},{8,12},{10,14},{12,16},{14,18},{16,20},{1... | collective-permute-start | bytes 393224 | tf_op jit(solution)/shard_map/ppermute | solution.py:323
  3.7 2.1 %collective-permute-start.2 = (bf16[256,256]{1,0:T(8,128)(2,1)S(1)}, bf16[256,256]{1,0:T(8,128)(2,1)S(1)}, u32[]{:S(2)}, u32[]{:S(2)}) collective-permute-start(bf16[256,256]{1,0:T(8,128)(2,1)S(1)} %settle.1.kv_ref), channel_id=1, source_target_pairs={{0,2},{2,8},{4,6},{6,12},{8,10},{10,16},{12,14},{14,20},{16,18},{1... | collective-permute-start | bytes 393224 | tf_op jit(solution)/shard_map/ppermute | solution.py:331
  5.8 0.0 copy-done
  5.8 0.0 copy-done.1
  5.8 0.0 copy-done.2
  5.8 1.4 %own_forward.1 = (bf16[8,256,256]{2,1,0:T(8,128)(2,1)S(1)}, f32[16,256]{1,0:T(8,128)S(1)}, f32[8,128,256]{2,1,0:T(8,128)S(1)}, f32[3,256,256]{2,1,0:T(8,128)S(1)...) custom-call(s32[32,128]{1,0:T(8,128)S(1)} %bitcast.1, bf16[256,1024]{1,0:T(8,128)(2,1)S(1)} %copy-done, ...), custom_call_target="tpu_custom_call" | custom-call | flops 2048 | tf_op jit(solution)/shard_map/own_forward/pallas_call | solution.py:279
  7.3 2.7 %collective-permute-done.refs_2_.kv_ref = bf16[256,256]{1,0:T(8,128)(2,1)S(1)} collective-permute-done((bf16[256,256]{1,0:T(8,128)(2,1)S(1)}, bf16[256,256]{1,0:T(8,128)(2,1)S(1)}, u32[]{:S(2)}, u32[]{:S(2)}) %collective-permute-start) | collective-permute-done | bytes 131104 | tf_op jit(solution)/shard_map/ppermute | solution.py:323
  10.0 2.0 %collective-permute-start.1 = (bf16[256,256]{1,0:T(8,128)(2,1)S(1)}, bf16[256,256]{1,0:T(8,128)(2,1)S(1)}, u32[]{:S(2)}, u32[]{:S(2)}) collective-permute-start(bf16[256,256]{1,0:T(8,128)(2,1)S(1)} %collective-permute-done.refs_2_.kv_ref), channel_id=1, source_target_pairs={{0,2},{2,0},{4,6},{6,4},{8,10},{10,8},{12,14},{14,12},{16,18},{18,... | collective-permute-start | bytes 393224 | tf_op jit(solution)/shard_map/ppermute | solution.py:332
  12.0 0.2 line_forward.1
  12.2 0.0 collective-permute-done.2.refs_2_.side_ref.kv_ref
  12.2 1.3 %side_forward.1 = (bf16[8,256,256]{2,1,0:T(8,128)(2,1)S(1)}, f32[16,256]{1,0:T(8,128)S(1)}, f32[8,128,256]{2,1,0:T(8,128)S(1)}) custom-call(s32[32,128]{1,0:T(8,128)S(1)} %bitcast.3, bf16[256,1024]{1,0:T(8,128)(2,1)S(1)} %copy-done, bf16[256,256]{1,0:T(8,128)(2,1)S(1)} %collective-permute-done.2.refs_2_.side_ref.kv_ref, ...), custom_call_target="tpu_custom_call" | custom-call | flops 2048 | tf_op jit(solution)/shard_map/side_forward/pallas_call | solution.py:279
  13.5 0.0 collective-permute-done.1.mate_ref
  13.5 0.8 %rest_forward.1 = (bf16[8,128,256]{2,1,0:T(8,128)(2,1)S(1)}, bf16[256,256]{1,0:T(8,128)(2,1)S(1)}, f32[8,128,256]{2,1,0:T(8,128)S(1)}, f32[4,8,256]{2,1,0:T(8,128)S(1)}, f32[8,256]{1,0:T(8,128)S(1)}) custom-call(s32[32,128]{1,0:T(8,128)S(1)} %bitcast.4, bf16[256,1024]{1,0:T(8,128)(2,1)S(1)} %copy-done, bf16[256,1024]{1,0:T(8,128)(2,1)S(1)} %copy-done.1, ...), custom_call_target="tpu_custom_call" | custom-call | flops 2048 | tf_op jit(solution)/shard_map/rest_forward/pallas_call | solution.py:279
  14.3 0.1 collective-permute-start.3
  14.3 1.5 %line_backward.1 = (f32[256,256]{1,0:T(8,128)S(1)}, bf16[256,256]{1,0:T(8,128)(2,1)S(1)}, f32[8,128,256]{2,1,0:T(8,128)S(1)}) custom-call(s32[32,128]{1,0:T(8,128)S(1)} %bitcast.5, bf16[256,1024]{1,0:T(8,128)(2,1)S(1)} %copy-done, bf16[256,1024]{1,0:T(8,128)(2,1)S(1)} %copy-done.1, bf16[256,256]{1,0:T(8,128)(2,1)S(1)} %collective-permute-done.refs_2_.kv_ref, ...), custom_call_target="tpu_custom_call" | custom-call | flops 2048 | tf_op jit(solution)/shard_map/line_backward/pallas_call | solution.py:279
  15.8 0.0 collective-permute-done.3.mate_ref
  15.9 2.5 %collective-permute-start.4 = (bf16[256,256]{1,0:T(8,128)(2,1)S(1)}, bf16[256,256]{1,0:T(8,128)(2,1)S(1)}, u32[]{:S(2)}, u32[]{:S(2)}) collective-permute-start(bf16[256,256]{1,0:T(8,128)(2,1)S(1)} %line_add.1), channel_id=1, source_target_pairs={{4,0},{6,2},{8,4},{10,6},{12,8},{14,10},{16,12},{18,14},{20,16},{2... | collective-permute-start | bytes 393224 | tf_op jit(solution)/shard_map/ppermute | solution.py:360
  18.4 0.1 side_backward.1
  18.5 0.7 %collective-permute-start.6 = (bf16[256,256]{1,0:T(8,128)(2,1)S(1)}, bf16[256,256]{1,0:T(8,128)(2,1)S(1)}, u32[]{:S(2)}, u32[]{:S(2)}) collective-permute-start(bf16[256,256]{1,0:T(8,128)(2,1)S(1)} %get-tuple-element.63), channel_id=1, source_target_pairs={{8,2},{12,6},{16,10},{20,14},{24,18},{28,22},{6,12},{10,16},{14,20... | collective-permute-start | bytes 393224 | tf_op jit(solution)/shard_map/ppermute | solution.py:358
  19.2 0.1 collective-permute-start.5
  19.3 1.8 %own_backward.1 = (f32[256,256]{1,0:T(8,128)S(1)}, bf16[256,1024]{1,0:T(8,128)(2,1)}, bf16[256,1024]{1,0:T(8,128)(2,1)}) custom-call(bf16[256,1024]{1,0:T(8,128)(2,1)S(1)} %copy-done, bf16[256,1024]{1,0:T(8,128)(2,1)S(1)} %copy-done.1, bf16[256,256]{1,0:T(8,128)(2,1)S(1)} %settle.1.kv_ref, bf16[8,256,256]{2,1,0:T(8,128)(2,1)S(1)} %get-tuple-element.35.e_ref, ...), custom_call_target="tpu_custom_call" | custom-call | flops 2048 | tf_op jit(solution)/shard_map/own_backward/pallas_call | solution.py:279
  21.0 0.0 collective-permute-done.4.line_ref
  21.1 2.6 %collective-permute-done.6.far_ref = bf16[256,256]{1,0:T(8,128)(2,1)S(1)} collective-permute-done((bf16[256,256]{1,0:T(8,128)(2,1)S(1)}, bf16[256,256]{1,0:T(8,128)(2,1)S(1)}, u32[]{:S(2)}, u32[]{:S(2)}) %collective-permute-start.6) | collective-permute-done | bytes 131104 | tf_op jit(solution)/shard_map/ppermute | solution.py:358
  23.7 0.0 collective-permute-done.5.near_ref
  23.7 0.7 %side_sum.1 = (bf16[256,128]{1,0:T(8,128)(2,1)}, bf16[256,128]{1,0:T(8,128)(2,1)}) custom-call(f32[256,256]{1,0:T(8,128)S(1)} %line_sum.1.sum_ref, bf16[256,256]{1,0:T(8,128)(2,1)S(1)} %collective-permute-done.5.near_ref, bf16[256,256]{1,0:T(8,128)(2,1)S(1)} %collective-permute-done.6.far_ref), custom_call_target="tpu_custom_call" | custom-call | tf_op jit(solution)/shard_map/side_sum/pallas_call | solution.py:279
  (3 shorter events, 0.1 us)
Async XLA Ops:
  1.5 4.3 %copy-start = (bf16[256,1024]{1,0:T(8,128)(2,1)S(1)}, bf16[256,1024]{1,0:T(8,128)(2,1)}, u32[]{:S(2)}) copy-start(bf16[256,1024]{1,0:T(8,128)(2,1)} %q_ref.9) | copy-start | bytes 1572868
  1.5 4.3 %copy-start.1 = (bf16[256,1024]{1,0:T(8,128)(2,1)S(1)}, bf16[256,1024]{1,0:T(8,128)(2,1)}, u32[]{:S(2)}) copy-start(bf16[256,1024]{1,0:T(8,128)(2,1)} %g_ref.9) | copy-start | bytes 1572868
  1.6 4.3 %copy-start.2 = (s32[4096]{0:T(1024)S(1)}, s32[4096]{0:T(1024)}, u32[]{:S(2)}) copy-start(s32[4096]{0:T(1024)} %param.8) | copy-start | bytes 49156
  1.6 8.4 %collective-permute-start = (bf16[256,256]{1,0:T(8,128)(2,1)S(1)}, bf16[256,256]{1,0:T(8,128)(2,1)S(1)}, u32[]{:S(2)}, u32[]{:S(2)}) collective-permute-start(bf16[256,256]{1,0:T(8,128)(2,1)S(1)} %settle.1.kv_ref), channel_id=1, source_target_pairs={{0,4},{2,6},{4,8},{6,10},{8,12},{10,14},{12,16},{14,18},{16,20},{1... | collective-permute-start | bytes 393224 | tf_op jit(solution)/shard_map/ppermute | solution.py:323
  3.7 8.5 %collective-permute-start.2 = (bf16[256,256]{1,0:T(8,128)(2,1)S(1)}, bf16[256,256]{1,0:T(8,128)(2,1)S(1)}, u32[]{:S(2)}, u32[]{:S(2)}) collective-permute-start(bf16[256,256]{1,0:T(8,128)(2,1)S(1)} %settle.1.kv_ref), channel_id=1, source_target_pairs={{0,2},{2,8},{4,6},{6,12},{8,10},{10,16},{12,14},{14,20},{16,18},{1... | collective-permute-start | bytes 393224 | tf_op jit(solution)/shard_map/ppermute | solution.py:331
  10.0 3.5 %collective-permute-start.1 = (bf16[256,256]{1,0:T(8,128)(2,1)S(1)}, bf16[256,256]{1,0:T(8,128)(2,1)S(1)}, u32[]{:S(2)}, u32[]{:S(2)}) collective-permute-start(bf16[256,256]{1,0:T(8,128)(2,1)S(1)} %collective-permute-done.refs_2_.kv_ref), channel_id=1, source_target_pairs={{0,2},{2,0},{4,6},{6,4},{8,10},{10,8},{12,14},{14,12},{16,18},{18,... | collective-permute-start | bytes 393224 | tf_op jit(solution)/shard_map/ppermute | solution.py:332
  14.3 1.6 %collective-permute-start.3 = (bf16[256,256]{1,0:T(8,128)(2,1)S(1)}, bf16[256,256]{1,0:T(8,128)(2,1)S(1)}, u32[]{:S(2)}, u32[]{:S(2)}) collective-permute-start(bf16[256,256]{1,0:T(8,128)(2,1)S(1)} %get-tuple-element.52), channel_id=1, source_target_pairs={{0,2},{2,0},{4,6},{6,4},{8,10},{10,8},{12,14},{14,12},{16,18},{18,... | collective-permute-start | bytes 393224 | tf_op jit(solution)/shard_map/ppermute | solution.py:348
  15.9 5.2 %collective-permute-start.4 = (bf16[256,256]{1,0:T(8,128)(2,1)S(1)}, bf16[256,256]{1,0:T(8,128)(2,1)S(1)}, u32[]{:S(2)}, u32[]{:S(2)}) collective-permute-start(bf16[256,256]{1,0:T(8,128)(2,1)S(1)} %line_add.1), channel_id=1, source_target_pairs={{4,0},{6,2},{8,4},{10,6},{12,8},{14,10},{16,12},{18,14},{20,16},{2... | collective-permute-start | bytes 393224 | tf_op jit(solution)/shard_map/ppermute | solution.py:360
  18.5 5.3 %collective-permute-start.6 = (bf16[256,256]{1,0:T(8,128)(2,1)S(1)}, bf16[256,256]{1,0:T(8,128)(2,1)S(1)}, u32[]{:S(2)}, u32[]{:S(2)}) collective-permute-start(bf16[256,256]{1,0:T(8,128)(2,1)S(1)} %get-tuple-element.63), channel_id=1, source_target_pairs={{8,2},{12,6},{16,10},{20,14},{24,18},{28,22},{6,12},{10,16},{14,20... | collective-permute-start | bytes 393224 | tf_op jit(solution)/shard_map/ppermute | solution.py:358
  19.2 4.5 %collective-permute-start.5 = (bf16[256,256]{1,0:T(8,128)(2,1)S(1)}, bf16[256,256]{1,0:T(8,128)(2,1)S(1)}, u32[]{:S(2)}, u32[]{:S(2)}) collective-permute-start(bf16[256,256]{1,0:T(8,128)(2,1)S(1)} %get-tuple-element.63), channel_id=1, source_target_pairs={{0,2},{2,0},{4,6},{6,4},{8,10},{10,8},{12,14},{14,12},{16,18},{18,... | collective-permute-start | bytes 393224 | tf_op jit(solution)/shard_map/ppermute | solution.py:359

commit v5 on v4

--- a/solution.py
+++ b/solution.py
@@ -50,27 +50,30 @@
         bias[i * LANES : (i + 1) * LANES, :] = jnp.where(same, 0.0, MASKED)
 
 
-def forward(q_ref, kv_ref, bias, e_ref, stat_ref, out_ref, s_ref, vt_ref):
+def forward(q_ref, kv_ref, bias, gt_ref, e_ref, stat_ref, out_ref, s_ref, vt_ref):
     dim = kv_ref.shape[1] // 2
     heads = q_ref.shape[1] // dim
     factor = dim**-0.5 * LOG2_E
     vt_ref[...] = jnp.transpose(kv_ref[:, dim:])
     for h in range(heads):
-        s = nt(kv_ref[:, :dim], q_ref[:, h * dim : (h + 1) * dim]) + bias[...]
-        s_ref[h] = s
-        stat_ref[h : h + 1, :] = jnp.max(s, axis=0, keepdims=True)
-    for h in range(heads):
-        e = jnp.exp2((s_ref[h] - stat_ref[h : h + 1, :]) * factor)
+        s_ref[h] = nt(kv_ref[:, :dim], q_ref[:, h * dim : (h + 1) * dim])
+    for h in range(heads):
+        s = s_ref[h] * factor + bias[...]
+        top = jnp.max(s, axis=0, keepdims=True)
+        e = jnp.exp2(s - top)
         e_ref[h] = e.astype(jnp.bfloat16)
+        stat_ref[h : h + 1, :] = top
         stat_ref[heads + h : heads + h + 1, :] = jnp.sum(e, axis=0, keepdims=True)
     for h in range(heads):
-        out_ref[h] = nn(vt_ref[...], e_ref[h])
+        out = nn(vt_ref[...], e_ref[h])
+        out_ref[h] = out
+        stat_ref[2 * heads + h : 2 * heads + h + 1, :] = jnp.sum(out * gt_ref[h].astype(jnp.float32), axis=0, keepdims=True)
 
 
 def forward_unseen(stat_ref, out_ref):
     heads = out_ref.shape[0]
     stat_ref[:heads, :] = jnp.full((heads, stat_ref.shape[1]), MASKED, jnp.float32)
-    stat_ref[heads:, :] = jnp.zeros((heads, stat_ref.shape[1]), jnp.float32)
+    stat_ref[heads:, :] = jnp.zeros((2 * heads, stat_ref.shape[1]), jnp.float32)
     out_ref[...] = jnp.zeros(out_ref.shape, out_ref.dtype)
 
 
@@ -79,10 +82,10 @@
     heads = g_ref.shape[1] // dim
     kt_ref[...] = jnp.transpose(kv_ref[:, :dim])
     for h in range(heads):
-        probs = e_ref[h].astype(jnp.float32) * scale_ref[h : h + 1, :]
-        p_ref[h] = probs.astype(jnp.bfloat16)
+        probs = e_ref[h] * scale_ref[h : h + 1, :].astype(jnp.bfloat16)
+        p_ref[h] = probs
         grad_p = nt(kv_ref[:, dim:], g_ref[:, h * dim : (h + 1) * dim]) if dp is None else dp[h]
-        ds_ref[h] = (probs * (grad_p - delta_ref[h : h + 1, :])).astype(jnp.bfloat16)
+        ds_ref[h] = probs * (grad_p - delta_ref[h : h + 1, :]).astype(jnp.bfloat16)
     for h in range(heads):
         gq_out(h, nn(kt_ref[...], ds_ref[h]))
 
@@ -120,21 +123,21 @@
     dim = kv_ref.shape[1] // 2
     heads = q_ref.shape[1] // dim
     mask_bias(OWN, doc_ref, bias)
-    forward(q_ref, kv_ref, bias, e_ref, stat_ref, out_ref, s_ref, vt_ref)
+    for h in range(heads):
+        gt_ref[h] = jnp.transpose(g_ref[:, h * dim : (h + 1) * dim])
+    forward(q_ref, kv_ref, bias, gt_ref, e_ref, stat_ref, out_ref, s_ref, vt_ref)
     for role in (MATE, LINE, SIDE):
         mask_bias(role, doc_ref, bias_ref.at[role - 1])
     for h in range(heads):
-        g = g_ref[:, h * dim : (h + 1) * dim]
-        gt_ref[h] = jnp.transpose(g)
-        dp_ref[h] = nt(kv_ref[:, dim:], g)
-
-
-def next_kernel(role, doc_ref, q_ref, kv_ref, bias_ref, e_ref, stat_ref, out_ref, s_ref, vt_ref):
+        dp_ref[h] = nt(kv_ref[:, dim:], g_ref[:, h * dim : (h + 1) * dim])
+
+
+def next_kernel(role, doc_ref, q_ref, kv_ref, bias_ref, gt_ref, e_ref, stat_ref, out_ref, s_ref, vt_ref):
     seen = is_seen(role, doc_ref, kv_ref.shape[0])
 
     @pl.when(seen)
     def _():
-        forward(q_ref, kv_ref, bias_ref.at[role - 1], e_ref, stat_ref, out_ref, s_ref, vt_ref)
+        forward(q_ref, kv_ref, bias_ref.at[role - 1], gt_ref, e_ref, stat_ref, out_ref, s_ref, vt_ref)
 
     @pl.when(jnp.logical_not(seen))
     def _():
@@ -142,98 +145,95 @@
 
 
 def next_backward(seen, q_ref, g_ref, kv_ref, e_ref, scale_ref, delta_ref, gq_in, part_ref, gq_ref, kt_ref, p_ref, ds_ref):
-    @pl.when(seen)
-    def _():
+    def run():
         def put(h, value):
             gq_ref[h] = value if gq_in is None else gq_in[h] + value
 
         backward_queries(g_ref, kv_ref, e_ref, scale_ref, delta_ref, put, kt_ref, p_ref, ds_ref)
         backward_keys(q_ref, g_ref, p_ref, ds_ref, part_ref)
 
+    if seen is True:
+        run()
+        return
+    pl.when(seen)(run)
+
     @pl.when(jnp.logical_not(seen))
     def _():
         backward_unseen(part_ref, gq_in, gq_ref)
 
 
 def rest_kernel(
-    doc_ref, q_ref, g_ref, mate_ref, bias_ref, gt_ref, own_stat, own_o, line_stat, line_o, side_stat, side_o,
-    att_t, mate_part, gq_part, scale_ref, delta_ref,
-    s_ref, vt_ref, mate_e, mate_stat, mate_o, kt_ref, p_ref, ds_ref,
+    doc_ref, q_ref, g_ref, mate_ref, side_ref, bias_ref, gt_ref, own_stat, line_stat, side_stat, side_e,
+    mate_o, mate_part, side_part, gq_part, scale_ref, delta_ref,
+    s_ref, vt_ref, mate_e, mate_stat, kt_ref, p_ref, ds_ref,
 ):
     dim = mate_ref.shape[1] // 2
     heads = q_ref.shape[1] // dim
-    factor = dim**-0.5 * LOG2_E
-    next_kernel(MATE, doc_ref, q_ref, mate_ref, bias_ref, mate_e, mate_stat, mate_o, s_ref, vt_ref)
+    next_kernel(MATE, doc_ref, q_ref, mate_ref, bias_ref, gt_ref, mate_e, mate_stat, mate_o, s_ref, vt_ref)
     stats = (own_stat, mate_stat, line_stat, side_stat)
     tops = [ref[:heads, :] for ref in stats]
     top = jnp.maximum(jnp.maximum(tops[0], tops[1]), jnp.maximum(tops[2], tops[3]))
-    parts = [jnp.exp2((t - top) * factor) for t in tops]
-    inverse = 1.0 / sum(p * ref[heads:, :] for p, ref in zip(parts, stats))
+    parts = [jnp.exp2(t - top) for t in tops]
+    inverse = 1.0 / sum(p * ref[heads : 2 * heads, :] for p, ref in zip(parts, stats))
     for b in range(4):
         scale_ref[b] = parts[b] * inverse
-    for h in range(heads):
-        out = sum(ref[h] * scale_ref[b, h : h + 1, :] for b, ref in enumerate((own_o, mate_o, line_o, side_o)))
-        att_t[h] = out.astype(jnp.bfloat16)
-        delta_ref[h : h + 1, :] = jnp.sum(out * gt_ref[h].astype(jnp.float32), axis=0, keepdims=True)
+    delta_ref[...] = sum(p * ref[2 * heads :, :] for p, ref in zip(parts, stats)) * inverse
+    rows = mate_ref.shape[0]
+    seen = is_seen(MATE, doc_ref, rows)
+
+    @pl.when(seen)
+    def _():
+        next_backward(
+            True, q_ref, g_ref, mate_ref, mate_e, scale_ref.at[MATE], delta_ref, None, mate_part, gq_part, kt_ref, p_ref, ds_ref
+        )
+
+    @pl.when(jnp.logical_not(seen))
+    def _():
+        mate_part[...] = jnp.zeros(mate_part.shape, mate_part.dtype)
+        next_backward(
+            is_seen(SIDE, doc_ref, rows), q_ref, g_ref, side_ref, side_e, scale_ref.at[SIDE], delta_ref, None,
+            side_part, gq_part, kt_ref, p_ref, ds_ref,
+        )
+
+
+def line_kernel(doc_ref, q_ref, g_ref, kv_ref, e_ref, scale_ref, delta_ref, gq_in, part_ref, gq_ref, kt_ref, p_ref, ds_ref):
     next_backward(
-        is_seen(MATE, doc_ref, mate_ref.shape[0]), q_ref, g_ref, mate_ref, mate_e, scale_ref.at[MATE], delta_ref, None,
-        mate_part, gq_part, kt_ref, p_ref, ds_ref,
-    )
-
-
-def line_kernel(
-    doc_ref, q_ref, g_ref, kv_ref, e_ref, side_ref, side_e, scale_ref, delta_ref, gq_in,
-    part_ref, side_part, gq_ref, kt_ref, p_ref, ds_ref,
-):
-    rows = kv_ref.shape[0]
-    first_chip = lax.axis_index("ctx") < 2
-    common = (q_ref, g_ref)
-
-    @pl.when(jnp.logical_not(first_chip))
-    def _():
-        next_backward(
-            is_seen(LINE, doc_ref, rows), *common, kv_ref, e_ref, scale_ref.at[LINE], delta_ref, gq_in,
-            part_ref, gq_ref, kt_ref, p_ref, ds_ref,
-        )
-
-    @pl.when(first_chip)
-    def _():
-        part_ref[...] = jnp.zeros(part_ref.shape, part_ref.dtype)
-        next_backward(
-            is_seen(SIDE, doc_ref, rows), *common, side_ref, side_e, scale_ref.at[SIDE], delta_ref, gq_in,
-            side_part, gq_ref, kt_ref, p_ref, ds_ref,
-        )
-
-
-def turn(h, value, buf):
-    buf[:, h * value.shape[0] : (h + 1) * value.shape[0]] = jnp.transpose(value.astype(jnp.bfloat16))
+        is_seen(LINE, doc_ref, kv_ref.shape[0]), q_ref, g_ref, kv_ref, e_ref, scale_ref.at[LINE], delta_ref, gq_in,
+        part_ref, gq_ref, kt_ref, p_ref, ds_ref,
+    )
 
 
 def side_kernel(
     doc_ref, q_ref, g_ref, kv_ref, e_ref, scale_ref, delta_ref, gq_in, early_part, part_ref, gq_ref, kt_ref, p_ref, ds_ref
 ):
-    first_chip = lax.axis_index("ctx") < 2
-
-    @pl.when(jnp.logical_not(first_chip))
+    rows = kv_ref.shape[0]
+    late = is_seen(MATE, doc_ref, rows)
+
+    @pl.when(late)
     def _():
         next_backward(
-            is_seen(SIDE, doc_ref, kv_ref.shape[0]), q_ref, g_ref, kv_ref, e_ref, scale_ref.at[SIDE], delta_ref, gq_in,
+            is_seen(SIDE, doc_ref, rows), q_ref, g_ref, kv_ref, e_ref, scale_ref.at[SIDE], delta_ref, gq_in,
             part_ref, gq_ref, kt_ref, p_ref, ds_ref,
         )
 
-    @pl.when(first_chip)
+    @pl.when(jnp.logical_not(late))
     def _():
         part_ref[...] = early_part[...]
         gq_ref[...] = gq_in[...]
 
 
+def turn(h, value, buf):
+    buf[:, h * value.shape[0] : (h + 1) * value.shape[0]] = jnp.transpose(value.astype(jnp.bfloat16))
+
+
 def last_kernel(
-    q_ref, g_ref, kv_ref, e_ref, scale_ref, delta_ref, gq_in, dp_ref, att_t, part_ref, gq_ref, att_ref,
+    q_ref, g_ref, kv_ref, e_ref, scale_ref, delta_ref, gq_in, dp_ref, own_o, mate_o, line_o, side_o, part_ref, gq_ref, att_ref,
     kt_ref, p_ref, ds_ref, buf, att_buf, sems,
 ):
     factor = (kv_ref.shape[1] // 2) ** -0.5
-    for h in range(att_t.shape[0]):
-        turn(h, att_t[h], att_buf)
+    for h in range(own_o.shape[0]):
+        out = sum(ref[h] * scale_ref[b, h : h + 1, :] for b, ref in enumerate((own_o, mate_o, line_o, side_o)))
+        turn(h, out, att_buf)
     att_copy = pltpu.make_async_copy(att_buf, att_ref, sems.at[0])
     gq_copy = pltpu.make_async_copy(buf, gq_ref, sems.at[1])
     att_copy.start()
@@ -306,7 +306,7 @@
     flip = lambda pairs: [(b, a) for a, b in pairs]
     f32, bf16 = jnp.float32, jnp.bfloat16
     shape = jax.ShapeDtypeStruct
-    e_shape, stat_shape, out_shape = shape((heads, rows, rows), bf16), shape((2 * heads, rows), f32), shape((heads, dim, rows), f32)
+    e_shape, stat_shape, out_shape = shape((heads, rows, rows), bf16), shape((3 * heads, rows), f32), shape((heads, dim, rows), f32)
     pair, pair_sent = shape((rows, 2 * dim), f32), shape((rows, 2 * dim), bf16)
     wide = shape(queries.shape, bf16)
     buffer = lambda like: pltpu.VMEM(like.shape, like.dtype)
@@ -333,22 +333,21 @@
 
     def first(name, role, kv):
         return call(
-            name, lambda *refs: next_kernel(role, *refs), (docs, q, kv, bias), (e_shape, stat_shape, out_shape), ahead, work
+            name, lambda *refs: next_kernel(role, *refs), (docs, q, kv, bias, gt), (e_shape, stat_shape, out_shape), ahead, work
         )
 
     line_e, line_stat, line_o = first("line_forward", LINE, line)
     side_e, side_stat, side_o = first("side_forward", SIDE, side)
-    attended_t, mate_part, gq, scales, delta = call(
+    mate_o, mate_part, early_part, gq, scales, delta = call(
         "rest_forward", rest_kernel,
-        (docs, q, g, mate, bias, gt, own_stat, own_o, line_stat, line_o, side_stat, side_o),
-        (shape((heads, dim, rows), bf16), pair_sent, out_shape, shape((4, heads, rows), f32), shape((heads, rows), f32)),
-        [*ahead, buffer(e_shape), buffer(stat_shape), buffer(out_shape), *back],
+        (docs, q, g, mate, side, bias, gt, own_stat, line_stat, side_stat, side_e),
+        (out_shape, pair_sent, pair_sent, out_shape, shape((4, heads, rows), f32), shape((heads, rows), f32)),
+        [*ahead, buffer(e_shape), buffer(stat_shape), *back],
         work,
     )
     mate_back = lax.ppermute(mate_part, "ctx", to_mate)
-    line_part, early_part, gq = call(
-        "line_backward", line_kernel, (docs, q, g, line, line_e, side, side_e, scales, delta, gq), (pair, pair_sent, out_shape),
-        back, work,
+    line_part, gq = call(
+        "line_backward", line_kernel, (docs, q, g, line, line_e, scales, delta, gq), (pair, out_shape), back, work
     )
     line_part = call("line_add", line_add_kernel, (line_part, mate_back), (pair_sent,), [], 0)[0]
     line_part, gq = lax.optimization_barrier((line_part, gq))
@@ -359,7 +358,7 @@
     side_near = lax.ppermute(side_part, "ctx", to_mate)
     line_back = lax.ppermute(line_part, "ctx", flip(to_line))
     own_part, grad_query, attended = call(
-        "own_backward", last_kernel, (q, g, own, own_e, scales, delta, gq, dp, attended_t), (pair, wide, wide),
+        "own_backward", last_kernel, (q, g, own, own_e, scales, delta, gq, dp, own_o, mate_o, line_o, side_o), (pair, wide, wide),
         [*back, buffer(wide), buffer(wide), pltpu.SemaphoreType.DMA((2,))], work, (), (1, 2),
     )
     total = call("line_sum", line_sum_kernel, (own_part, line_back), (pair,), [], work)[0]

time: 24.8 us -> 24.1 us (0.972)
  starting transfers between devices: 9.64 us -> 8.78 us
  waiting for transfers between devices: 5.34 us -> 5.93 us
  Pallas kernels: 8.63 us -> 8.38 us
    ppermute x1, waiting for transfers between devices: 2.65 us -> 1.54 us  [body(): side_far = lax.ppermute(side_part, 'ctx', three_back(count))]
    ppermute x1, waiting for transfers between devices: 0.01 us -> 1.1 us  [body(): mate_back = lax.ppermute(mate_part, 'ctx', to_mate)]
    ppermute x1, starting transfers between devices: 2.51 us -> 1.8 us  [body(): line_back = lax.ppermute(line_part, 'ctx', flip(to_line))]
    ppermute x1, waiting for transfers between devices: 0.01 us -> 0.64 us  [body(): line_back = lax.ppermute(line_part, 'ctx', flip(to_line))]
    pallas_call x12, Pallas kernels: 8.63 us -> 8.38 us  [call(): pl.pallas_call(kernel, name=name, out_shape=outs, in_specs=[far if i in f...]
  transfers between devices with their start and end apart: 7 -> 7, of which waited for: 2 -> 4; matrix products, arithmetic and copies ran while one was open for 0% -> 0% of each run, Pallas kernels for 26% -> 21%
where the time goes in v5:
time: 24.1 us; the launch traced here: 23.9 us
  starting transfers between devices  8.78 us (36%)
  Pallas kernels  8.38 us (35%)
  waiting for transfers between devices  5.93 us (25%)
  between operations  0.76 us (3%)
    pallas_call x12, Pallas kernels, call(): pl.pallas_call(kernel, name=name, out_shape=outs, in_specs=[far if i in f...  8.38 us
    ppermute x1, waiting for transfers between devices, body(): line = lax.ppermute(own, 'ctx', to_line)  2.64 us
    ppermute x1, starting transfers between devices, body(): side = lax.ppermute(own, 'ctx', to_side)  2.14 us
    ppermute x1, starting transfers between devices, body(): line = lax.ppermute(own, 'ctx', to_line)  2.12 us
    ppermute x1, starting transfers between devices, body(): mate = lax.ppermute(line, 'ctx', to_mate)  2 us
    ppermute x1, starting transfers between devices, body(): line_back = lax.ppermute(line_part, 'ctx', flip(to_line))  1.8 us
    ppermute x1, waiting for transfers between devices, body(): side_far = lax.ppermute(side_part, 'ctx', three_back(count))  1.54 us
    ppermute x1, waiting for transfers between devices, body(): mate_back = lax.ppermute(mate_part, 'ctx', to_mate)  1.1 us
  transfers between devices with their start and end apart: 7, of which 4 were waited for; matrix products, arithmetic and copies ran while one was open for 0% of the time, Pallas kernels for 21%

profile of v5, /device:TPU:1, one launch (start us, length us, event | category | flops | bytes accessed | tf_op | source)
XLA Modules:
  0.0 23.9 jit_solution(4465402485183460436)
XLA Ops:
  0.6 0.9 %pack.1.in_ref = bf16[256,256]{1,0:T(8,128)(2,1)S(1)} custom-call(bf16[256,128]{1,0:T(8,128)(2,1)} %k_ref.1, bf16[256,128]{1,0:T(8,128)(2,1)} %v_ref.1), custom_call_target="tpu_custom_call" | custom-call | tf_op jit(solution)/shard_map/pack/pallas_call | solution.py:279
  1.5 0.0 copy-start
  1.5 0.0 copy-start.1
  1.6 0.0 copy-start.2
  1.6 2.1 %collective-permute-start = (bf16[256,256]{1,0:T(8,128)(2,1)S(1)}, bf16[256,256]{1,0:T(8,128)(2,1)S(1)}, u32[]{:S(2)}, u32[]{:S(2)}) collective-permute-start(bf16[256,256]{1,0:T(8,128)(2,1)S(1)} %settle.1.kv_ref), channel_id=1, source_target_pairs={{0,4},{2,6},{4,8},{6,10},{8,12},{10,14},{12,16},{14,18},{16,20},{1... | collective-permute-start | bytes 393224 | tf_op jit(solution)/shard_map/ppermute | solution.py:323
  3.7 2.1 %collective-permute-start.2 = (bf16[256,256]{1,0:T(8,128)(2,1)S(1)}, bf16[256,256]{1,0:T(8,128)(2,1)S(1)}, u32[]{:S(2)}, u32[]{:S(2)}) collective-permute-start(bf16[256,256]{1,0:T(8,128)(2,1)S(1)} %settle.1.kv_ref), channel_id=1, source_target_pairs={{0,2},{2,8},{4,6},{6,12},{8,10},{10,16},{12,14},{14,20},{16,18},{1... | collective-permute-start | bytes 393224 | tf_op jit(solution)/shard_map/ppermute | solution.py:331
  5.8 0.0 copy-done
  5.8 0.0 copy-done.1
  5.8 0.0 copy-done.2
  5.8 1.5 %own_forward.1 = (bf16[8,256,256]{2,1,0:T(8,128)(2,1)S(1)}, f32[24,256]{1,0:T(8,128)S(1)}, f32[8,128,256]{2,1,0:T(8,128)S(1)}, f32[3,256,256]{2,1,0:T(8,128)S(1)...) custom-call(s32[32,128]{1,0:T(8,128)S(1)} %bitcast.1, bf16[256,1024]{1,0:T(8,128)(2,1)S(1)} %copy-done, ...), custom_call_target="tpu_custom_call" | custom-call | flops 2048 | tf_op jit(solution)/shard_map/own_forward/pallas_call | solution.py:279
  7.3 2.6 %collective-permute-done.refs_2_.kv_ref = bf16[256,256]{1,0:T(8,128)(2,1)S(1)} collective-permute-done((bf16[256,256]{1,0:T(8,128)(2,1)S(1)}, bf16[256,256]{1,0:T(8,128)(2,1)S(1)}, u32[]{:S(2)}, u32[]{:S(2)}) %collective-permute-start) | collective-permute-done | bytes 131104 | tf_op jit(solution)/shard_map/ppermute | solution.py:323
  10.0 2.0 %collective-permute-start.1 = (bf16[256,256]{1,0:T(8,128)(2,1)S(1)}, bf16[256,256]{1,0:T(8,128)(2,1)S(1)}, u32[]{:S(2)}, u32[]{:S(2)}) collective-permute-start(bf16[256,256]{1,0:T(8,128)(2,1)S(1)} %collective-permute-done.refs_2_.kv_ref), channel_id=1, source_target_pairs={{0,2},{2,0},{4,6},{6,4},{8,10},{10,8},{12,14},{14,12},{16,18},{18,... | collective-permute-start | bytes 393224 | tf_op jit(solution)/shard_map/ppermute | solution.py:332
  12.0 0.2 line_forward.1
  12.2 0.0 collective-permute-done.2.refs_2_.side_ref.kv_ref
  12.2 1.3 %side_forward.1 = (bf16[8,256,256]{2,1,0:T(8,128)(2,1)S(1)}, f32[24,256]{1,0:T(8,128)S(1)}, f32[8,128,256]{2,1,0:T(8,128)S(1)}) custom-call(s32[32,128]{1,0:T(8,128)S(1)} %bitcast.3, bf16[256,1024]{1,0:T(8,128)(2,1)S(1)} %copy-done, bf16[256,256]{1,0:T(8,128)(2,1)S(1)} %collective-permute-done.2.refs_2_.side_ref.kv_ref, ...), custom_call_target="tpu_custom_call" | custom-call | flops 2048 | tf_op jit(solution)/shard_map/side_forward/pallas_call | solution.py:279
  13.4 0.0 collective-permute-done.1.mate_ref
  13.4 1.7 %rest_forward.1 = (f32[8,128,256]{2,1,0:T(8,128)S(1)}, bf16[256,256]{1,0:T(8,128)(2,1)S(1)}, bf16[256,256]{1,0:T(8,128)(2,1)S(1)}, f32[8,128,256]{2,1,0:T(8,128)...) custom-call(s32[32,128]{1,0:T(8,128)S(1)} %bitcast.4, bf16[256,1024]{1,0:T(8,128)(2,1)S(1)} %copy-done, ...), custom_call_target="tpu_custom_call" | custom-call | flops 2048 | tf_op jit(solution)/shard_map/rest_forward/pallas_call | solution.py:279
  15.2 0.1 collective-permute-start.3
  15.2 0.2 line_backward.1
  15.5 1.1 %collective-permute-done.3.mate_ref = bf16[256,256]{1,0:T(8,128)(2,1)S(1)} collective-permute-done((bf16[256,256]{1,0:T(8,128)(2,1)S(1)}, bf16[256,256]{1,0:T(8,128)(2,1)S(1)}, u32[]{:S(2)}, u32[]{:S(2)}) %collective-permute-start.3) | collective-permute-done | bytes 131104 | tf_op jit(solution)/shard_map/ppermute | solution.py:348
  16.6 1.8 %collective-permute-start.4 = (bf16[256,256]{1,0:T(8,128)(2,1)S(1)}, bf16[256,256]{1,0:T(8,128)(2,1)S(1)}, u32[]{:S(2)}, u32[]{:S(2)}) collective-permute-start(bf16[256,256]{1,0:T(8,128)(2,1)S(1)} %line_add.1), channel_id=1, source_target_pairs={{4,0},{6,2},{8,4},{10,6},{12,8},{14,10},{16,12},{18,14},{20,16},{2... | collective-permute-start | bytes 393224 | tf_op jit(solution)/shard_map/ppermute | solution.py:359
  18.4 0.2 side_backward.1
  18.6 0.5 %collective-permute-start.6 = (bf16[256,256]{1,0:T(8,128)(2,1)S(1)}, bf16[256,256]{1,0:T(8,128)(2,1)S(1)}, u32[]{:S(2)}, u32[]{:S(2)}) collective-permute-start(bf16[256,256]{1,0:T(8,128)(2,1)S(1)} %get-tuple-element.63), channel_id=1, source_target_pairs={{8,2},{12,6},{16,10},{20,14},{24,18},{28,22},{6,12},{10,16},{14,20... | collective-permute-start | bytes 393224 | tf_op jit(solution)/shard_map/ppermute | solution.py:357
  19.1 0.1 collective-permute-start.5
  19.3 1.7 %own_backward.1 = (f32[256,256]{1,0:T(8,128)S(1)}, bf16[256,1024]{1,0:T(8,128)(2,1)}, bf16[256,1024]{1,0:T(8,128)(2,1)}) custom-call(bf16[256,1024]{1,0:T(8,128)(2,1)S(1)} %copy-done, bf16[256,1024]{1,0:T(8,128)(2,1)S(1)} %copy-done.1, bf16[256,256]{1,0:T(8,128)(2,1)S(1)} %settle.1.kv_ref, bf16[8,256,256]{2,1,0:T(8,128)(2,1)S(1)} %get-tuple-element.35.e_ref, ...), custom_call_target="tpu_custom_call" | custom-call | flops 2048 | tf_op jit(solution)/shard_map/own_backward/pallas_call | solution.py:279
  21.0 0.6 %collective-permute-done.4.line_ref = bf16[256,256]{1,0:T(8,128)(2,1)S(1)} collective-permute-done((bf16[256,256]{1,0:T(8,128)(2,1)S(1)}, bf16[256,256]{1,0:T(8,128)(2,1)S(1)}, u32[]{:S(2)}, u32[]{:S(2)}) %collective-permute-start.4) | collective-permute-done | bytes 131104 | tf_op jit(solution)/shard_map/ppermute | solution.py:359
  21.6 1.5 %collective-permute-done.6.far_ref = bf16[256,256]{1,0:T(8,128)(2,1)S(1)} collective-permute-done((bf16[256,256]{1,0:T(8,128)(2,1)S(1)}, bf16[256,256]{1,0:T(8,128)(2,1)S(1)}, u32[]{:S(2)}, u32[]{:S(2)}) %collective-permute-start.6) | collective-permute-done | bytes 131104 | tf_op jit(solution)/shard_map/ppermute | solution.py:357
  23.2 0.0 collective-permute-done.5.near_ref
  23.2 0.7 %side_sum.1 = (bf16[256,128]{1,0:T(8,128)(2,1)}, bf16[256,128]{1,0:T(8,128)(2,1)}) custom-call(f32[256,256]{1,0:T(8,128)S(1)} %line_sum.1.sum_ref, bf16[256,256]{1,0:T(8,128)(2,1)S(1)} %collective-permute-done.5.near_ref, bf16[256,256]{1,0:T(8,128)(2,1)S(1)} %collective-permute-done.6.far_ref), custom_call_target="tpu_custom_call" | custom-call | tf_op jit(solution)/shard_map/side_sum/pallas_call | solution.py:279
  (3 shorter events, 0.1 us)
Async XLA Ops:
  1.5 4.3 %copy-start = (bf16[256,1024]{1,0:T(8,128)(2,1)S(1)}, bf16[256,1024]{1,0:T(8,128)(2,1)}, u32[]{:S(2)}) copy-start(bf16[256,1024]{1,0:T(8,128)(2,1)} %q_ref.9) | copy-start | bytes 1572868
  1.5 4.3 %copy-start.1 = (bf16[256,1024]{1,0:T(8,128)(2,1)S(1)}, bf16[256,1024]{1,0:T(8,128)(2,1)}, u32[]{:S(2)}) copy-start(bf16[256,1024]{1,0:T(8,128)(2,1)} %g_ref.9) | copy-start | bytes 1572868
  1.6 4.3 %copy-start.2 = (s32[4096]{0:T(1024)S(1)}, s32[4096]{0:T(1024)}, u32[]{:S(2)}) copy-start(s32[4096]{0:T(1024)} %param.8) | copy-start | bytes 49156
  1.6 8.4 %collective-permute-start = (bf16[256,256]{1,0:T(8,128)(2,1)S(1)}, bf16[256,256]{1,0:T(8,128)(2,1)S(1)}, u32[]{:S(2)}, u32[]{:S(2)}) collective-permute-start(bf16[256,256]{1,0:T(8,128)(2,1)S(1)} %settle.1.kv_ref), channel_id=1, source_target_pairs={{0,4},{2,6},{4,8},{6,10},{8,12},{10,14},{12,16},{14,18},{16,20},{1... | collective-permute-start | bytes 393224 | tf_op jit(solution)/shard_map/ppermute | solution.py:323
  3.7 8.5 %collective-permute-start.2 = (bf16[256,256]{1,0:T(8,128)(2,1)S(1)}, bf16[256,256]{1,0:T(8,128)(2,1)S(1)}, u32[]{:S(2)}, u32[]{:S(2)}) collective-permute-start(bf16[256,256]{1,0:T(8,128)(2,1)S(1)} %settle.1.kv_ref), channel_id=1, source_target_pairs={{0,2},{2,8},{4,6},{6,12},{8,10},{10,16},{12,14},{14,20},{16,18},{1... | collective-permute-start | bytes 393224 | tf_op jit(solution)/shard_map/ppermute | solution.py:331
  10.0 3.5 %collective-permute-start.1 = (bf16[256,256]{1,0:T(8,128)(2,1)S(1)}, bf16[256,256]{1,0:T(8,128)(2,1)S(1)}, u32[]{:S(2)}, u32[]{:S(2)}) collective-permute-start(bf16[256,256]{1,0:T(8,128)(2,1)S(1)} %collective-permute-done.refs_2_.kv_ref), channel_id=1, source_target_pairs={{0,2},{2,0},{4,6},{6,4},{8,10},{10,8},{12,14},{14,12},{16,18},{18,... | collective-permute-start | bytes 393224 | tf_op jit(solution)/shard_map/ppermute | solution.py:332
  15.2 1.4 %collective-permute-start.3 = (bf16[256,256]{1,0:T(8,128)(2,1)S(1)}, bf16[256,256]{1,0:T(8,128)(2,1)S(1)}, u32[]{:S(2)}, u32[]{:S(2)}) collective-permute-start(bf16[256,256]{1,0:T(8,128)(2,1)S(1)} %get-tuple-element.49), channel_id=1, source_target_pairs={{0,2},{2,0},{4,6},{6,4},{8,10},{10,8},{12,14},{14,12},{16,18},{18,... | collective-permute-start | bytes 393224 | tf_op jit(solution)/shard_map/ppermute | solution.py:348
  16.6 5.0 %collective-permute-start.4 = (bf16[256,256]{1,0:T(8,128)(2,1)S(1)}, bf16[256,256]{1,0:T(8,128)(2,1)S(1)}, u32[]{:S(2)}, u32[]{:S(2)}) collective-permute-start(bf16[256,256]{1,0:T(8,128)(2,1)S(1)} %line_add.1), channel_id=1, source_target_pairs={{4,0},{6,2},{8,4},{10,6},{12,8},{14,10},{16,12},{18,14},{20,16},{2... | collective-permute-start | bytes 393224 | tf_op jit(solution)/shard_map/ppermute | solution.py:359
  18.6 4.5 %collective-permute-start.6 = (bf16[256,256]{1,0:T(8,128)(2,1)S(1)}, bf16[256,256]{1,0:T(8,128)(2,1)S(1)}, u32[]{:S(2)}, u32[]{:S(2)}) collective-permute-start(bf16[256,256]{1,0:T(8,128)(2,1)S(1)} %get-tuple-element.63), channel_id=1, source_target_pairs={{8,2},{12,6},{16,10},{20,14},{24,18},{28,22},{6,12},{10,16},{14,20... | collective-permute-start | bytes 393224 | tf_op jit(solution)/shard_map/ppermute | solution.py:357
  19.1 4.0 %collective-permute-start.5 = (bf16[256,256]{1,0:T(8,128)(2,1)S(1)}, bf16[256,256]{1,0:T(8,128)(2,1)S(1)}, u32[]{:S(2)}, u32[]{:S(2)}) collective-permute-start(bf16[256,256]{1,0:T(8,128)(2,1)S(1)} %get-tuple-element.63), channel_id=1, source_target_pairs={{0,2},{2,0},{4,6},{6,4},{8,10},{10,8},{12,14},{14,12},{16,18},{18,... | collective-permute-start | bytes 393224 | tf_op jit(solution)/shard_map/ppermute | solution.py:358

commit v6 on v5

--- a/solution.py
+++ b/solution.py
@@ -28,11 +28,15 @@
     return here * steps, lax.rem(block + count, count) * steps, block >= 0
 
 
-def is_seen(role, doc_ref, rows):
+def find_seen(role, doc_ref, rows):
     mine, at, valid = place(role, rows)
     first = jnp.min(doc_ref[pl.ds(mine, 1), :].astype(jnp.float32))
     last = jnp.max(doc_ref[pl.ds(at + rows // LANES - 1, 1), :].astype(jnp.float32))
     return valid & (first == last)
+
+
+def is_seen(role, seen_ref):
+    return seen_ref[role : role + 1, :][0, 0] > 0
 
 
 def mask_bias(role, doc_ref, bias):
@@ -119,7 +123,7 @@
     out_ref[:16, :] = in_ref[:16, :]
 
 
-def own_kernel(doc_ref, q_ref, g_ref, kv_ref, e_ref, stat_ref, out_ref, bias_ref, gt_ref, dp_ref, bias, s_ref, vt_ref):
+def own_kernel(doc_ref, q_ref, g_ref, kv_ref, e_ref, stat_ref, out_ref, bias_ref, gt_ref, dp_ref, seen_ref, bias, s_ref, vt_ref):
     dim = kv_ref.shape[1] // 2
     heads = q_ref.shape[1] // dim
     mask_bias(OWN, doc_ref, bias)
@@ -128,12 +132,14 @@
     forward(q_ref, kv_ref, bias, gt_ref, e_ref, stat_ref, out_ref, s_ref, vt_ref)
     for role in (MATE, LINE, SIDE):
         mask_bias(role, doc_ref, bias_ref.at[role - 1])
+        seen = find_seen(role, doc_ref, kv_ref.shape[0]).astype(jnp.int32)
+        seen_ref[role : role + 1, :] = jnp.full((1, LANES), seen, jnp.int32)
     for h in range(heads):
         dp_ref[h] = nt(kv_ref[:, dim:], g_ref[:, h * dim : (h + 1) * dim])
 
 
-def next_kernel(role, doc_ref, q_ref, kv_ref, bias_ref, gt_ref, e_ref, stat_ref, out_ref, s_ref, vt_ref):
-    seen = is_seen(role, doc_ref, kv_ref.shape[0])
+def next_kernel(role, seen_ref, q_ref, kv_ref, bias_ref, gt_ref, e_ref, stat_ref, out_ref, s_ref, vt_ref):
+    seen = is_seen(role, seen_ref)
 
     @pl.when(seen)
     def _():
@@ -163,13 +169,13 @@
 
 
 def rest_kernel(
-    doc_ref, q_ref, g_ref, mate_ref, side_ref, bias_ref, gt_ref, own_stat, line_stat, side_stat, side_e,
+    seen_ref, q_ref, g_ref, mate_ref, side_ref, bias_ref, gt_ref, own_stat, line_stat, side_stat, side_e,
     mate_o, mate_part, side_part, gq_part, scale_ref, delta_ref,
     s_ref, vt_ref, mate_e, mate_stat, kt_ref, p_ref, ds_ref,
 ):
     dim = mate_ref.shape[1] // 2
     heads = q_ref.shape[1] // dim
-    next_kernel(MATE, doc_ref, q_ref, mate_ref, bias_ref, gt_ref, mate_e, mate_stat, mate_o, s_ref, vt_ref)
+    next_kernel(MATE, seen_ref, q_ref, mate_ref, bias_ref, gt_ref, mate_e, mate_stat, mate_o, s_ref, vt_ref)
     stats = (own_stat, mate_stat, line_stat, side_stat)
     tops = [ref[:heads, :] for ref in stats]
     top = jnp.maximum(jnp.maximum(tops[0], tops[1]), jnp.maximum(tops[2], tops[3]))
@@ -179,7 +185,7 @@
         scale_ref[b] = parts[b] * inverse
     delta_ref[...] = sum(p * ref[2 * heads :, :] for p, ref in zip(parts, stats)) * inverse
     rows = mate_ref.shape[0]
-    seen = is_seen(MATE, doc_ref, rows)
+    seen = is_seen(MATE, seen_ref)
 
     @pl.when(seen)
     def _():
@@ -191,28 +197,28 @@
     def _():
         mate_part[...] = jnp.zeros(mate_part.shape, mate_part.dtype)
         next_backward(
-            is_seen(SIDE, doc_ref, rows), q_ref, g_ref, side_ref, side_e, scale_ref.at[SIDE], delta_ref, None,
+            is_seen(SIDE, seen_ref), q_ref, g_ref, side_ref, side_e, scale_ref.at[SIDE], delta_ref, None,
             side_part, gq_part, kt_ref, p_ref, ds_ref,
         )
 
 
-def line_kernel(doc_ref, q_ref, g_ref, kv_ref, e_ref, scale_ref, delta_ref, gq_in, part_ref, gq_ref, kt_ref, p_ref, ds_ref):
+def line_kernel(seen_ref, q_ref, g_ref, kv_ref, e_ref, scale_ref, delta_ref, gq_in, part_ref, gq_ref, kt_ref, p_ref, ds_ref):
     next_backward(
-        is_seen(LINE, doc_ref, kv_ref.shape[0]), q_ref, g_ref, kv_ref, e_ref, scale_ref.at[LINE], delta_ref, gq_in,
+        is_seen(LINE, seen_ref), q_ref, g_ref, kv_ref, e_ref, scale_ref.at[LINE], delta_ref, gq_in,
         part_ref, gq_ref, kt_ref, p_ref, ds_ref,
     )
 
 
 def side_kernel(
-    doc_ref, q_ref, g_ref, kv_ref, e_ref, scale_ref, delta_ref, gq_in, early_part, part_ref, gq_ref, kt_ref, p_ref, ds_ref
+    seen_ref, q_ref, g_ref, kv_ref, e_ref, scale_ref, delta_ref, gq_in, early_part, part_ref, gq_ref, kt_ref, p_ref, ds_ref
 ):
     rows = kv_ref.shape[0]
-    late = is_seen(MATE, doc_ref, rows)
+    late = is_seen(MATE, seen_ref)
 
     @pl.when(late)
     def _():
         next_backward(
-            is_seen(SIDE, doc_ref, rows), q_ref, g_ref, kv_ref, e_ref, scale_ref.at[SIDE], delta_ref, gq_in,
+            is_seen(SIDE, seen_ref), q_ref, g_ref, kv_ref, e_ref, scale_ref.at[SIDE], delta_ref, gq_in,
             part_ref, gq_ref, kt_ref, p_ref, ds_ref,
         )
 
@@ -322,9 +328,10 @@
     own = call("settle", settle_kernel, (own,), (pair_sent,), [], 1 << 33, (), (), {0: 0})[0]
     line = lax.ppermute(own, "ctx", to_line)
     q, g = queries, grad_out
-    own_e, own_stat, own_o, bias, gt, dp = call(
+    own_e, own_stat, own_o, bias, gt, dp, seen = call(
         "own_forward", own_kernel, (docs, q, g, own),
-        (e_shape, stat_shape, out_shape, shape((3, rows, rows), f32), shape((heads, dim, rows), bf16), shape((heads, rows, rows), f32)),
+        (e_shape, stat_shape, out_shape, shape((3, rows, rows), f32), shape((heads, dim, rows), bf16), shape((heads, rows, rows), f32),
+         shape((8, LANES), jnp.int32)),
         [pltpu.VMEM((rows, rows), f32), *ahead], work,
     )
     line, own_stat = lax.optimization_barrier((line, own_stat))
@@ -333,26 +340,26 @@
 
     def first(name, role, kv):
         return call(
-            name, lambda *refs: next_kernel(role, *refs), (docs, q, kv, bias, gt), (e_shape, stat_shape, out_shape), ahead, work
+            name, lambda *refs: next_kernel(role, *refs), (seen, q, kv, bias, gt), (e_shape, stat_shape, out_shape), ahead, work
         )
 
     line_e, line_stat, line_o = first("line_forward", LINE, line)
     side_e, side_stat, side_o = first("side_forward", SIDE, side)
     mate_o, mate_part, early_part, gq, scales, delta = call(
         "rest_forward", rest_kernel,
-        (docs, q, g, mate, side, bias, gt, own_stat, line_stat, side_stat, side_e),
+        (seen, q, g, mate, side, bias, gt, own_stat, line_stat, side_stat, side_e),
         (out_shape, pair_sent, pair_sent, out_shape, shape((4, heads, rows), f32), shape((heads, rows), f32)),
         [*ahead, buffer(e_shape), buffer(stat_shape), *back],
         work,
     )
     mate_back = lax.ppermute(mate_part, "ctx", to_mate)
     line_part, gq = call(
-        "line_backward", line_kernel, (docs, q, g, line, line_e, scales, delta, gq), (pair, out_shape), back, work
+        "line_backward", line_kernel, (seen, q, g, line, line_e, scales, delta, gq), (pair, out_shape), back, work
     )
     line_part = call("line_add", line_add_kernel, (line_part, mate_back), (pair_sent,), [], 0)[0]
     line_part, gq = lax.optimization_barrier((line_part, gq))
     side_part, gq = call(
-        "side_backward", side_kernel, (docs, q, g, side, side_e, scales, delta, gq, early_part), (pair_sent, out_shape), back, work
+        "side_backward", side_kernel, (seen, q, g, side, side_e, scales, delta, gq, early_part), (pair_sent, out_shape), back, work
     )
     side_far = lax.ppermute(side_part, "ctx", three_back(count))
     side_near = lax.ppermute(side_part, "ctx", to_mate)

time: 24.1 us -> 23.9 us (level)
  Pallas kernels: 8.38 us -> 7.75 us
  waiting for transfers between devices: 5.93 us -> 6.37 us
    pallas_call x12, Pallas kernels: 8.38 us -> 7.75 us  [call(): pl.pallas_call(kernel, name=name, out_shape=outs, in_specs=[far if i in f...]
  transfers between devices with their start and end apart: 7 -> 7, of which waited for: 4 -> 4; matrix products, arithmetic and copies ran while one was open for 0% -> 0% of each run, Pallas kernels for 21% -> 20%
where the time goes in v6:
time: 23.9 us; the launch traced here: 23.6 us
  starting transfers between devices  8.71 us (36%)
  Pallas kernels  7.75 us (32%)
  waiting for transfers between devices  6.37 us (27%)
  between operations  0.76 us (3%)
    pallas_call x12, Pallas kernels, call(): pl.pallas_call(kernel, name=name, out_shape=outs, in_specs=[far if i in f...  7.75 us
    ppermute x1, waiting for transfers between devices, body(): line = lax.ppermute(own, 'ctx', to_line)  2.63 us
    ppermute x1, starting transfers between devices, body(): side = lax.ppermute(own, 'ctx', to_side)  2.14 us
    ppermute x1, starting transfers between devices, body(): line = lax.ppermute(own, 'ctx', to_line)  2.12 us
    ppermute x1, starting transfers between devices, body(): mate = lax.ppermute(line, 'ctx', to_mate)  2 us
    ppermute x1, starting transfers between devices, body(): line_back = lax.ppermute(line_part, 'ctx', flip(to_line))  1.86 us
    ppermute x1, waiting for transfers between devices, body(): side_far = lax.ppermute(side_part, 'ctx', three_back(count))  1.75 us
    ppermute x1, waiting for transfers between devices, body(): mate_back = lax.ppermute(mate_part, 'ctx', to_mate)  1.2 us
  transfers between devices with their start and end apart: 7, of which 4 were waited for; matrix products, arithmetic and copies ran while one was open for 0% of the time, Pallas kernels for 20%

profile of v6, /device:TPU:1, one launch (start us, length us, event | category | flops | bytes accessed | tf_op | source)
XLA Modules:
  0.0 23.6 jit_solution(1299028927919078865)
XLA Ops:
  0.6 0.9 %pack.1.in_ref = bf16[256,256]{1,0:T(8,128)(2,1)S(1)} custom-call(bf16[256,128]{1,0:T(8,128)(2,1)} %k_ref.1, bf16[256,128]{1,0:T(8,128)(2,1)} %v_ref.1), custom_call_target="tpu_custom_call" | custom-call | tf_op jit(solution)/shard_map/pack/pallas_call | solution.py:285
  1.5 0.0 copy-start
  1.5 0.0 copy-start.1
  1.6 0.0 copy-start.2
  1.6 2.1 %collective-permute-start = (bf16[256,256]{1,0:T(8,128)(2,1)S(1)}, bf16[256,256]{1,0:T(8,128)(2,1)S(1)}, u32[]{:S(2)}, u32[]{:S(2)}) collective-permute-start(bf16[256,256]{1,0:T(8,128)(2,1)S(1)} %settle.1.kv_ref), channel_id=1, source_target_pairs={{0,4},{2,6},{4,8},{6,10},{8,12},{10,14},{12,16},{14,18},{16,20},{1... | collective-permute-start | bytes 393224 | tf_op jit(solution)/shard_map/ppermute | solution.py:329
  3.7 2.1 %collective-permute-start.2 = (bf16[256,256]{1,0:T(8,128)(2,1)S(1)}, bf16[256,256]{1,0:T(8,128)(2,1)S(1)}, u32[]{:S(2)}, u32[]{:S(2)}) collective-permute-start(bf16[256,256]{1,0:T(8,128)(2,1)S(1)} %settle.1.kv_ref), channel_id=1, source_target_pairs={{0,2},{2,8},{4,6},{6,12},{8,10},{10,16},{12,14},{14,20},{16,18},{1... | collective-permute-start | bytes 393224 | tf_op jit(solution)/shard_map/ppermute | solution.py:338
  5.8 0.0 copy-done
  5.8 0.0 copy-done.1
  5.8 0.0 copy-done.2
  5.8 1.5 %own_forward.1 = (bf16[8,256,256]{2,1,0:T(8,128)(2,1)S(1)}, f32[24,256]{1,0:T(8,128)S(1)}, f32[8,128,256]{2,1,0:T(8,128)S(1)}, f32[3,256,256]{2,1,0:T(8,128)S(1)...) custom-call(s32[32,128]{1,0:T(8,128)S(1)} %bitcast.1, ...), custom_call_target="tpu_custom_call" | custom-call | flops 2048 | tf_op jit(solution)/shard_map/own_forward/pallas_call | solution.py:285
  7.3 2.6 %collective-permute-done.refs_2_.kv_ref = bf16[256,256]{1,0:T(8,128)(2,1)S(1)} collective-permute-done((bf16[256,256]{1,0:T(8,128)(2,1)S(1)}, bf16[256,256]{1,0:T(8,128)(2,1)S(1)}, u32[]{:S(2)}, u32[]{:S(2)}) %collective-permute-start) | collective-permute-done | bytes 131104 | tf_op jit(solution)/shard_map/ppermute | solution.py:329
  10.0 2.0 %collective-permute-start.1 = (bf16[256,256]{1,0:T(8,128)(2,1)S(1)}, bf16[256,256]{1,0:T(8,128)(2,1)S(1)}, u32[]{:S(2)}, u32[]{:S(2)}) collective-permute-start(bf16[256,256]{1,0:T(8,128)(2,1)S(1)} %collective-permute-done.refs_2_.kv_ref), channel_id=1, source_target_pairs={{0,2},{2,0},{4,6},{6,4},{8,10},{10,8},{12,14},{14,12},{16,18},{18,... | collective-permute-start | bytes 393224 | tf_op jit(solution)/shard_map/ppermute | solution.py:339
  12.0 0.1 line_forward.1
  12.1 0.0 collective-permute-done.2.refs_2_.side_ref.kv_ref
  12.1 1.2 %side_forward.1 = (bf16[8,256,256]{2,1,0:T(8,128)(2,1)S(1)}, f32[24,256]{1,0:T(8,128)S(1)}, f32[8,128,256]{2,1,0:T(8,128)S(1)}) custom-call(s32[8,128]{1,0:T(8,128)S(1)} %get-tuple-element.37.refs_0_.seen_ref, bf16[256,1024]{1,0:T(8,128)(2,1)S(1)} %copy-done, bf16[256,256]{1,0:T(8,128)(2,1)S(1)} %collective-permute-done.2.refs_2_.side_ref.kv_ref, ...), custom_call_target="tpu_custom_call" | custom-call | flops 2048 | tf_op jit(solution)/shard_map/side_forward/pallas_call | solution.py:285
  13.3 0.0 collective-permute-done.1.mate_ref
  13.3 1.4 %rest_forward.1 = (f32[8,128,256]{2,1,0:T(8,128)S(1)}, bf16[256,256]{1,0:T(8,128)(2,1)S(1)}, bf16[256,256]{1,0:T(8,128)(2,1)S(1)}, f32[8,128,256]{2,1,0:T(8,128)...) custom-call(s32[8,128]{1,0:T(8,128)S(1)} %get-tuple-element.37.refs_0_.seen_ref, bf16[256,1024]{1,0:T(8,128)(2,1)S(1)} %copy-done, ...), custom_call_target="tpu_custom_call" | custom-call | flops 2048 | tf_op jit(solution)/shard_map/rest_forward/pallas_call | solution.py:285
  14.7 0.1 collective-permute-start.3
  14.8 0.1 line_backward.1
  14.9 1.2 %collective-permute-done.3.mate_ref = bf16[256,256]{1,0:T(8,128)(2,1)S(1)} collective-permute-done((bf16[256,256]{1,0:T(8,128)(2,1)S(1)}, bf16[256,256]{1,0:T(8,128)(2,1)S(1)}, u32[]{:S(2)}, u32[]{:S(2)}) %collective-permute-start.3) | collective-permute-done | bytes 131104 | tf_op jit(solution)/shard_map/ppermute | solution.py:355
  16.1 1.9 %collective-permute-start.4 = (bf16[256,256]{1,0:T(8,128)(2,1)S(1)}, bf16[256,256]{1,0:T(8,128)(2,1)S(1)}, u32[]{:S(2)}, u32[]{:S(2)}) collective-permute-start(bf16[256,256]{1,0:T(8,128)(2,1)S(1)} %line_add.1), channel_id=1, source_target_pairs={{4,0},{6,2},{8,4},{10,6},{12,8},{14,10},{16,12},{18,14},{20,16},{2... | collective-permute-start | bytes 393224 | tf_op jit(solution)/shard_map/ppermute | solution.py:366
  18.0 0.1 side_backward.1
  18.1 0.4 %collective-permute-start.6 = (bf16[256,256]{1,0:T(8,128)(2,1)S(1)}, bf16[256,256]{1,0:T(8,128)(2,1)S(1)}, u32[]{:S(2)}, u32[]{:S(2)}) collective-permute-start(bf16[256,256]{1,0:T(8,128)(2,1)S(1)} %get-tuple-element.65), channel_id=1, source_target_pairs={{8,2},{12,6},{16,10},{20,14},{24,18},{28,22},{6,12},{10,16},{14,20... | collective-permute-start | bytes 393224 | tf_op jit(solution)/shard_map/ppermute | solution.py:364
  18.6 0.1 collective-permute-start.5
  18.6 1.7 %own_backward.1 = (f32[256,256]{1,0:T(8,128)S(1)}, bf16[256,1024]{1,0:T(8,128)(2,1)}, bf16[256,1024]{1,0:T(8,128)(2,1)}) custom-call(bf16[256,1024]{1,0:T(8,128)(2,1)S(1)} %copy-done, bf16[256,1024]{1,0:T(8,128)(2,1)S(1)} %copy-done.1, bf16[256,256]{1,0:T(8,128)(2,1)S(1)} %settle.1.kv_ref, bf16[8,256,256]{2,1,0:T(8,128)(2,1)S(1)} %get-tuple-element.36.e_ref, ...), custom_call_target="tpu_custom_call" | custom-call | flops 2048 | tf_op jit(solution)/shard_map/own_backward/pallas_call | solution.py:285
  20.3 0.8 %collective-permute-done.4.line_ref = bf16[256,256]{1,0:T(8,128)(2,1)S(1)} collective-permute-done((bf16[256,256]{1,0:T(8,128)(2,1)S(1)}, bf16[256,256]{1,0:T(8,128)(2,1)S(1)}, u32[]{:S(2)}, u32[]{:S(2)}) %collective-permute-start.4) | collective-permute-done | bytes 131104 | tf_op jit(solution)/shard_map/ppermute | solution.py:366
  21.2 1.7 %collective-permute-done.6.far_ref = bf16[256,256]{1,0:T(8,128)(2,1)S(1)} collective-permute-done((bf16[256,256]{1,0:T(8,128)(2,1)S(1)}, bf16[256,256]{1,0:T(8,128)(2,1)S(1)}, u32[]{:S(2)}, u32[]{:S(2)}) %collective-permute-start.6) | collective-permute-done | bytes 131104 | tf_op jit(solution)/shard_map/ppermute | solution.py:364
  22.9 0.0 collective-permute-done.5.near_ref
  22.9 0.7 %side_sum.1 = (bf16[256,128]{1,0:T(8,128)(2,1)}, bf16[256,128]{1,0:T(8,128)(2,1)}) custom-call(f32[256,256]{1,0:T(8,128)S(1)} %line_sum.1.sum_ref, bf16[256,256]{1,0:T(8,128)(2,1)S(1)} %collective-permute-done.5.near_ref, bf16[256,256]{1,0:T(8,128)(2,1)S(1)} %collective-permute-done.6.far_ref), custom_call_target="tpu_custom_call" | custom-call | tf_op jit(solution)/shard_map/side_sum/pallas_call | solution.py:285
  (3 shorter events, 0.1 us)
Async XLA Ops:
  1.5 4.3 %copy-start = (bf16[256,1024]{1,0:T(8,128)(2,1)S(1)}, bf16[256,1024]{1,0:T(8,128)(2,1)}, u32[]{:S(2)}) copy-start(bf16[256,1024]{1,0:T(8,128)(2,1)} %q_ref.9) | copy-start | bytes 1572868
  1.5 4.3 %copy-start.1 = (bf16[256,1024]{1,0:T(8,128)(2,1)S(1)}, bf16[256,1024]{1,0:T(8,128)(2,1)}, u32[]{:S(2)}) copy-start(bf16[256,1024]{1,0:T(8,128)(2,1)} %g_ref.9) | copy-start | bytes 1572868
  1.6 4.3 %copy-start.2 = (s32[4096]{0:T(1024)S(1)}, s32[4096]{0:T(1024)}, u32[]{:S(2)}) copy-start(s32[4096]{0:T(1024)} %param.8) | copy-start | bytes 49156
  1.6 8.4 %collective-permute-start = (bf16[256,256]{1,0:T(8,128)(2,1)S(1)}, bf16[256,256]{1,0:T(8,128)(2,1)S(1)}, u32[]{:S(2)}, u32[]{:S(2)}) collective-permute-start(bf16[256,256]{1,0:T(8,128)(2,1)S(1)} %settle.1.kv_ref), channel_id=1, source_target_pairs={{0,4},{2,6},{4,8},{6,10},{8,12},{10,14},{12,16},{14,18},{16,20},{1... | collective-permute-start | bytes 393224 | tf_op jit(solution)/shard_map/ppermute | solution.py:329
  3.7 8.4 %collective-permute-start.2 = (bf16[256,256]{1,0:T(8,128)(2,1)S(1)}, bf16[256,256]{1,0:T(8,128)(2,1)S(1)}, u32[]{:S(2)}, u32[]{:S(2)}) collective-permute-start(bf16[256,256]{1,0:T(8,128)(2,1)S(1)} %settle.1.kv_ref), channel_id=1, source_target_pairs={{0,2},{2,8},{4,6},{6,12},{8,10},{10,16},{12,14},{14,20},{16,18},{1... | collective-permute-start | bytes 393224 | tf_op jit(solution)/shard_map/ppermute | solution.py:338
  10.0 3.3 %collective-permute-start.1 = (bf16[256,256]{1,0:T(8,128)(2,1)S(1)}, bf16[256,256]{1,0:T(8,128)(2,1)S(1)}, u32[]{:S(2)}, u32[]{:S(2)}) collective-permute-start(bf16[256,256]{1,0:T(8,128)(2,1)S(1)} %collective-permute-done.refs_2_.kv_ref), channel_id=1, source_target_pairs={{0,2},{2,0},{4,6},{6,4},{8,10},{10,8},{12,14},{14,12},{16,18},{18,... | collective-permute-start | bytes 393224 | tf_op jit(solution)/shard_map/ppermute | solution.py:339
  14.7 1.4 %collective-permute-start.3 = (bf16[256,256]{1,0:T(8,128)(2,1)S(1)}, bf16[256,256]{1,0:T(8,128)(2,1)S(1)}, u32[]{:S(2)}, u32[]{:S(2)}) collective-permute-start(bf16[256,256]{1,0:T(8,128)(2,1)S(1)} %get-tuple-element.51), channel_id=1, source_target_pairs={{0,2},{2,0},{4,6},{6,4},{8,10},{10,8},{12,14},{14,12},{16,18},{18,... | collective-permute-start | bytes 393224 | tf_op jit(solution)/shard_map/ppermute | solution.py:355
  16.1 5.0 %collective-permute-start.4 = (bf16[256,256]{1,0:T(8,128)(2,1)S(1)}, bf16[256,256]{1,0:T(8,128)(2,1)S(1)}, u32[]{:S(2)}, u32[]{:S(2)}) collective-permute-start(bf16[256,256]{1,0:T(8,128)(2,1)S(1)} %line_add.1), channel_id=1, source_target_pairs={{4,0},{6,2},{8,4},{10,6},{12,8},{14,10},{16,12},{18,14},{20,16},{2... | collective-permute-start | bytes 393224 | tf_op jit(solution)/shard_map/ppermute | solution.py:366
  18.1 4.8 %collective-permute-start.6 = (bf16[256,256]{1,0:T(8,128)(2,1)S(1)}, bf16[256,256]{1,0:T(8,128)(2,1)S(1)}, u32[]{:S(2)}, u32[]{:S(2)}) collective-permute-start(bf16[256,256]{1,0:T(8,128)(2,1)S(1)} %get-tuple-element.65), channel_id=1, source_target_pairs={{8,2},{12,6},{16,10},{20,14},{24,18},{28,22},{6,12},{10,16},{14,20... | collective-permute-start | bytes 393224 | tf_op jit(solution)/shard_map/ppermute | solution.py:364
  18.6 4.4 %collective-permute-start.5 = (bf16[256,256]{1,0:T(8,128)(2,1)S(1)}, bf16[256,256]{1,0:T(8,128)(2,1)S(1)}, u32[]{:S(2)}, u32[]{:S(2)}) collective-permute-start(bf16[256,256]{1,0:T(8,128)(2,1)S(1)} %get-tuple-element.65), channel_id=1, source_target_pairs={{0,2},{2,0},{4,6},{6,4},{8,10},{10,8},{12,14},{14,12},{16,18},{18,... | collective-permute-start | bytes 393224 | tf_op jit(solution)/shard_map/ppermute | solution.py:365

commit v7 on v6

--- a/solution.py
+++ b/solution.py
@@ -210,9 +210,9 @@
 
 
 def side_kernel(
-    seen_ref, q_ref, g_ref, kv_ref, e_ref, scale_ref, delta_ref, gq_in, early_part, part_ref, gq_ref, kt_ref, p_ref, ds_ref
+    seen_ref, q_ref, g_ref, kv_ref, e_ref, scale_ref, delta_ref, gq_in, early_part, line_part,
+    part_ref, near_ref, gq_ref, kt_ref, p_ref, ds_ref,
 ):
-    rows = kv_ref.shape[0]
     late = is_seen(MATE, seen_ref)
 
     @pl.when(late)
@@ -226,6 +226,9 @@
     def _():
         part_ref[...] = early_part[...]
         gq_ref[...] = gq_in[...]
+
+    joint = is_joint(lax.axis_index("ctx") // 2, lax.axis_size("ctx") // 2)
+    near_ref[...] = jnp.where(joint, line_part[...], part_ref[...])
 
 
 def turn(h, value, buf):
@@ -266,15 +269,24 @@
 
 
 def line_sum_kernel(own_ref, line_ref, out_ref):
-    out_ref[...] = own_ref[...] + line_ref[...].astype(jnp.float32)
-
-
-def side_sum_kernel(sum_ref, near_ref, far_ref, k_ref, v_ref):
+    chip, chips = lax.axis_index("ctx") // 2, lax.axis_size("ctx") // 2
+    in_ring = (chip < chips - 1) & (chip != chips - SECOND - 1)
+    out_ref[...] = own_ref[...] + jnp.where(in_ring, line_ref[...].astype(jnp.float32), 0.0)
+
+
+def far_sum_kernel(sum_ref, far_ref, out_ref):
     here, count = lax.axis_index("ctx"), lax.axis_size("ctx")
-    dim = k_ref.shape[1]
     even = lax.rem(here, 2) == 0
-    side = jnp.where(even, near_ref[...].astype(jnp.float32), far_ref[...].astype(jnp.float32))
-    total = sum_ref[...] + jnp.where(even | (here + 3 < count), side, 0.0)
+    taken = (even & is_joint(here // 2, count // 2)) | (jnp.logical_not(even) & (here + 3 < count))
+    out_ref[...] = sum_ref[...] + jnp.where(taken, far_ref[...].astype(jnp.float32), 0.0)
+
+
+def near_sum_kernel(sum_ref, near_ref, k_ref, v_ref):
+    here, count = lax.axis_index("ctx"), lax.axis_size("ctx")
+    chip, dim = here // 2, k_ref.shape[1]
+    even, joint = lax.rem(here, 2) == 0, is_joint(chip, count // 2)
+    taken = (chip == count // 2 - SECOND - 1) | (jnp.logical_not(joint) & even)
+    total = sum_ref[...] + jnp.where(taken, near_ref[...].astype(jnp.float32), 0.0)
     k_ref[...] = total[:, :dim].astype(jnp.bfloat16)
     v_ref[...] = total[:, dim:].astype(jnp.bfloat16)
 
@@ -295,10 +307,35 @@
     )(*args)
 
 
+SECOND = 3
+
+
+def line_rings(count):
+    to = {i: i - 2 for i in range(count)}
+    first = count - 2 * SECOND
+    to.update({core: first - 2 + core for core in (0, 1)})
+    to.update({first + core: count - 2 + core for core in (0, 1)})
+    return list(to.items())
+
+
+def is_joint(chip, chips):
+    return (chip == chips - SECOND - 1) | (chip == chips - SECOND)
+
+
+def near_swaps(count):
+    to = {i: i ^ 1 for i in range(count)}
+    first = count - 2 * SECOND
+    for i in (first - 2, first - 1):
+        to[i], to[i + 2] = i + 2, i
+    return list(to.items())
+
+
 def three_back(count):
     to = {i: i - 3 for i in range(4, count, 2)}
     to.update({i: i + 3 for i in range(3, count - 3, 2)})
     to.update({0: 2, 1: 0, 2: 4, count - 3: count - 1, count - 1: count - 3})
+    i = count - 2 * SECOND - 1
+    to.update({i: i - 1, i + 2: i + 1, i - 4: i + 3, i - 2: i + 5})
     return list(to.items())
 
 
@@ -309,7 +346,6 @@
     to_mate = [(i, i ^ 1) for i in range(count)]
     to_line = [(i, (i + 2) % count) for i in range(count)]
     to_side = [(i, (i + 1 + 2 * (i % 2)) % count) for i in range(count)]
-    flip = lambda pairs: [(b, a) for a, b in pairs]
     f32, bf16 = jnp.float32, jnp.bfloat16
     shape = jax.ShapeDtypeStruct
     e_shape, stat_shape, out_shape = shape((heads, rows, rows), bf16), shape((3 * heads, rows), f32), shape((heads, dim, rows), f32)
@@ -358,19 +394,21 @@
     )
     line_part = call("line_add", line_add_kernel, (line_part, mate_back), (pair_sent,), [], 0)[0]
     line_part, gq = lax.optimization_barrier((line_part, gq))
-    side_part, gq = call(
-        "side_backward", side_kernel, (seen, q, g, side, side_e, scales, delta, gq, early_part), (pair_sent, out_shape), back, work
+    side_part, near_part, gq = call(
+        "side_backward", side_kernel, (seen, q, g, side, side_e, scales, delta, gq, early_part, line_part),
+        (pair_sent, pair_sent, out_shape), back, work,
     )
     side_far = lax.ppermute(side_part, "ctx", three_back(count))
-    side_near = lax.ppermute(side_part, "ctx", to_mate)
-    line_back = lax.ppermute(line_part, "ctx", flip(to_line))
+    side_near = lax.ppermute(near_part, "ctx", near_swaps(count))
+    line_back = lax.ppermute(line_part, "ctx", line_rings(count))
     own_part, grad_query, attended = call(
         "own_backward", last_kernel, (q, g, own, own_e, scales, delta, gq, dp, own_o, mate_o, line_o, side_o), (pair, wide, wide),
         [*back, buffer(wide), buffer(wide), pltpu.SemaphoreType.DMA((2,))], work, (), (1, 2),
     )
     total = call("line_sum", line_sum_kernel, (own_part, line_back), (pair,), [], work)[0]
     narrow = shape((rows, dim), bf16)
-    grad_key, grad_value = call("side_sum", side_sum_kernel, (total, side_near, side_far), (narrow, narrow), [], 0)
+    total = call("far_sum", far_sum_kernel, (total, side_far), (pair,), [], work)[0]
+    grad_key, grad_value = call("near_sum", near_sum_kernel, (total, side_near), (narrow, narrow), [], 0)
     return attended, grad_query, grad_key, grad_value
 
 

time: 23.9 us -> 24 us (level)
  starting transfers between devices: 8.71 us -> 9.14 us
    ppermute x2, waiting for transfers between devices: 0.79 us -> 0.33 us  [the longest x1 0.33 us: body(): line_back = lax.ppermute(line_part, 'ctx', line_rings(count))]
    ppermute x1, waiting for transfers between devices: 1.75 us -> 2.02 us  [body(): side_far = lax.ppermute(side_part, 'ctx', three_back(count))]
    ppermute x1, starting transfers between devices: 0.45 us -> 0.7 us  [body(): side_far = lax.ppermute(side_part, 'ctx', three_back(count))]
    pallas_call x12 -> x13, Pallas kernels: 7.75 us -> 7.83 us  [call(): pl.pallas_call(kernel, name=name, out_shape=outs, in_specs=[far if i in f...]
where the time goes in v7:
time: 24 us; the launch traced here: 23.9 us
  starting transfers between devices  9.14 us (38%)
  Pallas kernels  7.83 us (33%)
  waiting for transfers between devices  6.18 us (26%)
  between operations  0.78 us (3%)
    pallas_call x13, Pallas kernels, call(): pl.pallas_call(kernel, name=name, out_shape=outs, in_specs=[far if i in f...  7.83 us
    ppermute x1, waiting for transfers between devices, body(): line = lax.ppermute(own, 'ctx', to_line)  2.63 us
    ppermute x1, starting transfers between devices, body(): side = lax.ppermute(own, 'ctx', to_side)  2.14 us
    ppermute x1, starting transfers between devices, body(): line = lax.ppermute(own, 'ctx', to_line)  2.12 us
    ppermute x1, starting transfers between devices, body(): line_back = lax.ppermute(line_part, 'ctx', line_rings(count))  2.03 us
    ppermute x1, waiting for transfers between devices, body(): side_far = lax.ppermute(side_part, 'ctx', three_back(count))  2.02 us
    ppermute x1, starting transfers between devices, body(): mate = lax.ppermute(line, 'ctx', to_mate)  2 us
    ppermute x1, waiting for transfers between devices, body(): mate_back = lax.ppermute(mate_part, 'ctx', to_mate)  1.2 us
  transfers between devices with their start and end apart: 7, of which 4 were waited for; matrix products, arithmetic and copies ran while one was open for 0% of the time, Pallas kernels for 20%

profile of v7, /device:TPU:1, one launch (start us, length us, event | category | flops | bytes accessed | tf_op | source)
XLA Modules:
  0.0 23.9 jit_solution(10692787750447597445)
XLA Ops:
  0.6 0.9 %pack.1.in_ref = bf16[256,256]{1,0:T(8,128)(2,1)S(1)} custom-call(bf16[256,128]{1,0:T(8,128)(2,1)} %k_ref.1, bf16[256,128]{1,0:T(8,128)(2,1)} %v_ref.1), custom_call_target="tpu_custom_call" | custom-call | tf_op jit(solution)/shard_map/pack/pallas_call | solution.py:297
  1.5 0.0 copy-start
  1.5 0.0 copy-start.1
  1.6 0.0 copy-start.2
  1.6 2.1 %collective-permute-start = (bf16[256,256]{1,0:T(8,128)(2,1)S(1)}, bf16[256,256]{1,0:T(8,128)(2,1)S(1)}, u32[]{:S(2)}, u32[]{:S(2)}) collective-permute-start(bf16[256,256]{1,0:T(8,128)(2,1)S(1)} %settle.1.kv_ref), channel_id=1, source_target_pairs={{0,4},{2,6},{4,8},{6,10},{8,12},{10,14},{12,16},{14,18},{16,20},{1... | collective-permute-start | bytes 393224 | tf_op jit(solution)/shard_map/ppermute | solution.py:365
  3.7 2.1 %collective-permute-start.2 = (bf16[256,256]{1,0:T(8,128)(2,1)S(1)}, bf16[256,256]{1,0:T(8,128)(2,1)S(1)}, u32[]{:S(2)}, u32[]{:S(2)}) collective-permute-start(bf16[256,256]{1,0:T(8,128)(2,1)S(1)} %settle.1.kv_ref), channel_id=1, source_target_pairs={{0,2},{2,8},{4,6},{6,12},{8,10},{10,16},{12,14},{14,20},{16,18},{1... | collective-permute-start | bytes 393224 | tf_op jit(solution)/shard_map/ppermute | solution.py:374
  5.8 0.0 copy-done
  5.8 0.0 copy-done.1
  5.8 0.0 copy-done.2
  5.8 1.5 %own_forward.1 = (bf16[8,256,256]{2,1,0:T(8,128)(2,1)S(1)}, f32[24,256]{1,0:T(8,128)S(1)}, f32[8,128,256]{2,1,0:T(8,128)S(1)}, f32[3,256,256]{2,1,0:T(8,128)S(1)...) custom-call(s32[32,128]{1,0:T(8,128)S(1)} %bitcast.1, ...), custom_call_target="tpu_custom_call" | custom-call | flops 2048 | tf_op jit(solution)/shard_map/own_forward/pallas_call | solution.py:297
  7.3 2.6 %collective-permute-done.refs_2_.kv_ref = bf16[256,256]{1,0:T(8,128)(2,1)S(1)} collective-permute-done((bf16[256,256]{1,0:T(8,128)(2,1)S(1)}, bf16[256,256]{1,0:T(8,128)(2,1)S(1)}, u32[]{:S(2)}, u32[]{:S(2)}) %collective-permute-start) | collective-permute-done | bytes 131104 | tf_op jit(solution)/shard_map/ppermute | solution.py:365
  10.0 2.0 %collective-permute-start.1 = (bf16[256,256]{1,0:T(8,128)(2,1)S(1)}, bf16[256,256]{1,0:T(8,128)(2,1)S(1)}, u32[]{:S(2)}, u32[]{:S(2)}) collective-permute-start(bf16[256,256]{1,0:T(8,128)(2,1)S(1)} %collective-permute-done.refs_2_.kv_ref), channel_id=1, source_target_pairs={{0,2},{2,0},{4,6},{6,4},{8,10},{10,8},{12,14},{14,12},{16,18},{18,... | collective-permute-start | bytes 393224 | tf_op jit(solution)/shard_map/ppermute | solution.py:375
  12.0 0.1 line_forward.1
  12.1 0.0 collective-permute-done.2.refs_2_.side_ref.kv_ref
  12.1 1.2 %side_forward.1 = (bf16[8,256,256]{2,1,0:T(8,128)(2,1)S(1)}, f32[24,256]{1,0:T(8,128)S(1)}, f32[8,128,256]{2,1,0:T(8,128)S(1)}) custom-call(s32[8,128]{1,0:T(8,128)S(1)} %get-tuple-element.38.refs_0_.seen_ref, bf16[256,1024]{1,0:T(8,128)(2,1)S(1)} %copy-done, bf16[256,256]{1,0:T(8,128)(2,1)S(1)} %collective-permute-done.2.refs_2_.side_ref.kv_ref, ...), custom_call_target="tpu_custom_call" | custom-call | flops 2048 | tf_op jit(solution)/shard_map/side_forward/pallas_call | solution.py:297
  13.3 0.0 collective-permute-done.1.mate_ref
  13.3 1.4 %rest_forward.1 = (f32[8,128,256]{2,1,0:T(8,128)S(1)}, bf16[256,256]{1,0:T(8,128)(2,1)S(1)}, bf16[256,256]{1,0:T(8,128)(2,1)S(1)}, f32[8,128,256]{2,1,0:T(8,128)...) custom-call(s32[8,128]{1,0:T(8,128)S(1)} %get-tuple-element.38.refs_0_.seen_ref, bf16[256,1024]{1,0:T(8,128)(2,1)S(1)} %copy-done, ...), custom_call_target="tpu_custom_call" | custom-call | flops 2048 | tf_op jit(solution)/shard_map/rest_forward/pallas_call | solution.py:297
  14.7 0.1 collective-permute-start.3
  14.8 0.1 line_backward.1
  14.9 1.2 %collective-permute-done.3.mate_ref = bf16[256,256]{1,0:T(8,128)(2,1)S(1)} collective-permute-done((bf16[256,256]{1,0:T(8,128)(2,1)S(1)}, bf16[256,256]{1,0:T(8,128)(2,1)S(1)}, u32[]{:S(2)}, u32[]{:S(2)}) %collective-permute-start.3) | collective-permute-done | bytes 131104 | tf_op jit(solution)/shard_map/ppermute | solution.py:391
  16.1 2.0 %collective-permute-start.4 = (bf16[256,256]{1,0:T(8,128)(2,1)S(1)}, bf16[256,256]{1,0:T(8,128)(2,1)S(1)}, u32[]{:S(2)}, u32[]{:S(2)}) collective-permute-start(bf16[256,256]{1,0:T(8,128)(2,1)S(1)} %line_add.1.line_part), channel_id=1, source_target_pairs={{0,16},{2,18},{4,0},{6,2},{8,4},{10,6},{12,8},{14,10},{16,12},{18,... | collective-permute-start | bytes 393224 | tf_op jit(solution)/shard_map/ppermute | solution.py:403
  18.2 0.1 side_backward.1
  18.3 0.7 %collective-permute-start.5 = (bf16[256,256]{1,0:T(8,128)(2,1)S(1)}, bf16[256,256]{1,0:T(8,128)(2,1)S(1)}, u32[]{:S(2)}, u32[]{:S(2)}) collective-permute-start(bf16[256,256]{1,0:T(8,128)(2,1)S(1)} %get-tuple-element.66), channel_id=1, source_target_pairs={{8,2},{12,6},{16,10},{20,14},{24,18},{28,22},{6,12},{10,24},{14,28... | collective-permute-start | bytes 393224 | tf_op jit(solution)/shard_map/ppermute | solution.py:401
  19.0 0.1 collective-permute-start.6
  19.1 1.7 %own_backward.1 = (f32[256,256]{1,0:T(8,128)S(1)}, bf16[256,1024]{1,0:T(8,128)(2,1)}, bf16[256,1024]{1,0:T(8,128)(2,1)}) custom-call(bf16[256,1024]{1,0:T(8,128)(2,1)S(1)} %copy-done, bf16[256,1024]{1,0:T(8,128)(2,1)S(1)} %copy-done.1, bf16[256,256]{1,0:T(8,128)(2,1)S(1)} %settle.1.kv_ref, bf16[8,256,256]{2,1,0:T(8,128)(2,1)S(1)} %get-tuple-element.37.e_ref, ...), custom_call_target="tpu_custom_call" | custom-call | flops 2048 | tf_op jit(solution)/shard_map/own_backward/pallas_call | solution.py:297
  20.8 0.3 %collective-permute-done.4.line_ref = bf16[256,256]{1,0:T(8,128)(2,1)S(1)} collective-permute-done((bf16[256,256]{1,0:T(8,128)(2,1)S(1)}, bf16[256,256]{1,0:T(8,128)(2,1)S(1)}, u32[]{:S(2)}, u32[]{:S(2)}) %collective-permute-start.4) | collective-permute-done | bytes 131104 | tf_op jit(solution)/shard_map/ppermute | solution.py:403
  21.2 2.0 %collective-permute-done.5.far_ref = bf16[256,256]{1,0:T(8,128)(2,1)S(1)} collective-permute-done((bf16[256,256]{1,0:T(8,128)(2,1)S(1)}, bf16[256,256]{1,0:T(8,128)(2,1)S(1)}, u32[]{:S(2)}, u32[]{:S(2)}) %collective-permute-start.5) | collective-permute-done | bytes 131104 | tf_op jit(solution)/shard_map/ppermute | solution.py:401
  23.2 0.0 collective-permute-done.6.near_ref
  23.2 0.7 %near_sum.1 = (bf16[256,128]{1,0:T(8,128)(2,1)}, bf16[256,128]{1,0:T(8,128)(2,1)}) custom-call(f32[256,256]{1,0:T(8,128)S(1)} %far_sum.1.sum_ref, bf16[256,256]{1,0:T(8,128)(2,1)S(1)} %collective-permute-done.6.near_ref), custom_call_target="tpu_custom_call" | custom-call | tf_op jit(solution)/shard_map/near_sum/pallas_call | solution.py:297
  (4 shorter events, 0.1 us)
Async XLA Ops:
  1.5 4.3 %copy-start = (bf16[256,1024]{1,0:T(8,128)(2,1)S(1)}, bf16[256,1024]{1,0:T(8,128)(2,1)}, u32[]{:S(2)}) copy-start(bf16[256,1024]{1,0:T(8,128)(2,1)} %q_ref.9) | copy-start | bytes 1572868
  1.5 4.3 %copy-start.1 = (bf16[256,1024]{1,0:T(8,128)(2,1)S(1)}, bf16[256,1024]{1,0:T(8,128)(2,1)}, u32[]{:S(2)}) copy-start(bf16[256,1024]{1,0:T(8,128)(2,1)} %g_ref.9) | copy-start | bytes 1572868
  1.6 4.3 %copy-start.2 = (s32[4096]{0:T(1024)S(1)}, s32[4096]{0:T(1024)}, u32[]{:S(2)}) copy-start(s32[4096]{0:T(1024)} %param.8) | copy-start | bytes 49156
  1.6 8.4 %collective-permute-start = (bf16[256,256]{1,0:T(8,128)(2,1)S(1)}, bf16[256,256]{1,0:T(8,128)(2,1)S(1)}, u32[]{:S(2)}, u32[]{:S(2)}) collective-permute-start(bf16[256,256]{1,0:T(8,128)(2,1)S(1)} %settle.1.kv_ref), channel_id=1, source_target_pairs={{0,4},{2,6},{4,8},{6,10},{8,12},{10,14},{12,16},{14,18},{16,20},{1... | collective-permute-start | bytes 393224 | tf_op jit(solution)/shard_map/ppermute | solution.py:365
  3.7 8.4 %collective-permute-start.2 = (bf16[256,256]{1,0:T(8,128)(2,1)S(1)}, bf16[256,256]{1,0:T(8,128)(2,1)S(1)}, u32[]{:S(2)}, u32[]{:S(2)}) collective-permute-start(bf16[256,256]{1,0:T(8,128)(2,1)S(1)} %settle.1.kv_ref), channel_id=1, source_target_pairs={{0,2},{2,8},{4,6},{6,12},{8,10},{10,16},{12,14},{14,20},{16,18},{1... | collective-permute-start | bytes 393224 | tf_op jit(solution)/shard_map/ppermute | solution.py:374
  10.0 3.3 %collective-permute-start.1 = (bf16[256,256]{1,0:T(8,128)(2,1)S(1)}, bf16[256,256]{1,0:T(8,128)(2,1)S(1)}, u32[]{:S(2)}, u32[]{:S(2)}) collective-permute-start(bf16[256,256]{1,0:T(8,128)(2,1)S(1)} %collective-permute-done.refs_2_.kv_ref), channel_id=1, source_target_pairs={{0,2},{2,0},{4,6},{6,4},{8,10},{10,8},{12,14},{14,12},{16,18},{18,... | collective-permute-start | bytes 393224 | tf_op jit(solution)/shard_map/ppermute | solution.py:375
  14.7 1.4 %collective-permute-start.3 = (bf16[256,256]{1,0:T(8,128)(2,1)S(1)}, bf16[256,256]{1,0:T(8,128)(2,1)S(1)}, u32[]{:S(2)}, u32[]{:S(2)}) collective-permute-start(bf16[256,256]{1,0:T(8,128)(2,1)S(1)} %get-tuple-element.52), channel_id=1, source_target_pairs={{0,2},{2,0},{4,6},{6,4},{8,10},{10,8},{12,14},{14,12},{16,18},{18,... | collective-permute-start | bytes 393224 | tf_op jit(solution)/shard_map/ppermute | solution.py:391
  16.1 5.0 %collective-permute-start.4 = (bf16[256,256]{1,0:T(8,128)(2,1)S(1)}, bf16[256,256]{1,0:T(8,128)(2,1)S(1)}, u32[]{:S(2)}, u32[]{:S(2)}) collective-permute-start(bf16[256,256]{1,0:T(8,128)(2,1)S(1)} %line_add.1.line_part), channel_id=1, source_target_pairs={{0,16},{2,18},{4,0},{6,2},{8,4},{10,6},{12,8},{14,10},{16,12},{18,... | collective-permute-start | bytes 393224 | tf_op jit(solution)/shard_map/ppermute | solution.py:403
  18.3 4.9 %collective-permute-start.5 = (bf16[256,256]{1,0:T(8,128)(2,1)S(1)}, bf16[256,256]{1,0:T(8,128)(2,1)S(1)}, u32[]{:S(2)}, u32[]{:S(2)}) collective-permute-start(bf16[256,256]{1,0:T(8,128)(2,1)S(1)} %get-tuple-element.66), channel_id=1, source_target_pairs={{8,2},{12,6},{16,10},{20,14},{24,18},{28,22},{6,12},{10,24},{14,28... | collective-permute-start | bytes 393224 | tf_op jit(solution)/shard_map/ppermute | solution.py:401
  19.0 4.2 %collective-permute-start.6 = (bf16[256,256]{1,0:T(8,128)(2,1)S(1)}, bf16[256,256]{1,0:T(8,128)(2,1)S(1)}, u32[]{:S(2)}, u32[]{:S(2)}) collective-permute-start(bf16[256,256]{1,0:T(8,128)(2,1)S(1)} %get-tuple-element.67), channel_id=1, source_target_pairs={{0,2},{2,0},{4,6},{6,4},{8,10},{10,8},{12,14},{14,12},{16,20},{18,... | collective-permute-start | bytes 393224 | tf_op jit(solution)/shard_map/ppermute | solution.py:402

commit v8 on v6

--- a/solution.py
+++ b/solution.py
@@ -30,9 +30,16 @@
 
 def find_seen(role, doc_ref, rows):
     mine, at, valid = place(role, rows)
+    steps = rows // LANES
     first = jnp.min(doc_ref[pl.ds(mine, 1), :].astype(jnp.float32))
-    last = jnp.max(doc_ref[pl.ds(at + rows // LANES - 1, 1), :].astype(jnp.float32))
-    return valid & (first == last)
+    last = jnp.max(doc_ref[pl.ds(at + steps - 1, 1), :].astype(jnp.float32))
+    middle = jnp.max(doc_ref[pl.ds(at + steps // 2 - 1, 1), :].astype(jnp.float32))
+    level = (last == first).astype(jnp.int32) + (middle == first).astype(jnp.int32)
+    return jnp.where(valid, level, 0)
+
+
+def seen_level(role, seen_ref):
+    return seen_ref[role : role + 1, :][0, 0]
 
 
 def is_seen(role, seen_ref):
@@ -54,22 +61,23 @@
         bias[i * LANES : (i + 1) * LANES, :] = jnp.where(same, 0.0, MASKED)
 
 
-def forward(q_ref, kv_ref, bias, gt_ref, e_ref, stat_ref, out_ref, s_ref, vt_ref):
+def forward(q_ref, kv_ref, bias, gt_ref, e_ref, stat_ref, out_ref, s_ref, vt_ref, start=0):
     dim = kv_ref.shape[1] // 2
     heads = q_ref.shape[1] // dim
     factor = dim**-0.5 * LOG2_E
-    vt_ref[...] = jnp.transpose(kv_ref[:, dim:])
-    for h in range(heads):
-        s_ref[h] = nt(kv_ref[:, :dim], q_ref[:, h * dim : (h + 1) * dim])
-    for h in range(heads):
-        s = s_ref[h] * factor + bias[...]
+    keys = slice(start, kv_ref.shape[0])
+    vt_ref[:, keys] = jnp.transpose(kv_ref[keys, dim:])
+    for h in range(heads):
+        s_ref[h, keys, :] = nt(kv_ref[keys, :dim], q_ref[:, h * dim : (h + 1) * dim])
+    for h in range(heads):
+        s = s_ref[h, keys, :] * factor + bias[keys, :]
         top = jnp.max(s, axis=0, keepdims=True)
         e = jnp.exp2(s - top)
-        e_ref[h] = e.astype(jnp.bfloat16)
+        e_ref[h, keys, :] = e.astype(jnp.bfloat16)
         stat_ref[h : h + 1, :] = top
         stat_ref[heads + h : heads + h + 1, :] = jnp.sum(e, axis=0, keepdims=True)
     for h in range(heads):
-        out = nn(vt_ref[...], e_ref[h])
+        out = nn(vt_ref[:, keys], e_ref[h, keys, :])
         out_ref[h] = out
         stat_ref[2 * heads + h : 2 * heads + h + 1, :] = jnp.sum(out * gt_ref[h].astype(jnp.float32), axis=0, keepdims=True)
 
@@ -81,26 +89,30 @@
     out_ref[...] = jnp.zeros(out_ref.shape, out_ref.dtype)
 
 
-def backward_queries(g_ref, kv_ref, e_ref, scale_ref, delta_ref, gq_out, kt_ref, p_ref, ds_ref, dp=None):
+def backward_queries(g_ref, kv_ref, e_ref, scale_ref, delta_ref, gq_out, kt_ref, p_ref, ds_ref, dp=None, start=0):
     dim = kv_ref.shape[1] // 2
     heads = g_ref.shape[1] // dim
-    kt_ref[...] = jnp.transpose(kv_ref[:, :dim])
-    for h in range(heads):
-        probs = e_ref[h] * scale_ref[h : h + 1, :].astype(jnp.bfloat16)
-        p_ref[h] = probs
-        grad_p = nt(kv_ref[:, dim:], g_ref[:, h * dim : (h + 1) * dim]) if dp is None else dp[h]
-        ds_ref[h] = probs * (grad_p - delta_ref[h : h + 1, :]).astype(jnp.bfloat16)
-    for h in range(heads):
-        gq_out(h, nn(kt_ref[...], ds_ref[h]))
-
-
-def backward_keys(q_ref, g_ref, p_ref, ds_ref, part_ref):
-    dim = part_ref.shape[1] // 2
+    keys = slice(start, kv_ref.shape[0])
+    kt_ref[:, keys] = jnp.transpose(kv_ref[keys, :dim])
+    for h in range(heads):
+        probs = e_ref[h, keys, :] * scale_ref[h : h + 1, :].astype(jnp.bfloat16)
+        p_ref[h, keys, :] = probs
+        grad_p = nt(kv_ref[keys, dim:], g_ref[:, h * dim : (h + 1) * dim]) if dp is None else dp[h]
+        ds_ref[h, keys, :] = probs * (grad_p - delta_ref[h : h + 1, :]).astype(jnp.bfloat16)
+    for h in range(heads):
+        gq_out(h, nn(kt_ref[:, keys], ds_ref[h, keys, :]))
+
+
+def backward_keys(q_ref, g_ref, p_ref, ds_ref, part_ref, start=0):
+    rows, dim = part_ref.shape[0], part_ref.shape[1] // 2
+    keys = slice(start, rows)
     cols = [slice(h * dim, (h + 1) * dim) for h in range(q_ref.shape[1] // dim)]
-    grad_v = sum(nn(p_ref[h], g_ref[:, c]) for h, c in enumerate(cols))
-    part_ref[:, dim:] = grad_v.astype(part_ref.dtype)
-    grad_k = sum(nn(ds_ref[h], q_ref[:, c]) for h, c in enumerate(cols))
-    part_ref[:, :dim] = (grad_k * dim**-0.5).astype(part_ref.dtype)
+    if start:
+        part_ref[:start, :] = jnp.zeros((start, 2 * dim), part_ref.dtype)
+    grad_v = sum(nn(p_ref[h, keys, :], g_ref[:, c]) for h, c in enumerate(cols))
+    part_ref[keys, dim:] = grad_v.astype(part_ref.dtype)
+    grad_k = sum(nn(ds_ref[h, keys, :], q_ref[:, c]) for h, c in enumerate(cols))
+    part_ref[keys, :dim] = (grad_k * dim**-0.5).astype(part_ref.dtype)
 
 
 def backward_unseen(part_ref, gq_in, gq_ref):
@@ -132,38 +144,37 @@
     forward(q_ref, kv_ref, bias, gt_ref, e_ref, stat_ref, out_ref, s_ref, vt_ref)
     for role in (MATE, LINE, SIDE):
         mask_bias(role, doc_ref, bias_ref.at[role - 1])
-        seen = find_seen(role, doc_ref, kv_ref.shape[0]).astype(jnp.int32)
+        seen = find_seen(role, doc_ref, kv_ref.shape[0])
         seen_ref[role : role + 1, :] = jnp.full((1, LANES), seen, jnp.int32)
     for h in range(heads):
         dp_ref[h] = nt(kv_ref[:, dim:], g_ref[:, h * dim : (h + 1) * dim])
 
 
 def next_kernel(role, seen_ref, q_ref, kv_ref, bias_ref, gt_ref, e_ref, stat_ref, out_ref, s_ref, vt_ref):
-    seen = is_seen(role, seen_ref)
-
-    @pl.when(seen)
-    def _():
-        forward(q_ref, kv_ref, bias_ref.at[role - 1], gt_ref, e_ref, stat_ref, out_ref, s_ref, vt_ref)
-
-    @pl.when(jnp.logical_not(seen))
+    level = seen_level(role, seen_ref)
+    for some, start in ((2, 0), (1, kv_ref.shape[0] // 2)):
+
+        @pl.when(level == some)
+        def _():
+            forward(q_ref, kv_ref, bias_ref.at[role - 1], gt_ref, e_ref, stat_ref, out_ref, s_ref, vt_ref, start)
+
+    @pl.when(level == 0)
     def _():
         forward_unseen(stat_ref, out_ref)
 
 
-def next_backward(seen, q_ref, g_ref, kv_ref, e_ref, scale_ref, delta_ref, gq_in, part_ref, gq_ref, kt_ref, p_ref, ds_ref):
-    def run():
-        def put(h, value):
-            gq_ref[h] = value if gq_in is None else gq_in[h] + value
-
-        backward_queries(g_ref, kv_ref, e_ref, scale_ref, delta_ref, put, kt_ref, p_ref, ds_ref)
-        backward_keys(q_ref, g_ref, p_ref, ds_ref, part_ref)
-
-    if seen is True:
-        run()
-        return
-    pl.when(seen)(run)
-
-    @pl.when(jnp.logical_not(seen))
+def next_backward(level, q_ref, g_ref, kv_ref, e_ref, scale_ref, delta_ref, gq_in, part_ref, gq_ref, kt_ref, p_ref, ds_ref):
+    def put(h, value):
+        gq_ref[h] = value if gq_in is None else gq_in[h] + value
+
+    for some, start in ((2, 0), (1, kv_ref.shape[0] // 2)):
+
+        @pl.when(level == some)
+        def _():
+            backward_queries(g_ref, kv_ref, e_ref, scale_ref, delta_ref, put, kt_ref, p_ref, ds_ref, None, start)
+            backward_keys(q_ref, g_ref, p_ref, ds_ref, part_ref, start)
+
+    @pl.when(level == 0)
     def _():
         backward_unseen(part_ref, gq_in, gq_ref)
 
@@ -190,21 +201,21 @@
     @pl.when(seen)
     def _():
         next_backward(
-            True, q_ref, g_ref, mate_ref, mate_e, scale_ref.at[MATE], delta_ref, None, mate_part, gq_part, kt_ref, p_ref, ds_ref
+            seen_level(MATE, seen_ref), q_ref, g_ref, mate_ref, mate_e, scale_ref.at[MATE], delta_ref, None, mate_part, gq_part, kt_ref, p_ref, ds_ref
         )
 
     @pl.when(jnp.logical_not(seen))
     def _():
         mate_part[...] = jnp.zeros(mate_part.shape, mate_part.dtype)
         next_backward(
-            is_seen(SIDE, seen_ref), q_ref, g_ref, side_ref, side_e, scale_ref.at[SIDE], delta_ref, None,
+            seen_level(SIDE, seen_ref), q_ref, g_ref, side_ref, side_e, scale_ref.at[SIDE], delta_ref, None,
             side_part, gq_part, kt_ref, p_ref, ds_ref,
         )
 
 
 def line_kernel(seen_ref, q_ref, g_ref, kv_ref, e_ref, scale_ref, delta_ref, gq_in, part_ref, gq_ref, kt_ref, p_ref, ds_ref):
     next_backward(
-        is_seen(LINE, seen_ref), q_ref, g_ref, kv_ref, e_ref, scale_ref.at[LINE], delta_ref, gq_in,
+        seen_level(LINE, seen_ref), q_ref, g_ref, kv_ref, e_ref, scale_ref.at[LINE], delta_ref, gq_in,
         part_ref, gq_ref, kt_ref, p_ref, ds_ref,
     )
 
@@ -218,7 +229,7 @@
     @pl.when(late)
     def _():
         next_backward(
-            is_seen(SIDE, seen_ref), q_ref, g_ref, kv_ref, e_ref, scale_ref.at[SIDE], delta_ref, gq_in,
+            seen_level(SIDE, seen_ref), q_ref, g_ref, kv_ref, e_ref, scale_ref.at[SIDE], delta_ref, gq_in,
             part_ref, gq_ref, kt_ref, p_ref, ds_ref,
         )
 

time: 23.9 us -> 23.7 us (level)
    ppermute x1, starting transfers between devices: 1.86 us -> 1.56 us  [body(): line_back = lax.ppermute(line_part, 'ctx', flip(to_line))]
    ppermute x1, starting transfers between devices: 0.45 us -> 0.73 us  [body(): side_far = lax.ppermute(side_part, 'ctx', three_back(count))]
  transfers between devices with their start and end apart: 7 -> 7, of which waited for: 4 -> 4; matrix products, arithmetic and copies ran while one was open for 0% -> 0% of each run, Pallas kernels for 20% -> 21%
where the time goes in v8:
time: 23.7 us; the launch traced here: 23.6 us
  starting transfers between devices  8.69 us (37%)
  Pallas kernels  7.95 us (34%)
  waiting for transfers between devices  6.19 us (26%)
  between operations  0.76 us (3%)
    pallas_call x12, Pallas kernels, call(): pl.pallas_call(kernel, name=name, out_shape=outs, in_specs=[far if i in f...  7.95 us
    ppermute x1, waiting for transfers between devices, body(): line = lax.ppermute(own, 'ctx', to_line)  2.61 us
    ppermute x1, starting transfers between devices, body(): side = lax.ppermute(own, 'ctx', to_side)  2.14 us
    ppermute x1, starting transfers between devices, body(): line = lax.ppermute(own, 'ctx', to_line)  2.12 us
    ppermute x1, starting transfers between devices, body(): mate = lax.ppermute(line, 'ctx', to_mate)  2 us
    ppermute x1, waiting for transfers between devices, body(): side_far = lax.ppermute(side_part, 'ctx', three_back(count))  1.76 us
    ppermute x1, starting transfers between devices, body(): line_back = lax.ppermute(line_part, 'ctx', flip(to_line))  1.56 us
    ppermute x1, waiting for transfers between devices, body(): mate_back = lax.ppermute(mate_part, 'ctx', to_mate)  1.01 us
  transfers between devices with their start and end apart: 7, of which 4 were waited for; matrix products, arithmetic and copies ran while one was open for 0% of the time, Pallas kernels for 21%

profile of v8, /device:TPU:1, one launch (start us, length us, event | category | flops | bytes accessed | tf_op | source)
XLA Modules:
  0.0 23.6 jit_solution(8246928097266365611)
XLA Ops:
  0.6 0.9 %pack.1.in_ref = bf16[256,256]{1,0:T(8,128)(2,1)S(1)} custom-call(bf16[256,128]{1,0:T(8,128)(2,1)} %k_ref.1, bf16[256,128]{1,0:T(8,128)(2,1)} %v_ref.1), custom_call_target="tpu_custom_call" | custom-call | tf_op jit(solution)/shard_map/pack/pallas_call | solution.py:296
  1.5 0.0 copy-start
  1.5 0.0 copy-start.1
  1.6 0.0 copy-start.2
  1.6 2.1 %collective-permute-start = (bf16[256,256]{1,0:T(8,128)(2,1)S(1)}, bf16[256,256]{1,0:T(8,128)(2,1)S(1)}, u32[]{:S(2)}, u32[]{:S(2)}) collective-permute-start(bf16[256,256]{1,0:T(8,128)(2,1)S(1)} %settle.1.kv_ref), channel_id=1, source_target_pairs={{0,4},{2,6},{4,8},{6,10},{8,12},{10,14},{12,16},{14,18},{16,20},{1... | collective-permute-start | bytes 393224 | tf_op jit(solution)/shard_map/ppermute | solution.py:340
  3.7 2.1 %collective-permute-start.2 = (bf16[256,256]{1,0:T(8,128)(2,1)S(1)}, bf16[256,256]{1,0:T(8,128)(2,1)S(1)}, u32[]{:S(2)}, u32[]{:S(2)}) collective-permute-start(bf16[256,256]{1,0:T(8,128)(2,1)S(1)} %settle.1.kv_ref), channel_id=1, source_target_pairs={{0,2},{2,8},{4,6},{6,12},{8,10},{10,16},{12,14},{14,20},{16,18},{1... | collective-permute-start | bytes 393224 | tf_op jit(solution)/shard_map/ppermute | solution.py:349
  5.8 0.0 copy-done
  5.8 0.0 copy-done.1
  5.8 0.0 copy-done.2
  5.8 1.5 %own_forward.1 = (bf16[8,256,256]{2,1,0:T(8,128)(2,1)S(1)}, f32[24,256]{1,0:T(8,128)S(1)}, f32[8,128,256]{2,1,0:T(8,128)S(1)}, f32[3,256,256]{2,1,0:T(8,128)S(1)...) custom-call(s32[32,128]{1,0:T(8,128)S(1)} %bitcast.1, ...), custom_call_target="tpu_custom_call" | custom-call | flops 2048 | tf_op jit(solution)/shard_map/own_forward/pallas_call | solution.py:296
  7.3 2.6 %collective-permute-done.refs_2_.kv_ref = bf16[256,256]{1,0:T(8,128)(2,1)S(1)} collective-permute-done((bf16[256,256]{1,0:T(8,128)(2,1)S(1)}, bf16[256,256]{1,0:T(8,128)(2,1)S(1)}, u32[]{:S(2)}, u32[]{:S(2)}) %collective-permute-start) | collective-permute-done | bytes 131104 | tf_op jit(solution)/shard_map/ppermute | solution.py:340
  10.0 2.0 %collective-permute-start.1 = (bf16[256,256]{1,0:T(8,128)(2,1)S(1)}, bf16[256,256]{1,0:T(8,128)(2,1)S(1)}, u32[]{:S(2)}, u32[]{:S(2)}) collective-permute-start(bf16[256,256]{1,0:T(8,128)(2,1)S(1)} %collective-permute-done.refs_2_.kv_ref), channel_id=1, source_target_pairs={{0,2},{2,0},{4,6},{6,4},{8,10},{10,8},{12,14},{14,12},{16,18},{18,... | collective-permute-start | bytes 393224 | tf_op jit(solution)/shard_map/ppermute | solution.py:350
  12.0 0.1 line_forward.1
  12.1 0.0 collective-permute-done.2.refs_2_.side_ref.kv_ref
  12.1 1.1 %side_forward.1 = (bf16[8,256,256]{2,1,0:T(8,128)(2,1)S(1)}, f32[24,256]{1,0:T(8,128)S(1)}, f32[8,128,256]{2,1,0:T(8,128)S(1)}) custom-call(s32[8,128]{1,0:T(8,128)S(1)} %get-tuple-element.37.refs_0_.seen_ref, bf16[256,1024]{1,0:T(8,128)(2,1)S(1)} %copy-done, bf16[256,256]{1,0:T(8,128)(2,1)S(1)} %collective-permute-done.2.refs_2_.side_ref.kv_ref, ...), custom_call_target="tpu_custom_call" | custom-call | flops 2048 | tf_op jit(solution)/shard_map/side_forward/pallas_call | solution.py:296
  13.2 0.0 collective-permute-done.1.mate_ref
  13.3 1.4 %rest_forward.1 = (f32[8,128,256]{2,1,0:T(8,128)S(1)}, bf16[256,256]{1,0:T(8,128)(2,1)S(1)}, bf16[256,256]{1,0:T(8,128)(2,1)S(1)}, f32[8,128,256]{2,1,0:T(8,128)...) custom-call(s32[8,128]{1,0:T(8,128)S(1)} %get-tuple-element.37.refs_0_.seen_ref, bf16[256,1024]{1,0:T(8,128)(2,1)S(1)} %copy-done, ...), custom_call_target="tpu_custom_call" | custom-call | flops 2048 | tf_op jit(solution)/shard_map/rest_forward/pallas_call | solution.py:296
  14.7 0.1 collective-permute-start.3
  14.8 0.3 %line_backward.1 = (f32[256,256]{1,0:T(8,128)S(1)}, f32[8,128,256]{2,1,0:T(8,128)S(1)}) custom-call(s32[8,128]{1,0:T(8,128)S(1)} %get-tuple-element.37.refs_0_.seen_ref, bf16[256,1024]{1,0:T(8,128)(2,1)S(1)} %copy-done, bf16[256,1024]{1,0:T(8,128)(2,1)S(1)} %copy-done.1, bf16[256,256]{1,0:T(8,128)(2,1)S(1)} %collective-permute-done.refs_2_.kv_ref, ...), custom_call_target="tpu_custom_call" | custom-call | flops 2048 | tf_op jit(solution)/shard_map/line_backward/pallas_call | solution.py:296
  15.1 1.0 %collective-permute-done.3.mate_ref = bf16[256,256]{1,0:T(8,128)(2,1)S(1)} collective-permute-done((bf16[256,256]{1,0:T(8,128)(2,1)S(1)}, bf16[256,256]{1,0:T(8,128)(2,1)S(1)}, u32[]{:S(2)}, u32[]{:S(2)}) %collective-permute-start.3) | collective-permute-done | bytes 131104 | tf_op jit(solution)/shard_map/ppermute | solution.py:366
  16.1 1.6 %collective-permute-start.4 = (bf16[256,256]{1,0:T(8,128)(2,1)S(1)}, bf16[256,256]{1,0:T(8,128)(2,1)S(1)}, u32[]{:S(2)}, u32[]{:S(2)}) collective-permute-start(bf16[256,256]{1,0:T(8,128)(2,1)S(1)} %line_add.1), channel_id=1, source_target_pairs={{4,0},{6,2},{8,4},{10,6},{12,8},{14,10},{16,12},{18,14},{20,16},{2... | collective-permute-start | bytes 393224 | tf_op jit(solution)/shard_map/ppermute | solution.py:377
  17.7 0.1 side_backward.1
  17.8 0.7 %collective-permute-start.6 = (bf16[256,256]{1,0:T(8,128)(2,1)S(1)}, bf16[256,256]{1,0:T(8,128)(2,1)S(1)}, u32[]{:S(2)}, u32[]{:S(2)}) collective-permute-start(bf16[256,256]{1,0:T(8,128)(2,1)S(1)} %get-tuple-element.65), channel_id=1, source_target_pairs={{8,2},{12,6},{16,10},{20,14},{24,18},{28,22},{6,12},{10,16},{14,20... | collective-permute-start | bytes 393224 | tf_op jit(solution)/shard_map/ppermute | solution.py:375
  18.5 0.1 collective-permute-start.5
  18.6 1.7 %own_backward.1 = (f32[256,256]{1,0:T(8,128)S(1)}, bf16[256,1024]{1,0:T(8,128)(2,1)}, bf16[256,1024]{1,0:T(8,128)(2,1)}) custom-call(bf16[256,1024]{1,0:T(8,128)(2,1)S(1)} %copy-done, bf16[256,1024]{1,0:T(8,128)(2,1)S(1)} %copy-done.1, bf16[256,256]{1,0:T(8,128)(2,1)S(1)} %settle.1.kv_ref, bf16[8,256,256]{2,1,0:T(8,128)(2,1)S(1)} %get-tuple-element.36.e_ref, ...), custom_call_target="tpu_custom_call" | custom-call | flops 2048 | tf_op jit(solution)/shard_map/own_backward/pallas_call | solution.py:296
  20.3 0.8 %collective-permute-done.4.line_ref = bf16[256,256]{1,0:T(8,128)(2,1)S(1)} collective-permute-done((bf16[256,256]{1,0:T(8,128)(2,1)S(1)}, bf16[256,256]{1,0:T(8,128)(2,1)S(1)}, u32[]{:S(2)}, u32[]{:S(2)}) %collective-permute-start.4) | collective-permute-done | bytes 131104 | tf_op jit(solution)/shard_map/ppermute | solution.py:377
  21.2 1.8 %collective-permute-done.6.far_ref = bf16[256,256]{1,0:T(8,128)(2,1)S(1)} collective-permute-done((bf16[256,256]{1,0:T(8,128)(2,1)S(1)}, bf16[256,256]{1,0:T(8,128)(2,1)S(1)}, u32[]{:S(2)}, u32[]{:S(2)}) %collective-permute-start.6) | collective-permute-done | bytes 131104 | tf_op jit(solution)/shard_map/ppermute | solution.py:375
  22.9 0.0 collective-permute-done.5.near_ref
  22.9 0.7 %side_sum.1 = (bf16[256,128]{1,0:T(8,128)(2,1)}, bf16[256,128]{1,0:T(8,128)(2,1)}) custom-call(f32[256,256]{1,0:T(8,128)S(1)} %line_sum.1.sum_ref, bf16[256,256]{1,0:T(8,128)(2,1)S(1)} %collective-permute-done.5.near_ref, bf16[256,256]{1,0:T(8,128)(2,1)S(1)} %collective-permute-done.6.far_ref), custom_call_target="tpu_custom_call" | custom-call | tf_op jit(solution)/shard_map/side_sum/pallas_call | solution.py:296
  (3 shorter events, 0.1 us)
Async XLA Ops:
  1.5 4.3 %copy-start = (bf16[256,1024]{1,0:T(8,128)(2,1)S(1)}, bf16[256,1024]{1,0:T(8,128)(2,1)}, u32[]{:S(2)}) copy-start(bf16[256,1024]{1,0:T(8,128)(2,1)} %q_ref.9) | copy-start | bytes 1572868
  1.5 4.3 %copy-start.1 = (bf16[256,1024]{1,0:T(8,128)(2,1)S(1)}, bf16[256,1024]{1,0:T(8,128)(2,1)}, u32[]{:S(2)}) copy-start(bf16[256,1024]{1,0:T(8,128)(2,1)} %g_ref.9) | copy-start | bytes 1572868
  1.6 4.3 %copy-start.2 = (s32[4096]{0:T(1024)S(1)}, s32[4096]{0:T(1024)}, u32[]{:S(2)}) copy-start(s32[4096]{0:T(1024)} %param.8) | copy-start | bytes 49156
  1.6 8.4 %collective-permute-start = (bf16[256,256]{1,0:T(8,128)(2,1)S(1)}, bf16[256,256]{1,0:T(8,128)(2,1)S(1)}, u32[]{:S(2)}, u32[]{:S(2)}) collective-permute-start(bf16[256,256]{1,0:T(8,128)(2,1)S(1)} %settle.1.kv_ref), channel_id=1, source_target_pairs={{0,4},{2,6},{4,8},{6,10},{8,12},{10,14},{12,16},{14,18},{16,20},{1... | collective-permute-start | bytes 393224 | tf_op jit(solution)/shard_map/ppermute | solution.py:340
  3.7 8.4 %collective-permute-start.2 = (bf16[256,256]{1,0:T(8,128)(2,1)S(1)}, bf16[256,256]{1,0:T(8,128)(2,1)S(1)}, u32[]{:S(2)}, u32[]{:S(2)}) collective-permute-start(bf16[256,256]{1,0:T(8,128)(2,1)S(1)} %settle.1.kv_ref), channel_id=1, source_target_pairs={{0,2},{2,8},{4,6},{6,12},{8,10},{10,16},{12,14},{14,20},{16,18},{1... | collective-permute-start | bytes 393224 | tf_op jit(solution)/shard_map/ppermute | solution.py:349
  10.0 3.3 %collective-permute-start.1 = (bf16[256,256]{1,0:T(8,128)(2,1)S(1)}, bf16[256,256]{1,0:T(8,128)(2,1)S(1)}, u32[]{:S(2)}, u32[]{:S(2)}) collective-permute-start(bf16[256,256]{1,0:T(8,128)(2,1)S(1)} %collective-permute-done.refs_2_.kv_ref), channel_id=1, source_target_pairs={{0,2},{2,0},{4,6},{6,4},{8,10},{10,8},{12,14},{14,12},{16,18},{18,... | collective-permute-start | bytes 393224 | tf_op jit(solution)/shard_map/ppermute | solution.py:350
  14.7 1.4 %collective-permute-start.3 = (bf16[256,256]{1,0:T(8,128)(2,1)S(1)}, bf16[256,256]{1,0:T(8,128)(2,1)S(1)}, u32[]{:S(2)}, u32[]{:S(2)}) collective-permute-start(bf16[256,256]{1,0:T(8,128)(2,1)S(1)} %get-tuple-element.51), channel_id=1, source_target_pairs={{0,2},{2,0},{4,6},{6,4},{8,10},{10,8},{12,14},{14,12},{16,18},{18,... | collective-permute-start | bytes 393224 | tf_op jit(solution)/shard_map/ppermute | solution.py:366
  16.1 5.0 %collective-permute-start.4 = (bf16[256,256]{1,0:T(8,128)(2,1)S(1)}, bf16[256,256]{1,0:T(8,128)(2,1)S(1)}, u32[]{:S(2)}, u32[]{:S(2)}) collective-permute-start(bf16[256,256]{1,0:T(8,128)(2,1)S(1)} %line_add.1), channel_id=1, source_target_pairs={{4,0},{6,2},{8,4},{10,6},{12,8},{14,10},{16,12},{18,14},{20,16},{2... | collective-permute-start | bytes 393224 | tf_op jit(solution)/shard_map/ppermute | solution.py:377
  17.8 5.1 %collective-permute-start.6 = (bf16[256,256]{1,0:T(8,128)(2,1)S(1)}, bf16[256,256]{1,0:T(8,128)(2,1)S(1)}, u32[]{:S(2)}, u32[]{:S(2)}) collective-permute-start(bf16[256,256]{1,0:T(8,128)(2,1)S(1)} %get-tuple-element.65), channel_id=1, source_target_pairs={{8,2},{12,6},{16,10},{20,14},{24,18},{28,22},{6,12},{10,16},{14,20... | collective-permute-start | bytes 393224 | tf_op jit(solution)/shard_map/ppermute | solution.py:375
  18.5 4.4 %collective-permute-start.5 = (bf16[256,256]{1,0:T(8,128)(2,1)S(1)}, bf16[256,256]{1,0:T(8,128)(2,1)S(1)}, u32[]{:S(2)}, u32[]{:S(2)}) collective-permute-start(bf16[256,256]{1,0:T(8,128)(2,1)S(1)} %get-tuple-element.65), channel_id=1, source_target_pairs={{0,2},{2,0},{4,6},{6,4},{8,10},{10,8},{12,14},{14,12},{16,18},{18,... | collective-permute-start | bytes 393224 | tf_op jit(solution)/shard_map/ppermute | solution.py:376

commit v9 on v8

--- a/solution.py
+++ b/solution.py
@@ -82,11 +82,10 @@
         stat_ref[2 * heads + h : 2 * heads + h + 1, :] = jnp.sum(out * gt_ref[h].astype(jnp.float32), axis=0, keepdims=True)
 
 
-def forward_unseen(stat_ref, out_ref):
-    heads = out_ref.shape[0]
+def forward_unseen(stat_ref):
+    heads = stat_ref.shape[0] // 3
     stat_ref[:heads, :] = jnp.full((heads, stat_ref.shape[1]), MASKED, jnp.float32)
     stat_ref[heads:, :] = jnp.zeros((2 * heads, stat_ref.shape[1]), jnp.float32)
-    out_ref[...] = jnp.zeros(out_ref.shape, out_ref.dtype)
 
 
 def backward_queries(g_ref, kv_ref, e_ref, scale_ref, delta_ref, gq_out, kt_ref, p_ref, ds_ref, dp=None, start=0):
@@ -131,10 +130,6 @@
         copy.wait()
 
 
-def settle_kernel(in_ref, out_ref):
-    out_ref[:16, :] = in_ref[:16, :]
-
-
 def own_kernel(doc_ref, q_ref, g_ref, kv_ref, e_ref, stat_ref, out_ref, bias_ref, gt_ref, dp_ref, seen_ref, bias, s_ref, vt_ref):
     dim = kv_ref.shape[1] // 2
     heads = q_ref.shape[1] // dim
@@ -160,7 +155,7 @@
 
     @pl.when(level == 0)
     def _():
-        forward_unseen(stat_ref, out_ref)
+        forward_unseen(stat_ref)
 
 
 def next_backward(level, q_ref, g_ref, kv_ref, e_ref, scale_ref, delta_ref, gq_in, part_ref, gq_ref, kt_ref, p_ref, ds_ref):
@@ -244,12 +239,16 @@
 
 
 def last_kernel(
-    q_ref, g_ref, kv_ref, e_ref, scale_ref, delta_ref, gq_in, dp_ref, own_o, mate_o, line_o, side_o, part_ref, gq_ref, att_ref,
+    seen_ref, q_ref, g_ref, kv_ref, e_ref, scale_ref, delta_ref, gq_in, dp_ref, own_o, mate_o, line_o, side_o,
+    part_ref, gq_ref, att_ref,
     kt_ref, p_ref, ds_ref, buf, att_buf, sems,
 ):
     factor = (kv_ref.shape[1] // 2) ** -0.5
+    seen = [is_seen(role, seen_ref) for role in (MATE, LINE, SIDE)]
     for h in range(own_o.shape[0]):
-        out = sum(ref[h] * scale_ref[b, h : h + 1, :] for b, ref in enumerate((own_o, mate_o, line_o, side_o)))
+        out = own_o[h] * scale_ref[OWN, h : h + 1, :]
+        for taken, b, ref in zip(seen, (MATE, LINE, SIDE), (mate_o, line_o, side_o)):
+            out = out + jnp.where(taken, ref[h] * scale_ref[b, h : h + 1, :], 0.0)
         turn(h, out, att_buf)
     att_copy = pltpu.make_async_copy(att_buf, att_ref, sems.at[0])
     gq_copy = pltpu.make_async_copy(buf, gq_ref, sems.at[1])
@@ -334,9 +333,8 @@
 
     docs = doc_ids.reshape(-1, LANES)
     own = call(
-        "pack", pack_kernel, (key_vectors, value_vectors), (pair_sent,), [pltpu.SemaphoreType.DMA((2,))], 0, (0, 1)
+        "pack", pack_kernel, (key_vectors, value_vectors), (pair_sent,), [pltpu.SemaphoreType.DMA((2,))], 1 << 33, (0, 1)
     )[0]
-    own = call("settle", settle_kernel, (own,), (pair_sent,), [], 1 << 33, (), (), {0: 0})[0]
     line = lax.ppermute(own, "ctx", to_line)
     q, g = queries, grad_out
     own_e, own_stat, own_o, bias, gt, dp, seen = call(
@@ -376,7 +374,7 @@
     side_near = lax.ppermute(side_part, "ctx", to_mate)
     line_back = lax.ppermute(line_part, "ctx", flip(to_line))
     own_part, grad_query, attended = call(
-        "own_backward", last_kernel, (q, g, own, own_e, scales, delta, gq, dp, own_o, mate_o, line_o, side_o), (pair, wide, wide),
+        "own_backward", last_kernel, (seen, q, g, own, own_e, scales, delta, gq, dp, own_o, mate_o, line_o, side_o), (pair, wide, wide),
         [*back, buffer(wide), buffer(wide), pltpu.SemaphoreType.DMA((2,))], work, (), (1, 2),
     )
     total = call("line_sum", line_sum_kernel, (own_part, line_back), (pair,), [], work)[0]

time: 23.7 us -> 23.8 us (level)
    pallas_call x12 -> x11, Pallas kernels: 7.95 us -> 8.02 us  [call(): pl.pallas_call(kernel, name=name, out_shape=outs, in_specs=[far if i in f...]
where the time goes in v9:
time: 23.8 us; the launch traced here: 23.6 us
  starting transfers between devices  8.76 us (37%)
  Pallas kernels  8.02 us (34%)
  waiting for transfers between devices  6.07 us (26%)
  between operations  0.76 us (3%)
    pallas_call x11, Pallas kernels, call(): pl.pallas_call(kernel, name=name, out_shape=outs, in_specs=[far if i in f...  8.02 us
    ppermute x1, waiting for transfers between devices, body(): line = lax.ppermute(own, 'ctx', to_line)  2.59 us
    ppermute x1, starting transfers between devices, body(): side = lax.ppermute(own, 'ctx', to_side)  2.14 us
    ppermute x1, starting transfers between devices, body(): line = lax.ppermute(own, 'ctx', to_line)  2.12 us
    ppermute x1, starting transfers between devices, body(): mate = lax.ppermute(line, 'ctx', to_mate)  2 us
    ppermute x1, waiting for transfers between devices, body(): side_far = lax.ppermute(side_part, 'ctx', three_back(count))  1.82 us
    ppermute x1, starting transfers between devices, body(): line_back = lax.ppermute(line_part, 'ctx', flip(to_line))  1.62 us
    ppermute x1, waiting for transfers between devices, body(): mate_back = lax.ppermute(mate_part, 'ctx', to_mate)  1.01 us
  transfers between devices with their start and end apart: 7, of which 4 were waited for; matrix products, arithmetic and copies ran while one was open for 0% of the time, Pallas kernels for 21%

profile of v9, /device:TPU:1, one launch (start us, length us, event | category | flops | bytes accessed | tf_op | source)
XLA Modules:
  0.0 23.6 jit_solution(12803936894998150937)
XLA Ops:
  0.6 0.0 copy-start
  0.6 0.0 copy-start.1
  0.7 0.0 copy-start.2
  0.7 1.0 %pack.1.kv_ref = bf16[256,256]{1,0:T(8,128)(2,1)S(1)} custom-call(bf16[256,128]{1,0:T(8,128)(2,1)} %k_ref.1, bf16[256,128]{1,0:T(8,128)(2,1)} %v_ref.1), custom_call_target="tpu_custom_call" | custom-call | flops 8589934592 | tf_op jit(solution)/shard_map/pack/pallas_call | solution.py:295
  1.6 2.1 %collective-permute-start = (bf16[256,256]{1,0:T(8,128)(2,1)S(1)}, bf16[256,256]{1,0:T(8,128)(2,1)S(1)}, u32[]{:S(2)}, u32[]{:S(2)}) collective-permute-start(bf16[256,256]{1,0:T(8,128)(2,1)S(1)} %pack.1.kv_ref), channel_id=1, source_target_pairs={{0,4},{2,6},{4,8},{6,10},{8,12},{10,14},{12,16},{14,18},{16,20},{1... | collective-permute-start | bytes 393224 | tf_op jit(solution)/shard_map/ppermute | solution.py:338
  3.8 2.1 %collective-permute-start.2 = (bf16[256,256]{1,0:T(8,128)(2,1)S(1)}, bf16[256,256]{1,0:T(8,128)(2,1)S(1)}, u32[]{:S(2)}, u32[]{:S(2)}) collective-permute-start(bf16[256,256]{1,0:T(8,128)(2,1)S(1)} %pack.1.kv_ref), channel_id=1, source_target_pairs={{0,2},{2,8},{4,6},{6,12},{8,10},{10,16},{12,14},{14,20},{16,18},{1... | collective-permute-start | bytes 393224 | tf_op jit(solution)/shard_map/ppermute | solution.py:347
  5.9 0.0 copy-done
  5.9 0.0 copy-done.1
  5.9 0.0 copy-done.2
  5.9 1.5 %own_forward.1 = (bf16[8,256,256]{2,1,0:T(8,128)(2,1)S(1)}, f32[24,256]{1,0:T(8,128)S(1)}, f32[8,128,256]{2,1,0:T(8,128)S(1)}, f32[3,256,256]{2,1,0:T(8,128)S(1)...) custom-call(s32[32,128]{1,0:T(8,128)S(1)} %bitcast.1, ...), custom_call_target="tpu_custom_call" | custom-call | flops 2048 | tf_op jit(solution)/shard_map/own_forward/pallas_call | solution.py:295
  7.4 2.6 %collective-permute-done.refs_2_.kv_ref = bf16[256,256]{1,0:T(8,128)(2,1)S(1)} collective-permute-done((bf16[256,256]{1,0:T(8,128)(2,1)S(1)}, bf16[256,256]{1,0:T(8,128)(2,1)S(1)}, u32[]{:S(2)}, u32[]{:S(2)}) %collective-permute-start) | collective-permute-done | bytes 131104 | tf_op jit(solution)/shard_map/ppermute | solution.py:338
  10.0 2.0 %collective-permute-start.1 = (bf16[256,256]{1,0:T(8,128)(2,1)S(1)}, bf16[256,256]{1,0:T(8,128)(2,1)S(1)}, u32[]{:S(2)}, u32[]{:S(2)}) collective-permute-start(bf16[256,256]{1,0:T(8,128)(2,1)S(1)} %collective-permute-done.refs_2_.kv_ref), channel_id=1, source_target_pairs={{0,2},{2,0},{4,6},{6,4},{8,10},{10,8},{12,14},{14,12},{16,18},{18,... | collective-permute-start | bytes 393224 | tf_op jit(solution)/shard_map/ppermute | solution.py:348
  12.1 0.0 collective-permute-done.2.refs_2_.side_ref.kv_ref
  12.1 1.1 %side_forward.1 = (bf16[8,256,256]{2,1,0:T(8,128)(2,1)S(1)}, f32[24,256]{1,0:T(8,128)S(1)}, f32[8,128,256]{2,1,0:T(8,128)S(1)}) custom-call(s32[8,128]{1,0:T(8,128)S(1)} %get-tuple-element.36.refs_0_.seen_ref, bf16[256,1024]{1,0:T(8,128)(2,1)S(1)} %copy-done, bf16[256,256]{1,0:T(8,128)(2,1)S(1)} %collective-permute-done.2.refs_2_.side_ref.kv_ref, ...), custom_call_target="tpu_custom_call" | custom-call | flops 2048 | tf_op jit(solution)/shard_map/side_forward/pallas_call | solution.py:295
  13.2 0.0 collective-permute-done.1.mate_ref
  13.3 1.3 %rest_forward.1 = (f32[8,128,256]{2,1,0:T(8,128)S(1)}, bf16[256,256]{1,0:T(8,128)(2,1)S(1)}, bf16[256,256]{1,0:T(8,128)(2,1)S(1)}, f32[8,128,256]{2,1,0:T(8,128)...) custom-call(s32[8,128]{1,0:T(8,128)S(1)} %get-tuple-element.36.refs_0_.seen_ref, bf16[256,1024]{1,0:T(8,128)(2,1)S(1)} %copy-done, ...), custom_call_target="tpu_custom_call" | custom-call | flops 2048 | tf_op jit(solution)/shard_map/rest_forward/pallas_call | solution.py:295
  14.6 0.1 collective-permute-start.3
  14.7 0.3 %line_backward.1 = (f32[256,256]{1,0:T(8,128)S(1)}, f32[8,128,256]{2,1,0:T(8,128)S(1)}) custom-call(s32[8,128]{1,0:T(8,128)S(1)} %get-tuple-element.36.refs_0_.seen_ref, bf16[256,1024]{1,0:T(8,128)(2,1)S(1)} %copy-done, bf16[256,1024]{1,0:T(8,128)(2,1)S(1)} %copy-done.1, bf16[256,256]{1,0:T(8,128)(2,1)S(1)} %collective-permute-done.refs_2_.kv_ref, ...), custom_call_target="tpu_custom_call" | custom-call | flops 2048 | tf_op jit(solution)/shard_map/line_backward/pallas_call | solution.py:295
  15.0 1.0 %collective-permute-done.3.mate_ref = bf16[256,256]{1,0:T(8,128)(2,1)S(1)} collective-permute-done((bf16[256,256]{1,0:T(8,128)(2,1)S(1)}, bf16[256,256]{1,0:T(8,128)(2,1)S(1)}, u32[]{:S(2)}, u32[]{:S(2)}) %collective-permute-start.3) | collective-permute-done | bytes 131104 | tf_op jit(solution)/shard_map/ppermute | solution.py:364
  16.1 1.6 %collective-permute-start.4 = (bf16[256,256]{1,0:T(8,128)(2,1)S(1)}, bf16[256,256]{1,0:T(8,128)(2,1)S(1)}, u32[]{:S(2)}, u32[]{:S(2)}) collective-permute-start(bf16[256,256]{1,0:T(8,128)(2,1)S(1)} %line_add.1), channel_id=1, source_target_pairs={{4,0},{6,2},{8,4},{10,6},{12,8},{14,10},{16,12},{18,14},{20,16},{2... | collective-permute-start | bytes 393224 | tf_op jit(solution)/shard_map/ppermute | solution.py:375
  17.7 0.1 side_backward.1
  17.8 0.7 %collective-permute-start.6 = (bf16[256,256]{1,0:T(8,128)(2,1)S(1)}, bf16[256,256]{1,0:T(8,128)(2,1)S(1)}, u32[]{:S(2)}, u32[]{:S(2)}) collective-permute-start(bf16[256,256]{1,0:T(8,128)(2,1)S(1)} %get-tuple-element.65), channel_id=1, source_target_pairs={{8,2},{12,6},{16,10},{20,14},{24,18},{28,22},{6,12},{10,16},{14,20... | collective-permute-start | bytes 393224 | tf_op jit(solution)/shard_map/ppermute | solution.py:373
  18.5 0.1 collective-permute-start.5
  18.6 1.8 %own_backward.1 = (f32[256,256]{1,0:T(8,128)S(1)}, bf16[256,1024]{1,0:T(8,128)(2,1)}, bf16[256,1024]{1,0:T(8,128)(2,1)}) custom-call(s32[8,128]{1,0:T(8,128)S(1)} %get-tuple-element.36.refs_0_.seen_ref, bf16[256,1024]{1,0:T(8,128)(2,1)S(1)} %copy-done, bf16[256,1024]{1,0:T(8,128)(2,1)S(1)} %copy-done.1, bf16[256,256]{1,0:T(8,128)(2,1)S(1)} %pack.1.kv_ref, ...), custom_call_target="tpu_custom_call" | custom-call | flops 2048 | tf_op jit(solution)/shard_map/own_backward/pallas_call | solution.py:295
  20.4 0.6 %collective-permute-done.4.line_ref = bf16[256,256]{1,0:T(8,128)(2,1)S(1)} collective-permute-done((bf16[256,256]{1,0:T(8,128)(2,1)S(1)}, bf16[256,256]{1,0:T(8,128)(2,1)S(1)}, u32[]{:S(2)}, u32[]{:S(2)}) %collective-permute-start.4) | collective-permute-done | bytes 131104 | tf_op jit(solution)/shard_map/ppermute | solution.py:375
  21.1 1.8 %collective-permute-done.6.far_ref = bf16[256,256]{1,0:T(8,128)(2,1)S(1)} collective-permute-done((bf16[256,256]{1,0:T(8,128)(2,1)S(1)}, bf16[256,256]{1,0:T(8,128)(2,1)S(1)}, u32[]{:S(2)}, u32[]{:S(2)}) %collective-permute-start.6) | collective-permute-done | bytes 131104 | tf_op jit(solution)/shard_map/ppermute | solution.py:373
  22.9 0.0 collective-permute-done.5.near_ref
  22.9 0.7 %side_sum.1 = (bf16[256,128]{1,0:T(8,128)(2,1)}, bf16[256,128]{1,0:T(8,128)(2,1)}) custom-call(f32[256,256]{1,0:T(8,128)S(1)} %line_sum.1.sum_ref, bf16[256,256]{1,0:T(8,128)(2,1)S(1)} %collective-permute-done.5.near_ref, bf16[256,256]{1,0:T(8,128)(2,1)S(1)} %collective-permute-done.6.far_ref), custom_call_target="tpu_custom_call" | custom-call | tf_op jit(solution)/shard_map/side_sum/pallas_call | solution.py:295
  (3 shorter events, 0.1 us)
Async XLA Ops:
  0.6 5.3 %copy-start = (bf16[256,1024]{1,0:T(8,128)(2,1)S(1)}, bf16[256,1024]{1,0:T(8,128)(2,1)}, u32[]{:S(2)}) copy-start(bf16[256,1024]{1,0:T(8,128)(2,1)} %q_ref.9) | copy-start | bytes 1572868
  0.6 5.3 %copy-start.1 = (bf16[256,1024]{1,0:T(8,128)(2,1)S(1)}, bf16[256,1024]{1,0:T(8,128)(2,1)}, u32[]{:S(2)}) copy-start(bf16[256,1024]{1,0:T(8,128)(2,1)} %g_ref.9) | copy-start | bytes 1572868
  0.7 5.3 %copy-start.2 = (s32[4096]{0:T(1024)S(1)}, s32[4096]{0:T(1024)}, u32[]{:S(2)}) copy-start(s32[4096]{0:T(1024)} %param.8) | copy-start | bytes 49156
  1.6 8.4 %collective-permute-start = (bf16[256,256]{1,0:T(8,128)(2,1)S(1)}, bf16[256,256]{1,0:T(8,128)(2,1)S(1)}, u32[]{:S(2)}, u32[]{:S(2)}) collective-permute-start(bf16[256,256]{1,0:T(8,128)(2,1)S(1)} %pack.1.kv_ref), channel_id=1, source_target_pairs={{0,4},{2,6},{4,8},{6,10},{8,12},{10,14},{12,16},{14,18},{16,20},{1... | collective-permute-start | bytes 393224 | tf_op jit(solution)/shard_map/ppermute | solution.py:338
  3.8 8.3 %collective-permute-start.2 = (bf16[256,256]{1,0:T(8,128)(2,1)S(1)}, bf16[256,256]{1,0:T(8,128)(2,1)S(1)}, u32[]{:S(2)}, u32[]{:S(2)}) collective-permute-start(bf16[256,256]{1,0:T(8,128)(2,1)S(1)} %pack.1.kv_ref), channel_id=1, source_target_pairs={{0,2},{2,8},{4,6},{6,12},{8,10},{10,16},{12,14},{14,20},{16,18},{1... | collective-permute-start | bytes 393224 | tf_op jit(solution)/shard_map/ppermute | solution.py:347
  10.0 3.2 %collective-permute-start.1 = (bf16[256,256]{1,0:T(8,128)(2,1)S(1)}, bf16[256,256]{1,0:T(8,128)(2,1)S(1)}, u32[]{:S(2)}, u32[]{:S(2)}) collective-permute-start(bf16[256,256]{1,0:T(8,128)(2,1)S(1)} %collective-permute-done.refs_2_.kv_ref), channel_id=1, source_target_pairs={{0,2},{2,0},{4,6},{6,4},{8,10},{10,8},{12,14},{14,12},{16,18},{18,... | collective-permute-start | bytes 393224 | tf_op jit(solution)/shard_map/ppermute | solution.py:348
  14.6 1.4 %collective-permute-start.3 = (bf16[256,256]{1,0:T(8,128)(2,1)S(1)}, bf16[256,256]{1,0:T(8,128)(2,1)S(1)}, u32[]{:S(2)}, u32[]{:S(2)}) collective-permute-start(bf16[256,256]{1,0:T(8,128)(2,1)S(1)} %get-tuple-element.51), channel_id=1, source_target_pairs={{0,2},{2,0},{4,6},{6,4},{8,10},{10,8},{12,14},{14,12},{16,18},{18,... | collective-permute-start | bytes 393224 | tf_op jit(solution)/shard_map/ppermute | solution.py:364
  16.1 5.0 %collective-permute-start.4 = (bf16[256,256]{1,0:T(8,128)(2,1)S(1)}, bf16[256,256]{1,0:T(8,128)(2,1)S(1)}, u32[]{:S(2)}, u32[]{:S(2)}) collective-permute-start(bf16[256,256]{1,0:T(8,128)(2,1)S(1)} %line_add.1), channel_id=1, source_target_pairs={{4,0},{6,2},{8,4},{10,6},{12,8},{14,10},{16,12},{18,14},{20,16},{2... | collective-permute-start | bytes 393224 | tf_op jit(solution)/shard_map/ppermute | solution.py:375
  17.8 5.1 %collective-permute-start.6 = (bf16[256,256]{1,0:T(8,128)(2,1)S(1)}, bf16[256,256]{1,0:T(8,128)(2,1)S(1)}, u32[]{:S(2)}, u32[]{:S(2)}) collective-permute-start(bf16[256,256]{1,0:T(8,128)(2,1)S(1)} %get-tuple-element.65), channel_id=1, source_target_pairs={{8,2},{12,6},{16,10},{20,14},{24,18},{28,22},{6,12},{10,16},{14,20... | collective-permute-start | bytes 393224 | tf_op jit(solution)/shard_map/ppermute | solution.py:373
  18.5 4.4 %collective-permute-start.5 = (bf16[256,256]{1,0:T(8,128)(2,1)S(1)}, bf16[256,256]{1,0:T(8,128)(2,1)S(1)}, u32[]{:S(2)}, u32[]{:S(2)}) collective-permute-start(bf16[256,256]{1,0:T(8,128)(2,1)S(1)} %get-tuple-element.65), channel_id=1, source_target_pairs={{0,2},{2,0},{4,6},{6,4},{8,10},{10,8},{12,14},{14,12},{16,18},{18,... | collective-permute-start | bytes 393224 | tf_op jit(solution)/shard_map/ppermute | solution.py:374
